TPU v7x, 32 devices: a whole 2x2x4 slice. The times are simulated.
32 devices in a mesh: trade: 8 (over z, y), path: 4 (over x, core).
Axes of the slice: x: 2, y: 2, z: 4, core: 2. Of those that a mesh axis runs over, the one named last changes fastest.
Arguments:
- shocks: bfloat16 [80, 32, 512], P(None, None, 'path'), may hold values from -6 to 6
- forward_start: float32 [80], replicated, may hold values from 0.01 to 0.06
- loading: float32 [80, 80], replicated, may hold values from -0.30186918 to 0.30186918
- coefficient: bfloat16 [4096, 160], P('trade'), may hold values from -0.5 to 0.5
- notional: float32 [4096], P('trade'), may hold values from -4 to 4
- ns_of_trade: int32 [4096], replicated, may hold values from 0 to 63, as said below
- agr_of_ns: int32 [64], P('trade'), may hold values from 0 to 31, as said below
- cpty_of_agr: int32 [32], P('trade'), may hold values from 0 to 31, as said below
- margin_lag: int32 [32], P('trade'), may hold values from 1 to 4
- default_weight: float32 [32, 32], P('trade'), may hold values from 0.02 to 0.2
Outputs:
- allocation: float32 [4096], P('trade')
- cva: float32 [32], P('trade')
Inputs may be any that keep to these rules, and one draw needn't show every extreme that they name: `ns_of_trade`: the trades of each block of 512 consecutive trades fall in exactly 2 netting sets of every block of 8 consecutive netting sets, and at most 96 of them in one such block of sets; in every block of trades half of the blocks of sets receive exactly 96. `agr_of_ns`: netting set n belongs to an agreement of block n // 8 of 4 consecutive agreements. `cpty_of_agr`: agreement a belongs to a counterparty of block a // 4 of 4 consecutive counterparties.
All inputs are finite; a program needn't handle non-finite values.
Results may differ from a plain program's by a relative error of at most 0.025.
Values may be sent and summed in bfloat16 or wider, within the bound.
No kernel may reach another device: no remote copies, remote signals or barrier semaphores. Data moves between devices by JAX's collectives and lax.ppermute only.
A program may use at most 64 MiB of HBM per device.

v0:
```python
import jax
import jax.numpy as jnp
from jax import lax
from jax.sharding import PartitionSpec as P

NS_DEV = 8
AG_DEV = 4
CP_DEV = 4
CAP = 2
LAG_MAX = 4


RATE_UNIT = 0.03
STEP = 0.25
SMOOTH = 0.5


def make_basis(walk, date_index, forward_start, loading):
    tenors = loading.shape[1]
    drift = 0.5 * STEP * jnp.sum(loading * loading, axis=0)
    moved = jnp.dot(
        loading.T, walk, precision=lax.Precision.HIGHEST, preferred_element_type=jnp.float32
    )
    log_fwd = (
        jnp.log(forward_start)[:, None]
        + jnp.sqrt(STEP) * moved
        - (date_index + 1.0)[None, :] * drift[:, None]
    )
    fwd = jnp.exp(log_fwd)
    lower = (jnp.arange(tenors)[None, :] <= jnp.arange(tenors)[:, None]).astype(jnp.float32)
    summed = jnp.dot(
        lower,
        jnp.log1p(STEP * fwd),
        precision=lax.Precision.HIGHEST,
        preferred_element_type=jnp.float32,
    )
    bond = jnp.exp(-summed)
    return jnp.concatenate([bond * fwd / RATE_UNIT, bond], axis=0).astype(jnp.bfloat16)


def collateral_terms(agreement, margin_lag, agr_weight, path_total):
    lagged = jnp.zeros_like(agreement)
    for lag_step in range(1, LAG_MAX + 1):
        shifted = jnp.pad(agreement[:, :-lag_step], ((0, 0), (lag_step, 0), (0, 0)))
        lagged = lagged + jnp.where((margin_lag == lag_step)[:, None, None], shifted, 0.0)
    excess = agreement - lagged
    spread_root = jnp.sqrt(excess * excess + SMOOTH * SMOOTH)
    exposure = 0.5 * (excess + spread_root)
    slope = 0.5 * (1.0 + excess / spread_root)
    weighted = agr_weight[:, :, None] * slope
    ahead = jnp.zeros_like(weighted)
    for lag_step in range(1, LAG_MAX + 1):
        shifted = jnp.pad(weighted[:, lag_step:], ((0, 0), (0, lag_step), (0, 0)))
        ahead = ahead + jnp.where((margin_lag == lag_step)[:, None, None], shifted, 0.0)
    grads = ((weighted - ahead) / path_total).astype(jnp.bfloat16)
    return (exposure, grads)


def price_rows(coef_rows, notional_rows, basis):
    underlying = jnp.dot(coef_rows, basis, preferred_element_type=jnp.float32)
    return (notional_rows[:, None] * jnp.maximum(underlying, 0.0)).astype(jnp.bfloat16)


def body(
    shocks,
    forward_start,
    loading,
    coefficient,
    notional,
    ns_of_trade,
    agr_of_ns,
    cpty_of_agr,
    margin_lag,
    default_weight,
):
    trade_count = lax.axis_size("trade")
    path_total = jnp.float32(shocks.shape[2] * lax.axis_size("path"))
    my_index = lax.axis_index("trade")
    tenors, date_count, path_dev = shocks.shape
    tr_dev = coefficient.shape[0]
    columns = date_count * path_dev
    highest = lax.Precision.HIGHEST
    walk = jnp.cumsum(shocks.astype(jnp.float32), axis=1).reshape(tenors, columns)
    date_index = (jnp.arange(columns) // path_dev).astype(jnp.float32)
    basis = make_basis(walk, date_index, forward_start, loading)
    own_sets = lax.dynamic_slice_in_dim(ns_of_trade, my_index * tr_dev, tr_dev, 0)
    agr_local = agr_of_ns - my_index * AG_DEV
    to_agr = (agr_local[:, None] == jnp.arange(AG_DEV, dtype=jnp.int32)[None, :]).astype(
        jnp.float32
    )
    cpty_local = cpty_of_agr - my_index * CP_DEV
    to_cpty = (cpty_local[:, None] == jnp.arange(CP_DEV, dtype=jnp.int32)[None, :]).astype(
        jnp.float32
    )
    agr_weight = jnp.einsum("ac,ct->at", to_cpty, default_weight, precision=highest)
    values = price_rows(coefficient, notional, basis)
    net_total = trade_count * NS_DEV
    slot_total = trade_count * CAP
    net_ids = jnp.arange(net_total, dtype=jnp.int32)
    own_hot = own_sets[:, None] == net_ids[None, :]
    present_own = jnp.any(own_hot, axis=0).reshape(trade_count, NS_DEV)
    rank_own = jnp.cumsum(present_own.astype(jnp.int32), axis=1) - 1
    owner_ids = jnp.arange(trade_count, dtype=jnp.int32)[:, None]
    slot_of_set = (owner_ids * CAP + rank_own).reshape(net_total)
    slot_of_trade = jnp.sum(jnp.where(own_hot, slot_of_set[None, :], 0), axis=1)
    slot_hot = (slot_of_trade[:, None] == jnp.arange(slot_total, dtype=jnp.int32)[None, :]).astype(
        jnp.bfloat16
    )
    outgoing = lax.dot_general(
        slot_hot, values, (((0,), (0,)), ((), ())), preferred_element_type=jnp.float32
    )
    outgoing = outgoing.reshape(trade_count, CAP, date_count, path_dev)
    my_sets = my_index * NS_DEV + jnp.arange(NS_DEV, dtype=jnp.int32)
    all_blocks = ns_of_trade.reshape(trade_count, tr_dev)
    present_in = jnp.any(all_blocks[:, :, None] == my_sets[None, None, :], axis=1)
    rank_in = jnp.cumsum(present_in.astype(jnp.int32), axis=1) - 1
    slot_rank = jnp.arange(CAP, dtype=jnp.int32)[None, :, None]
    slot_pick = (present_in[:, None, :] & (rank_in[:, None, :] == slot_rank)).astype(jnp.float32)
    received = lax.all_to_all(
        outgoing.astype(jnp.bfloat16), "trade", split_axis=0, concat_axis=0, tiled=True
    ).astype(outgoing.dtype)
    netted = jnp.einsum("sck,sctp->ktp", slot_pick, received, precision=highest)
    agreement = jnp.einsum("ka,ktp->atp", to_agr, netted, precision=highest)
    exposure, grads = collateral_terms(agreement, margin_lag, agr_weight, path_total)
    by_cpty = jnp.einsum("ac,atp->ctp", to_cpty, exposure, precision=highest)
    net_grads = jnp.einsum("ka,atp->ktp", to_agr, grads.astype(jnp.float32), precision=highest)
    slot_grads = jnp.einsum("sck,ktp->sctp", slot_pick, net_grads, precision=highest).astype(
        jnp.bfloat16
    )
    slot_grads, by_cpty = (slot_grads, by_cpty[None])
    returned = lax.all_to_all(slot_grads, "trade", split_axis=0, concat_axis=0, tiled=True)
    exposure_part = jnp.sum(by_cpty[0], axis=2)
    grad_rows = jnp.take(returned.reshape(slot_total, columns), slot_of_trade, axis=0)
    alloc_part = jnp.einsum("ic,ic->i", values, grad_rows, preferred_element_type=jnp.float32)
    expected = lax.psum(exposure_part, "path") / path_total
    cva = jnp.sum(default_weight * expected, axis=1)
    allocation = lax.psum(alloc_part, "path")
    return (allocation, cva)


def solution(mesh):
    placed = (
        P(None, None, "path"),
        P(),
        P(),
        P("trade", None),
        P("trade"),
        P(),
        P("trade"),
        P("trade"),
        P("trade"),
        P("trade", None),
    )
    return jax.shard_map(
        body, mesh=mesh, in_specs=placed, out_specs=(P("trade"), P("trade")), check_vma=False
    )
```

profile of v0, /device:TPU:0, one launch (start us, length us, event | category | flops | bytes accessed | tf_op | source)
XLA Modules:
  0.0 64.1 jit_solution(6991234229655494800)
XLA Ops:
  0.6 0.0 copy-start
  0.7 0.8 %multiply_reduce_fusion.1 = f32[80]{0:T(128)S(1)} fusion(f32[80,80]{1,0:T(8,128)} %param.12), kind=kLoop, calls=%fused_computation.45 | loop fusion | flops 12720 | bytes 25920 | tf_op jit(solution)/shard_map/reduce_sum | solution.py:20
  1.5 0.7 %log.3 = f32[80]{0:T(128)S(1)} log(f32[80]{0:T(128)} %param.11) | non-fusion elementwise | bytes 640 | tf_op jit(solution)/shard_map/log | solution.py:25
  2.2 1.2 %convert_element_type.65 = f32[80,32,128]{2,1,0:T(8,128)S(1)} convert(bf16[80,32,128]{2,1,0:T(8,128)(2,1)} %param.10) | non-fusion elementwise | flops 327680 | bytes 1966080 | tf_op jit(solution)/shard_map/convert_element_type | solution.py:83
  3.4 0.0 copy-start.1
  3.4 0.8 %fusion.10 = f32[80,32,128]{2,0,1:T(8,128)S(1)} fusion(f32[80,32,128]{2,1,0:T(8,128)S(1)} %convert_element_type.65), kind=kOutput, calls=%fused_computation.17 | output fusion | flops 10158080 | bytes 2621440 | tf_op jit(solution)/shard_map/jit(cumsum)/reduce_window_sum | solution.py:83
  4.2 0.0 copy-done.1
  4.2 1.5 %fusion.4 = f32[80,4096]{1,0:T(8,128)S(1)} fusion(f32[80,80]{1,0:T(8,128)S(1)} %copy-done.1, f32[80]{0:T(128)S(1)} %broadcast_multiply_fusion, f32[4096]{0:T(1024)S(1)} %fusion.27, f32[80]{0:T(128)S(1)} %log.3, f32[80,32,128]{2,0,1:T(8,128)S(1)} %fusion.10), kind=kOutput, calls=%fused_computation.9 | convolution fusion | flops 315883520 | bytes 2664064 | tf_op jit(solution)/shard_map/dot_general | solution.py:21
  5.8 0.0 copy-start.2
  5.8 0.0 copy-start.3
  5.8 1.5 %multiply_convert_fusion.1 = (bf16[80,4096]{1,0:T(8,128)(2,1)S(1)}, bf16[80,4096]{1,0:T(8,128)(2,1)S(1)}) fusion(f32[80,4096]{1,0:T(8,128)S(1)} %fusion.4), kind=kOutput, calls=%fused_computation.19 | convolution fusion | flops 316545280 | bytes 2621440 | tf_op jit(solution)/shard_map/dot_general | solution.py:31
  7.3 0.0 copy-done.2
  7.3 0.1 dynamic_slice.3
  7.3 0.1 fusion.20
  7.5 0.1 reshape.99
  7.6 0.2 reduce_window_sum.29
  7.7 0.1 add_add_fusion
  7.8 0.1 add.147
  7.9 0.1 select_reduce_fusion
  8.0 0.0 copy-done
  8.0 0.0 copy-done.3
  8.0 4.5 %bitcast_convert_fusion = (f32[512,4096]{0,1:T(8,128)}, bf16[4096,512]{1,0:T(8,128)(2,1)S(1)}) fusion(bf16[512,160]{0,1:T(8,128)(2,1)S(1)} %copy-done, bf16[80,4096]{1,0:T(8,128)(2,1)S(1)} %get-tuple-element.7, bf16[80,4096]{1,0:T(8,128)(2,1)S(1)} %get-tuple-element.6, f32[512]{0:T(512)S(1)} %copy-done.3), kind=kOutput, calls=%fused_computation.11 | convolution fusion | flops 682098688 | bytes 14059520 | tf_op jit(solution)/shard_map/dot_general | solution.py:60
  12.5 1.3 %fusion.14 = bf16[2,8,32,128]{3,1,2,0:T(8,128)(2,1)S(1)} fusion(bf16[4096,512]{1,0:T(8,128)(2,1)S(1)} %get-tuple-element.14, s32[512]{0:T(512)S(1)} %select_reduce_fusion), kind=kOutput, calls=%fused_computation.23 | convolution fusion | flops 67190784 | bytes 4327424 | tf_op jit(solution)/shard_map/dot_general | solution.py:109
  13.9 0.7 %copy.43 = bf16[8,2,32,128]{3,1,2,0:T(2,128)(2,1)} copy(bf16[8,2,32,128]{3,2,1,0:T(8,128)(2,1)S(1)} %bitcast.54) | data formatting | bytes 262144 | tf_op jit(solution)/shard_map/convert_element_type | solution.py:120
  14.7 7.3 %all-to-all-start = ((bf16[8,2,32,128]{3,1,2,0:T(2,128)(2,1)}), bf16[8,2,32,128]{3,1,2,0:T(2,128)(2,1)S(1)}, u32[]{:S(2)}, u32[]{:S(2)}) async-start(bf16[8,2,32,128]{3,1,2,0:T(2,128)(2,1)} %copy.43), calls=%async_computation | async-start | bytes 262144 | tf_op jit(solution)/shard_map/all_to_all | solution.py:119
  22.0 0.0 copy-done.5
  22.1 0.0 copy-done.4
  22.1 0.2 convolution_multiply_fusion.1
  22.3 0.3 compare_reduce_fusion
  22.6 8.9 %copy.55 = f32[512,4096]{1,0:T(8,128)} copy(f32[512,4096]{0,1:T(8,128)} %get-tuple-element.13) | data formatting | bytes 16777216
  31.5 0.1 copy.46
  31.6 0.2 reduce_window_sum.30
  31.8 0.0 all-to-all-done
  31.8 0.2 convolution_bitcast_fusion.1
  32.0 0.2 fusion.44
  32.2 0.2 add_multiply_fusion
  32.5 0.2 convolution_bitcast_fusion
  32.7 0.3 convolution_convert_fusion.1
  33.0 0.7 %copy.47 = bf16[8,2,32,128]{3,2,1,0:T(8,128)(2,1)} copy(bf16[8,2,32,128]{3,0,2,1:T(8,128)(2,1)S(1)} %convolution_convert_fusion.1) | data formatting | bytes 262144 | tf_op jit(solution)/shard_map/convert_element_type | solution.py:127
  33.6 6.0 %all-to-all-start.1 = ((bf16[8,2,32,128]{3,2,1,0:T(8,128)(2,1)}), bf16[8,2,32,128]{3,2,1,0:T(8,128)(2,1)S(1)}, u32[]{:S(2)}, u32[]{:S(2)}) async-start(bf16[8,2,32,128]{3,2,1,0:T(8,128)(2,1)} %copy.47), calls=%async_computation.1 | async-start | bytes 262144 | tf_op jit(solution)/shard_map/all_to_all | solution.py:131
  39.6 0.3 convolution_reduce_fusion
  40.0 0.1 copy.48
  40.1 6.9 %all-to-all-done.1 = bf16[8,2,32,128]{3,2,1,0:T(8,128)(2,1)S(1)} async-done(((bf16[8,2,32,128]{3,2,1,0:T(8,128)(2,1)}), bf16[8,2,32,128]{3,2,1,0:T(8,128)(2,1)S(1)}, u32[]{:S(2)}, u32[]{:S(2)}) %all-to-all-start.1) | async-done | bytes 131104 | tf_op jit(solution)/shard_map/all_to_all | solution.py:131
  47.0 0.1 copy.69
  47.0 4.4 %gather_fusion = bf16[512,4096]{1,0:T(8,128)(2,1)} fusion(bf16[16,4096]{1,0:T(8,128)(2,1)S(1)} %bitcast.52, s32[1024]{0:T(1024)S(1)} %pad_clamp_fusion), kind=kCustom, calls=%fused_computation | custom fusion | bytes 8390656 | tf_op jit(solution)/shard_map/jit(_take)/gather | solution.py:133
  51.4 5.8 %multiply_reduce_fusion = f32[512]{0:T(512)S(1)} fusion(f32[512,4096]{1,0:T(8,128)} %copy.55, bf16[512,4096]{1,0:T(8,128)(2,1)} %gather_fusion, pred[512]{0:T(512)(128)(4,1)S(1)} %compare_and_fusion), kind=kLoop, calls=%fused_computation.1 | loop fusion | flops 8388096 | bytes 12585472 | tf_op jit(solution)/shard_map/ic,ic->i/dot_general | solution.py:134
  57.2 6.2 %all-reduce.8 = (f32[512]{0:T(512)}, f32[4,32]{1,0:T(4,128)S(1)}) all-reduce(f32[512]{0:T(512)S(1)} %multiply_reduce_fusion, f32[4,32]{1,0:T(4,128)S(1)} %copy.48), channel_id=1, replica_groups=mesh['trade'=8,'path'=4] {'path'}, use_global_device_ids=true, to_apply=%region_7.8 | all-reduce | flops 640 | bytes 5120 | tf_op jit(solution)/shard_map/psum | solution.py:137
  63.4 0.6 multiply_reduce_fusion.2
  (29 shorter events, 0.2 us)
Async XLA Ops:
  0.6 7.4 %copy-start = (bf16[512,160]{0,1:T(8,128)(2,1)S(1)}, bf16[512,160]{0,1:T(8,128)(2,1)}, u32[]{:S(2)}) copy-start(bf16[512,160]{0,1:T(8,128)(2,1)} %param.13) | copy-start | bytes 491524
  3.4 0.8 %copy-start.1 = (f32[80,80]{1,0:T(8,128)S(1)}, f32[80,80]{1,0:T(8,128)}, u32[]{:S(2)}) copy-start(f32[80,80]{1,0:T(8,128)} %param.12) | copy-start | bytes 76804
  5.8 1.5 %copy-start.2 = (s32[4096]{0:T(1024)S(1)}, s32[4096]{0:T(1024)}, u32[]{:S(2)}) copy-start(s32[4096]{0:T(1024)} %param.15) | copy-start | bytes 49156
  5.8 2.2 %copy-start.3 = (f32[512]{0:T(512)S(1)}, f32[512]{0:T(512)}, u32[]{:S(2)}) copy-start(f32[512]{0:T(512)} %param.14) | copy-start | bytes 6148
  12.5 9.4 %copy-start.6 = (s32[4]{0:T(128)S(1)}, s32[4]{0:T(128)}, u32[]{:S(2)}) copy-start(s32[4]{0:T(128)} %param.17) | copy-start | bytes 52
  12.5 9.5 %copy-start.7 = (s32[8]{0:T(128)S(1)}, s32[8]{0:T(128)}, u32[]{:S(2)}) copy-start(s32[8]{0:T(128)} %param.16) | copy-start | bytes 100
  12.5 9.5 %copy-start.5 = (s32[4]{0:T(128)S(1)}, s32[4]{0:T(128)}, u32[]{:S(2)}) copy-start(s32[4]{0:T(128)} %param.18) | copy-start | bytes 52
  12.5 9.5 %copy-start.4 = (f32[4,32]{1,0:T(4,128)S(1)}, f32[4,32]{1,0:T(4,128)}, u32[]{:S(2)}) copy-start(f32[4,32]{1,0:T(4,128)} %param.19) | copy-start | bytes 1540
  14.7 17.1 %all-to-all-start = ((bf16[8,2,32,128]{3,1,2,0:T(2,128)(2,1)}), bf16[8,2,32,128]{3,1,2,0:T(2,128)(2,1)S(1)}, u32[]{:S(2)}, u32[]{:S(2)}) async-start(bf16[8,2,32,128]{3,1,2,0:T(2,128)(2,1)} %copy.43), calls=%async_computation | async-start | bytes 262144 | tf_op jit(solution)/shard_map/all_to_all | solution.py:119
  33.6 13.3 %all-to-all-start.1 = ((bf16[8,2,32,128]{3,2,1,0:T(8,128)(2,1)}), bf16[8,2,32,128]{3,2,1,0:T(8,128)(2,1)S(1)}, u32[]{:S(2)}, u32[]{:S(2)}) async-start(bf16[8,2,32,128]{3,2,1,0:T(8,128)(2,1)} %copy.47), calls=%async_computation.1 | async-start | bytes 262144 | tf_op jit(solution)/shard_map/all_to_all | solution.py:131
where the time goes:
time: 64.7 us; the launch traced here: 64.1 us
  local copies, waits for them, and re-layouts  16 us (25%)
  starting transfers between devices  13.3 us (21%)
  other arithmetic  10.5 us (16%)
  matrix products  10.3 us (16%)
  waiting for transfers between devices  6.92 us (11%)
  blocking collectives  6.24 us (10%)
  between operations  0.95 us (1%)
    unnamed x19, local copies, waits for them, and re-layouts  9.09 us
    all_to_all x1, starting transfers between devices, body(): lax.all_to_all(outgoing.astype(jnp.bfloat16), 'trade', split_axis=0, conc...  7.28 us
    all_to_all x1, waiting for transfers between devices, body(): lax.all_to_all(slot_grads, 'trade', split_axis=0, concat_axis=0, tiled=True)  6.91 us
    psum x1, blocking collectives, body(): allocation = lax.psum(alloc_part, 'path')  6.24 us
    all_to_all x1, starting transfers between devices, body(): lax.all_to_all(slot_grads, 'trade', split_axis=0, concat_axis=0, tiled=True)  5.99 us
    dot_general x1, other arithmetic, body(): jnp.einsum('ic,ic->i', values, grad_rows, preferred_element_type=jnp.floa...  5.81 us
    dot_general x1, matrix products, price_rows(): underlying = jnp.dot(coef_rows, basis, preferred_element_type=jnp.float32)  4.54 us
    gather x1, local copies, waits for them, and re-layouts, body(): jnp.take(returned.reshape(slot_total, columns), slot_of_trade, axis=0)  4.35 us
  transfers between devices with their start and end apart: 2, of which 1 were waited for; matrix products, arithmetic and copies ran while one was open for 16% of the time, Pallas kernels for 0%

commit v1 on v0

v1 whole, which is shorter than its diff:
```python
import functools

import jax
import jax.numpy as jnp
from jax import lax
from jax.experimental import pallas as pl
from jax.experimental.pallas import tpu as pltpu
from jax.sharding import PartitionSpec as P

NS_DEV = 8
AG_DEV = 4
LAG_MAX = 4
LANES = 128
TAIL = 16
OWNERS_PER_ROW = LANES // NS_DEV

RATE_UNIT = 0.03
STEP = 0.25
SMOOTH = 0.5

F32 = jnp.float32
BF16 = jnp.bfloat16
VMEM = pl.BlockSpec(memory_space=pltpu.VMEM)
SMEM = pl.BlockSpec(memory_space=pltpu.SMEM)


def iota(shape, dim):
    return lax.broadcasted_iota(jnp.int32, shape, dim)


def split_bf16(x, parts):
    pieces = []
    for _ in range(parts):
        piece = x.astype(BF16).astype(F32)
        pieces.append(piece)
        x = x - piece
    return pieces


def pack_kernel(me_ref, agr_ref, cpty_ref, lag_ref, coef_ref, notional_ref, weight_ref, out_ref):
    me = me_ref[0]
    rows, basis_rows = coef_ref.shape
    groups = rows // LANES
    out_ref[0:rows, :] = coef_ref[:, 0:LANES]
    out_ref[rows : rows + LANES, :] = jnp.concatenate(
        [coef_ref[LANES * g : LANES * (g + 1), LANES:basis_rows] for g in range(groups)], axis=1
    )
    high, low = split_bf16(notional_ref[...], 2)
    lane = iota((1, LANES), 1)
    set_row = jnp.zeros((1, LANES), F32)
    for n in range(NS_DEV):
        spot = NS_DEV * lax.rem(me, OWNERS_PER_ROW) + n
        set_row = jnp.where(lane == spot, (agr_ref[n] - me * AG_DEV).astype(F32), set_row)
    set_rows = jnp.where(iota((4, LANES), 0) == 0, set_row, 0.0)
    weight = weight_ref[...]
    dates = weight.shape[1]
    picked, lags = [], []
    for a in range(AG_DEV):
        row = weight[0:1]
        for c in range(1, weight.shape[0]):
            row = jnp.where(cpty_ref[a] - me * weight.shape[0] == c, weight[c : c + 1], row)
        picked.append(row)
        lags.append(jnp.full((1, LANES - 3 * dates), lag_ref[a].astype(F32)))
    picked = jnp.concatenate(picked, axis=0)
    table = jnp.concatenate(split_bf16(picked, 3) + [jnp.concatenate(lags, axis=0)], axis=1)
    tail = jnp.concatenate([high, low, set_rows, table], axis=0)
    out_ref[rows + LANES :, :] = tail.astype(BF16)


def basis_kernel(dates, paths, cols, me_ref, shocks_ref, start_ref, loading_ref, out_ref, wide_ref):
    me = me_ref[0]
    tenors = loading_ref.shape[0]
    wide_ref[...] = shocks_ref[...].astype(F32)
    lane = iota((tenors, LANES), 1)
    walk = jnp.zeros((tenors, LANES), F32)
    tiles = [jnp.zeros((tenors, LANES), F32) for _ in range(cols // LANES)]
    for s in range(dates):
        walk = walk + wide_ref[pl.ds(s, tenors, stride=dates), :]
        tile, offset = divmod(s * paths, LANES)
        moved = pltpu.roll(walk, lax.rem(offset + LANES - paths * me, LANES), 1)
        tiles[tile] = jnp.where((lane >= offset) & (lane < offset + paths), moved, tiles[tile])
    walk = jnp.concatenate(tiles, axis=1)
    loading_t = jnp.transpose(loading_ref[...])
    drift = 0.5 * STEP * jnp.sum(loading_t * loading_t, axis=1, keepdims=True)
    diag = iota((tenors, tenors), 0) == iota((tenors, tenors), 1)
    log_start = jnp.log(
        jnp.sum(jnp.where(diag, start_ref[...], 0.0), axis=1, keepdims=True)
    )
    moved = jnp.dot(
        loading_t, walk, precision=lax.Precision.HIGHEST, preferred_element_type=F32
    )
    date = (iota((1, cols), 1) // paths + 1).astype(F32)
    fwd = jnp.exp(log_start + (STEP**0.5) * moved - date * drift)
    lower = (iota((tenors, tenors), 1) <= iota((tenors, tenors), 0)).astype(F32)
    summed = jnp.dot(
        lower,
        jnp.log1p(STEP * fwd),
        precision=lax.Precision.HIGHEST,
        preferred_element_type=F32,
    )
    bond = jnp.exp(-summed)
    out_ref[0:tenors, :] = (bond * fwd / RATE_UNIT).astype(BF16)
    out_ref[tenors:, :] = bond.astype(BF16)


def main_kernel(
    owners, chunk, dates, paths, path_total, gath_ref, basis_ref, sets_ref, out_ref, val_ref, acc_ref
):
    groups = sets_ref.shape[0] // owners
    rows = groups * LANES
    cols = basis_ref.shape[1]
    extra = basis_ref.shape[0] - LANES
    agrs = owners * AG_DEV
    set_count = owners * NS_DEV
    chunks = owners // chunk
    span = chunk * LANES

    tail = rows + LANES
    set_rows = [jnp.zeros((1, LANES), F32) for _ in range(-(-owners // OWNERS_PER_ROW))]
    tables = []
    for b in range(owners):
        block = gath_ref[b, tail : tail + TAIL, :].astype(F32)
        set_rows[b // OWNERS_PER_ROW] = set_rows[b // OWNERS_PER_ROW] + block[8:9]
        tables.append(block[12:16])
    table = jnp.concatenate(tables, axis=0)
    lag = table[:, 3 * dates : 3 * dates + 1]
    spread = (
        (iota((3 * dates, cols), 0) % dates == iota((3 * dates, cols), 1) // paths)
    ).astype(F32).astype(BF16)
    weight = jnp.dot(
        table[:, 0 : 3 * dates].astype(BF16), spread, preferred_element_type=F32
    )

    def row_of(ref_rows, g):
        return jnp.concatenate([ref_rows[groups * b + g : groups * b + g + 1] for b in range(chunk)], axis=1)

    def hot_of(k, g):
        sets = sets_ref[pl.ds(pl.multiple_of(k * chunk * groups, 8), chunk * groups), :]
        sets = row_of(sets, g)
        local = jnp.zeros((8, span), F32)
        for q, row in enumerate(set_rows):
            width = min(LANES, set_count - q * LANES)
            hot = (iota((width, span), 0) + q * LANES == sets).astype(F32).astype(BF16)
            local = local + jnp.dot(
                jnp.broadcast_to(row[:, 0:width], (8, width)).astype(BF16),
                hot,
                preferred_element_type=F32,
            )
        agr = lax.shift_right_logical(sets, 3) * AG_DEV + local[0:1].astype(jnp.int32)
        return iota((agrs, span), 0) == agr

    acc_ref[...] = jnp.zeros_like(acc_ref)

    def price(k, g):
        block = pl.ds(k * chunk, chunk)
        left = gath_ref[block, LANES * g : LANES * (g + 1), :].reshape(span, LANES)
        right = gath_ref[block, rows : rows + LANES, :].reshape(span, LANES)
        parts = [basis_ref[0:LANES, :]]
        if g:
            parts.append(jnp.zeros((extra * g, cols), BF16))
        parts.append(basis_ref[LANES:, :])
        if g < groups - 1:
            parts.append(jnp.zeros((extra * (groups - 1 - g), cols), BF16))
        under = jnp.dot(
            jnp.concatenate([left, right], axis=1),
            jnp.concatenate(parts, axis=0),
            preferred_element_type=F32,
        )
        value = jnp.maximum(under, 0.0).astype(BF16)
        val_ref[k * groups + g] = value
        pieces = gath_ref[block, tail : tail + TAIL, :].astype(F32)
        high = jnp.concatenate([pieces[b, g : g + 1] for b in range(chunk)], axis=1)
        low = jnp.concatenate([pieces[b, groups + g : groups + g + 1] for b in range(chunk)], axis=1)
        hot = hot_of(k, g)
        left = jnp.concatenate([jnp.where(hot, high, 0.0), jnp.where(hot, low, 0.0)], axis=0)
        acc_ref[...] += jnp.dot(left.astype(BF16), value, preferred_element_type=F32)

    def price_chunk(k):
        for g in range(groups):
            price(k, g)

    run(chunks, price_chunk)

    agreement = acc_ref[0:agrs] + acc_ref[agrs:]
    lane = iota((1, cols), 1)
    lagged = jnp.zeros_like(agreement)
    for step in range(1, LAG_MAX + 1):
        back = pltpu.roll(agreement, step * paths, 1)
        lagged = jnp.where((lag == step) & (lane >= step * paths), back, lagged)
    excess = agreement - lagged
    root = jnp.sqrt(excess * excess + SMOOTH * SMOOTH)
    exposure = 0.5 * (excess + root)
    weighted = weight * (0.5 * (1.0 + excess / root))
    ahead = jnp.zeros_like(weighted)
    for step in range(1, LAG_MAX + 1):
        front = pltpu.roll(weighted, cols - step * paths, 1)
        ahead = jnp.where((lag == step) & (lane < cols - step * paths), front, ahead)
    grads = ((weighted - ahead) * (1.0 / path_total)).astype(BF16)
    spent = jnp.sum(weight * exposure, axis=1, keepdims=True) * (1.0 / path_total)

    def allocate_chunk(k):
        lines = []
        for g in range(groups):
            dots = lax.dot_general(
                grads, val_ref[k * groups + g], (((1,), (1,)), ((), ())), preferred_element_type=F32
            )
            lines.append(jnp.sum(jnp.where(hot_of(k, g), dots, 0.0), axis=0, keepdims=True))
        for b in range(chunk):
            alloc = [line[:, LANES * b : LANES * (b + 1)] for line in lines]
            out_ref[pl.ds(pl.multiple_of((k * chunk + b) * 8, 8), groups), :] = jnp.concatenate(alloc, axis=0)

    run(chunks, allocate_chunk)
    for b in range(owners):
        out_ref[8 * b + groups : 8 * b + groups + AG_DEV, :] = jnp.broadcast_to(
            spent[AG_DEV * b : AG_DEV * (b + 1)], (AG_DEV, LANES)
        )


def run(count, step):
    if count == 1:
        step(0)
    else:

        def loop_body(k, carry):
            step(k)
            return carry

        lax.fori_loop(0, count, loop_body, 0)


def body(
    shocks,
    forward_start,
    loading,
    coefficient,
    notional,
    ns_of_trade,
    agr_of_ns,
    cpty_of_agr,
    margin_lag,
    default_weight,
):
    owners = lax.axis_size("trade")
    path_total = float(shocks.shape[2] * lax.axis_size("path"))
    tenors, dates, path_dev = shocks.shape
    rows = coefficient.shape[0]
    groups = rows // LANES
    paths = path_dev // owners
    cols = max(dates * paths, LANES)
    chunk = min(owners, 8)
    me = lax.axis_index("trade").astype(jnp.int32).reshape(1)

    packed_rows = rows + LANES + TAIL
    packed = pl.pallas_call(
        pack_kernel,
        out_shape=jax.ShapeDtypeStruct((packed_rows, LANES), BF16),
        in_specs=[SMEM] * 4 + [VMEM] * 3,
        out_specs=VMEM,
        name="pack",
    )(
        me,
        agr_of_ns,
        cpty_of_agr,
        margin_lag,
        coefficient,
        notional.reshape(groups, LANES),
        default_weight,
    )
    gathered = lax.all_gather(packed, "trade", axis=0, tiled=False)

    basis = pl.pallas_call(
        functools.partial(basis_kernel, dates, paths, cols),
        out_shape=jax.ShapeDtypeStruct((2 * tenors, cols), BF16),
        in_specs=[SMEM] + [VMEM] * 3,
        out_specs=VMEM,
        scratch_shapes=[pltpu.VMEM((tenors * dates, path_dev), F32)],
        name="basis",
        compiler_params=pltpu.CompilerParams(vmem_limit_bytes=16 << 20),
        cost_estimate=pl.CostEstimate(
            flops=2 * 12 * tenors * tenors * cols, bytes_accessed=1 << 20, transcendentals=1 << 17
        ),
    )(me, shocks.reshape(tenors * dates, path_dev), forward_start.reshape(1, tenors), loading)

    need = 2 * owners * (packed_rows * LANES + rows * cols) + (12 << 20)
    partial = pl.pallas_call(
        functools.partial(main_kernel, owners, chunk, dates, paths, path_total),
        out_shape=jax.ShapeDtypeStruct((8 * owners, LANES), F32),
        in_specs=[VMEM] * 3,
        out_specs=VMEM,
        scratch_shapes=[
            pltpu.VMEM((owners * groups // chunk, chunk * LANES, cols), BF16),
            pltpu.VMEM((2 * owners * AG_DEV, cols), F32),
        ],
        name="value_and_allocate",
        compiler_params=pltpu.CompilerParams(vmem_limit_bytes=need),
    )(gathered, basis, ns_of_trade.reshape(owners * groups, LANES))

    total = lax.psum(partial, ("trade", "path"))
    own = lax.dynamic_slice_in_dim(total, 8 * me[0], 8, 0)
    allocation = own[0:groups].reshape(rows) * notional
    local = cpty_of_agr - me[0] * default_weight.shape[0]
    spent = own[groups : groups + AG_DEV, 0]
    picks = local[None, :] == jnp.arange(default_weight.shape[0], dtype=jnp.int32)[:, None]
    cva = jnp.sum(jnp.where(picks, spent[None, :], 0.0), axis=1)
    return (allocation, cva)


def solution(mesh):
    placed = (
        P(None, None, "path"),
        P(),
        P(),
        P("trade", None),
        P("trade"),
        P(),
        P("trade"),
        P("trade"),
        P("trade"),
        P("trade", None),
    )
    return jax.shard_map(
        body, mesh=mesh, in_specs=placed, out_specs=(P("trade"), P("trade")), check_vma=False
    )
```

time: 64.7 us -> 109 us (1.68)
  waiting for transfers between devices: 6.92 us -> 42.1 us
  blocking collectives: 6.24 us -> 39.2 us
  starting transfers between devices: 13.3 us -> 0.04 us
  between operations: 0.95 us -> 14.1 us
  local copies, waits for them, and re-layouts: 16 us -> 4.7 us
  matrix products: 10.3 us -> 0 us
  other arithmetic: 10.5 us -> 1.22 us
  Pallas kernels: 0 us -> 7.49 us
    all_gather x0 -> x1, waiting for transfers between devices: none -> 42.1 us  [body(): gathered = lax.all_gather(packed, 'trade', axis=0, tiled=False)]
    psum x1, blocking collectives: 6.24 us -> 39.2 us  [body(): total = lax.psum(partial, ('trade', 'path'))]
    all_to_all x2 -> x0, starting transfers between devices: 13.3 us -> none  [the longest x1 7.28 us: body(): lax.all_to_all(outgoing.astype(jnp.bfloat16), 'trade', split_axis=0, conc...]
    dot_general x10 -> x0, matrix products: 10.3 us -> none  [the longest x1 4.54 us: price_rows(): underlying = jnp.dot(coef_rows, basis, preferred_element_type=jnp.float32)]
    pallas_call x0 -> x3, Pallas kernels: none -> 7.49 us  [the longest x1 4.13 us: body(): pl.pallas_call(functools.partial(main_kernel, owners, chunk, dates, paths...]
    all_to_all x2 -> x0, waiting for transfers between devices: 6.92 us -> none  [the longest x1 6.91 us: body(): lax.all_to_all(slot_grads, 'trade', split_axis=0, concat_axis=0, tiled=True)]
    dot_general x1 -> x0, other arithmetic: 5.81 us -> none  [body(): jnp.einsum('ic,ic->i', values, grad_rows, preferred_element_type=jnp.floa...]
    unnamed x19 -> x15, local copies, waits for them, and re-layouts: 9.09 us -> 4.57 us
  transfers between devices with their start and end apart: 2 -> 1, of which waited for: 1 -> 1; matrix products, arithmetic and copies ran while one was open for 16% -> 0% of each run, Pallas kernels for 0% -> 1%
where the time goes in v1:
time: 109 us
  waiting for transfers between devices  42.1 us (39%)
  blocking collectives  39.2 us (36%)
  between operations  14.1 us (13%)
  Pallas kernels  7.49 us (7%)
  local copies, waits for them, and re-layouts  4.7 us (4%)
  other arithmetic  1.22 us (1%)
    all_gather x1, waiting for transfers between devices, body(): gathered = lax.all_gather(packed, 'trade', axis=0, tiled=False)  42.1 us
    psum x1, blocking collectives, body(): total = lax.psum(partial, ('trade', 'path'))  39.2 us
    unnamed x15, local copies, waits for them, and re-layouts  4.57 us
    pallas_call x1, Pallas kernels, body(): pl.pallas_call(functools.partial(main_kernel, owners, chunk, dates, paths...  4.13 us
  transfers between devices with their start and end apart: 1, of which 1 were waited for; matrix products, arithmetic and copies ran while one was open for 0% of the time, Pallas kernels for 1%

profile of v1, /device:TPU:0, one launch (start us, length us, event | category | flops | bytes accessed | tf_op | source)
XLA Modules:
  0.0 108.9 jit_solution(4762824126300808231)
XLA Ops:
  7.2 0.0 copy-start.6
  7.2 0.0 copy-start.1
  7.2 0.0 copy-start.3
  7.2 0.0 all-gather.3.cloned.1.call-start
  7.2 1.8 %copy.14.coef_ref = bf16[512,160]{1,0:T(8,128)(2,1)} copy(bf16[512,160]{0,1:T(8,128)(2,1)} %param.13) | data formatting | bytes 327680 | tf_op args[3]
  9.0 1.8 %pack.1 = bf16[656,128]{1,0:T(8,128)(2,1)} custom-call(s32[1]{0:T(128)} %bitcast.me_ref, s32[8]{0:T(128)} %agr_ref.1, s32[4]{0:T(128)} %cpty_ref.1, s32[4]{0:T(128)} %lag_ref.1, bf16[512,160]{1,0:T(8,128)(2,1)} %copy.14.coef_ref, f32[4,128]{1,0:T(4,128)} %bitcast.12, f32[4,32]{1,0:T(4,128)} %weight_ref.1), custom_call_target="tpu_custom_call" | custom-call | tf_op jit(solution)/shard_map/pack/pallas_call | solution.py:254
  10.8 0.0 copy-start.5
  10.8 0.0 all-gather.3.cloned.1.call-update
  10.8 0.0 copy-done.1
  10.8 0.0 copy-start.2
  10.8 0.8 copy-done.2
  11.6 0.0 copy-start.4
  11.6 0.7 copy-done.4
  12.3 1.6 %basis.1.basis_ref = bf16[160,512]{1,0:T(8,128)(2,1)S(1)} custom-call(s32[1]{0:T(128)} %bitcast.me_ref, bf16[2560,128]{1,0:T(8,128)(2,1)S(1)} %bitcast.9, f32[1,80]{1,0:T(1,128)S(1)} %bitcast.11, f32[80,80]{1,0:T(8,128)S(1)} %copy-done.2), custom_call_target="tpu_custom_call" | custom-call | flops 78643200 | bytes 1048576 | tf_op jit(solution)/shard_map/basis/pallas_call | solution.py:271
  13.9 0.0 copy-done.6
  13.9 42.1 %all-gather.3.cloned.1.call-done = bf16[5248,128]{1,0:T(8,128)(2,1)} async-done(((bf16[656,128]{1,0:T(8,128)(2,1)}), bf16[5248,128]{1,0:T(8,128)(2,1)}) %all-gather.3.cloned.1.call-update) | async-done | bytes 1343504 | tf_op jit(solution)/shard_map/all_gather | solution.py:269
  56.0 0.0 copy-done.3
  56.0 0.0 copy-start
  56.0 1.3 %copy-done = bf16[5248,128]{1,0:T(8,128)(2,1)S(1)} copy-done((bf16[5248,128]{1,0:T(8,128)(2,1)S(1)}, bf16[5248,128]{1,0:T(8,128)(2,1)}, u32[]{:S(2)}) %copy-start) | copy-done | bytes 1343512
  57.3 4.1 %value_and_allocate.1 = f32[64,128]{1,0:T(8,128)S(1)} custom-call(bf16[8,656,128]{2,1,0:T(8,128)(2,1)S(1)} %bitcast.8, bf16[160,512]{1,0:T(8,128)(2,1)S(1)} %basis.1.basis_ref, s32[32,128]{1,0:T(8,128)S(1)} %bitcast.10), custom_call_target="tpu_custom_call" | custom-call | tf_op jit(solution)/shard_map/value_and_allocate/pallas_call | solution.py:285
  61.5 39.2 %psum.7 = f32[64,128]{1,0:T(8,128)S(1)} all-reduce(f32[64,128]{1,0:T(8,128)S(1)} %value_and_allocate.1), channel_id=1, replica_groups=mesh['trade'=8,'path'=4] {'trade','path'}, use_global_device_ids=true, to_apply=%region_0.0 | all-reduce | flops 8192 | bytes 65536 | tf_op jit(solution)/shard_map/psum | solution.py:298
  100.7 0.0 copy-done.5
  100.7 0.6 bitcast_multiply_fusion
  101.3 0.1 slice_reduce_fusion
  101.4 0.6 select_reduce_fusion
  (2 shorter events, 0.0 us)
Async XLA Ops:
  7.2 6.7 %copy-start.6 = (s32[4]{0:T(128)S(1)}, s32[4]{0:T(128)}, u32[]{:S(2)}) copy-start(s32[4]{0:T(128)} %cpty_ref.1) | copy-start | bytes 52
  7.2 3.7 %copy-start.1 = (bf16[80,32,128]{2,1,0:T(8,128)(2,1)S(1)}, bf16[80,32,128]{2,1,0:T(8,128)(2,1)}, u32[]{:S(2)}) copy-start(bf16[80,32,128]{2,1,0:T(8,128)(2,1)} %param.10) | copy-start | bytes 1966084
  7.2 48.8 %copy-start.3 = (s32[4096]{0:T(1024)S(1)}, s32[4096]{0:T(1024)}, u32[]{:S(2)}) copy-start(s32[4096]{0:T(1024)} %param.15) | copy-start | bytes 49156
  7.2 48.8 %all-gather.3.cloned.1.call-start = ((), (), s32[]{:S(2)}) async-start(), calls=%async_computation | async-start | bytes 1511424 | tf_op jit(solution)/shard_map/all_gather | solution.py:269
  10.8 89.9 %copy-start.5 = (f32[512]{0:T(512)S(1)}, f32[512]{0:T(512)}, u32[]{:S(2)}) copy-start(f32[512]{0:T(512)} %param.14) | copy-start | bytes 6148
  10.8 0.8 copy-start.2
  11.6 0.7 copy-start.4
  56.0 1.3 %copy-start = (bf16[5248,128]{1,0:T(8,128)(2,1)S(1)}, bf16[5248,128]{1,0:T(8,128)(2,1)}, u32[]{:S(2)}) copy-start(bf16[5248,128]{1,0:T(8,128)(2,1)} %all-gather.3.cloned.1.call-done) | copy-start | bytes 4030468
Sparse Core Ops, SparseCore 0:
  10.9 45.0 all-gather.2

commit v2 on v0

v2 whole, which is shorter than its diff:
```python
import functools

import jax
import jax.numpy as jnp
from jax import lax
from jax.experimental import pallas as pl
from jax.experimental.pallas import tpu as pltpu
from jax.sharding import PartitionSpec as P

NS_DEV = 8
AG_DEV = 4
LAG_MAX = 4
LANES = 128
SUBS = 8
DIRECT = 16

RATE_UNIT = 0.03
STEP = 0.25
SMOOTH = 0.5

F32 = jnp.float32
BF16 = jnp.bfloat16
VMEM = pl.BlockSpec(memory_space=pltpu.VMEM)
SMEM = pl.BlockSpec(memory_space=pltpu.SMEM)
BOTH_LANES = (((1,), (1,)), ((), ()))


def iota(shape, dim):
    return lax.broadcasted_iota(jnp.int32, shape, dim)


def mask_bf16(mask):
    return mask.astype(F32).astype(BF16)


def split_bf16(x, parts):
    pieces = []
    for _ in range(parts):
        piece = x.astype(BF16)
        pieces.append(piece)
        x = x - piece.astype(F32)
    return pieces


def in_a_row(x):
    return jnp.concatenate([x[r : r + 1] for r in range(x.shape[0])], axis=1)


class Plan:
    def __init__(self, owners, rows, tenors, dates):
        most = 3 * rows // (2 * owners)
        self.owners = owners
        self.direct = owners <= DIRECT
        self.groups = 3 if most % 48 == 0 else 1
        self.part = -(-most // (16 * self.groups)) * 16
        self.room = self.groups * self.part
        self.height = self.room + self.part
        self.extra = 2 * tenors - LANES
        self.per_line = LANES // self.part
        self.lines = owners * self.part // LANES
        self.trades = owners * self.room
        self.tile = -(-(self.groups * self.lines + 1) // SUBS) * SUBS
        self.dates = dates
        self.width = 512


def pack_kernel(plan, me_ref, sets_ref, coef_ref, notional_ref, place_ref, *out_refs):
    me = me_ref[0]
    owners, part, room, extra = plan.owners, plan.part, plan.room, plan.extra
    lines = notional_ref.shape[0]
    rows = lines * LANES
    shared = SUBS // lines
    block = sets_ref[pl.ds(pl.multiple_of(me // shared * SUBS, SUBS), SUBS), :]
    own = block[0:lines]
    for b in range(1, shared):
        own = jnp.where(lax.rem(me, shared) == b, block[b * lines : (b + 1) * lines], own)
    sets = in_a_row(own)
    key = lax.shift_right_logical(sets, 3)
    local = sets - key * NS_DEV
    if plan.direct:
        key = lax.bitwise_xor(key, me)
    hot = iota((owners, rows), 0) == key
    before = mask_bf16(iota((rows, rows), 0) < iota((rows, rows), 1))
    count = jnp.dot(mask_bf16(hot), before, preferred_element_type=F32)
    rank = jnp.sum(jnp.where(hot, count, 0.0), axis=0, keepdims=True)
    place_ref[...] = jnp.concatenate(
        [key.astype(F32), rank, jnp.zeros((SUBS - 2, rows), F32)], axis=0
    )
    spot = key * room + rank.astype(jnp.int32)
    chosen = mask_bf16(iota((owners * room, rows), 0) == spot)
    notional = in_a_row(notional_ref[...])
    high = notional.astype(BF16).astype(F32)
    info = jnp.concatenate(
        [high, notional - high, local.astype(F32), jnp.zeros((13, rows), F32)], axis=0
    )
    table = jnp.concatenate([coef_ref[...], info.astype(BF16)], axis=0)
    moved = lax.dot_general(chosen, table, BOTH_LANES, preferred_element_type=F32)
    ids = LANES + extra
    for d in range(owners):
        message = out_refs[d] if plan.direct else out_refs[0].at[d]
        block = moved[d * room : (d + 1) * room]
        message[0:room, :] = block[:, 0:LANES].astype(BF16)
        split = [block[part * g : part * (g + 1)] for g in range(plan.groups)]
        lanes = [x[:, LANES:ids] for x in split]
        if plan.groups < 3:
            lanes.append(jnp.zeros((part, extra * (3 - plan.groups)), F32))
        lanes += [x[:, ids : ids + SUBS] for x in split]
        lanes.append(jnp.zeros((part, SUBS * (4 - plan.groups)), F32))
        message[room:, :] = jnp.concatenate(lanes, axis=1).astype(BF16)


def basis_kernel(plan, shocks_ref, start_ref, loading_ref, out_ref, wide_ref):
    tenors = loading_ref.shape[0]
    dates = plan.dates
    wide_ref[...] = shocks_ref[...].astype(F32)
    loading_t = jnp.transpose(loading_ref[...])
    drift = 0.5 * STEP * jnp.sum(loading_t * loading_t, axis=1, keepdims=True)
    diag = iota((tenors, tenors), 0) == iota((tenors, tenors), 1)
    log_start = jnp.log(jnp.sum(jnp.where(diag, start_ref[...], 0.0), axis=1, keepdims=True))
    loads = jnp.concatenate(split_bf16((STEP**0.5) * loading_t, 3), axis=1)
    lower = mask_bf16(iota((tenors, tenors), 1) <= iota((tenors, tenors), 0))
    lower = jnp.concatenate([lower, lower], axis=1)
    log_fwd = jnp.broadcast_to(log_start, (tenors, LANES))
    drift = jnp.broadcast_to(drift, (tenors, LANES))
    head = LANES - tenors
    step = plan.width // LANES
    for c in range(dates // step):
        shock = jnp.concatenate(
            [
                wide_ref[pl.ds(c * step + j, tenors, stride=dates), :].astype(BF16)
                for j in range(step)
            ],
            axis=1,
        )
        change = jnp.dot(
            loads, jnp.concatenate([shock] * 3, axis=0), preferred_element_type=F32
        )
        logs = []
        for j in range(step):
            log_fwd = log_fwd + (change[:, LANES * j : LANES * (j + 1)] - drift)
            logs.append(log_fwd)
        fwd = jnp.exp(jnp.concatenate(logs, axis=1))
        growth = split_bf16(jnp.log(1.0 + STEP * fwd), 2)
        summed = jnp.dot(lower, jnp.concatenate(growth, axis=0), preferred_element_type=F32)
        bond = jnp.exp(-summed)
        cols = slice(c * plan.width, (c + 1) * plan.width)
        out_ref[0:tenors, cols] = (bond * fwd * (1.0 / RATE_UNIT)).astype(BF16)
        bond = bond.astype(BF16)
        out_ref[tenors:LANES, cols] = bond[0:head]
        for g in range(plan.groups):
            out_ref[LANES + plan.extra * g : LANES + plan.extra * (g + 1), cols] = bond[head:]
        used = LANES + plan.extra * plan.groups
        out_ref[used:, cols] = jnp.zeros((2 * LANES - used, plan.width), BF16)


def main_kernel(plan, path_total, me_ref, agr_ref, cpty_ref, lag_ref, weight_ref, basis_ref, *refs):
    *in_refs, out_ref, val_ref = refs
    me = me_ref[0]
    part, room, dates = plan.part, plan.room, plan.dates
    cpty_dev = weight_ref.shape[0]

    def rows_of(first):
        if plan.direct:
            return jnp.concatenate([ref[first : first + part, :] for ref in in_refs], axis=0)
        return in_refs[0][:, first : first + part, :].reshape(plan.owners * part, LANES)

    rest = rows_of(room)
    lane = iota((1, LANES), 1)
    left, info = [], []
    for g in range(plan.groups):
        keep = mask_bf16((lane >= plan.extra * g) & (lane < plan.extra * (g + 1)))
        left.append(jnp.concatenate([rows_of(part * g), rest * keep], axis=1))
        pick = mask_bf16(iota((SUBS, LANES), 1) == 3 * plan.extra + SUBS * g + iota((SUBS, LANES), 0))
        info.append(lax.dot_general(pick, rest, BOTH_LANES, preferred_element_type=F32))
    left = jnp.concatenate(left, axis=0)
    info = jnp.concatenate(info, axis=1)
    local = info[2:3].astype(jnp.int32)
    agr = jnp.zeros_like(local)
    for n in range(NS_DEV):
        agr = jnp.where(local == n, agr_ref[n] - me * AG_DEV, agr)
    row = iota((SUBS, plan.trades), 0)
    hot = lax.rem(row, AG_DEV) == agr
    netting = jnp.where(hot, jnp.where(row < AG_DEV, info[0:1], info[1:2]), 0.0).astype(BF16)

    owed = []
    width = plan.width
    chunks = dates * LANES // width
    for c in range(chunks):
        under = jnp.dot(
            left, basis_ref[:, c * width : (c + 1) * width], preferred_element_type=F32
        )
        value = jnp.maximum(under, 0.0).astype(BF16)
        val_ref[c] = value
        both = jnp.dot(netting, value, preferred_element_type=F32)
        both = both + pltpu.roll(both, AG_DEV, 0)
        owed += [both[:, LANES * j : LANES * (j + 1)] for j in range(width // LANES)]

    member = lax.rem(iota((SUBS, LANES), 0), AG_DEV)
    lag = jnp.zeros((SUBS, LANES), jnp.int32)
    cpty = jnp.zeros((SUBS, LANES), jnp.int32)
    for a in range(AG_DEV):
        lag = jnp.where(member == a, lag_ref[a], lag)
        cpty = jnp.where(member == a, cpty_ref[a] - me * cpty_dev, cpty)
    lags = [lag == s for s in range(1, LAG_MAX + 1)]
    weight = jnp.zeros((SUBS, dates), F32)
    for c in range(cpty_dev):
        weight = jnp.where(cpty[:, 0:dates] == c, weight_ref[c : c + 1, :], weight)
    zero = jnp.zeros((SUBS, LANES), F32)
    spent, slopes = zero, []
    for t in range(dates):
        before = zero
        for s in range(1, min(t, LAG_MAX) + 1):
            before = jnp.where(lags[s - 1], owed[t - s], before)
        excess = owed[t] - before
        square = excess * excess + SMOOTH * SMOOTH
        root = jnp.sqrt(square)
        due = weight[:, t : t + 1]
        spent = spent + due * (0.5 * (excess + root))
        slopes.append(due * (0.5 * (1.0 + excess / root)))
    grads = []
    for t in range(dates):
        after = zero
        for s in range(1, min(dates - 1 - t, LAG_MAX) + 1):
            after = jnp.where(lags[s - 1], slopes[t + s], after)
        grads.append(((slopes[t] - after) * (1.0 / path_total)).astype(BF16))

    dots = jnp.zeros((SUBS, plan.trades), F32)
    step = width // LANES
    for c in range(chunks):
        part_grads = jnp.concatenate(grads[c * step : (c + 1) * step], axis=1)
        dots = dots + lax.dot_general(
            part_grads, val_ref[c], BOTH_LANES, preferred_element_type=F32
        )
    share = jnp.sum(jnp.where(hot & (row < AG_DEV), dots, 0.0), axis=0, keepdims=True)
    lines = [share[:, LANES * k : LANES * (k + 1)] for k in range(plan.trades // LANES)]
    spent = jnp.sum(spent, axis=1, keepdims=True) * (1.0 / path_total)
    mine = (lane == cpty) & (iota((SUBS, LANES), 0) < AG_DEV)
    lines.append(jnp.sum(jnp.where(mine, spent, 0.0), axis=0, keepdims=True))
    if len(lines) < plan.tile:
        lines.append(jnp.zeros((plan.tile - len(lines), LANES), F32))
    out_ref[...] = jnp.concatenate(lines, axis=0)


def finish_kernel(plan, me_ref, place_ref, notional_ref, own_ref, *refs):
    *in_refs, alloc_ref, cva_ref = refs
    me = me_ref[0]
    part, per_line = plan.part, plan.per_line
    rows = place_ref.shape[1]
    key = place_ref[0:1, :].astype(jnp.int32)
    rank = place_ref[1:2, :].astype(jnp.int32)
    group = lax.div(rank, part)
    slot = key if plan.direct else jnp.full_like(key, me)
    line = group * plan.lines + lax.div(slot, per_line)
    lane = lax.rem(slot, per_line) * part + (rank - group * part)
    if plan.direct:
        tiles = jnp.concatenate([ref[...] for ref in in_refs], axis=0)
    else:
        tiles = in_refs[0][...].reshape(plan.owners * plan.tile, LANES)
    hot = mask_bf16(iota((LANES, rows), 0) == lane)
    found = jnp.zeros((tiles.shape[0], rows), F32)
    for piece in split_bf16(tiles, 3):
        found = found + jnp.dot(piece, hot, preferred_element_type=F32)
    wanted = iota(found.shape, 0) == key * plan.tile + line
    share = jnp.sum(jnp.where(wanted, found, 0.0), axis=0, keepdims=True)
    alloc_ref[...] = share * in_a_row(notional_ref[...])
    last = plan.groups * plan.lines
    cva_ref[...] = own_ref[last : last + 1, 0 : cva_ref.shape[1]]


def permuted(x, axis, size, d):
    return lax.ppermute(x, axis, [(i, i ^ d) for i in range(size)])


def body(
    shocks,
    forward_start,
    loading,
    coefficient,
    notional,
    ns_of_trade,
    agr_of_ns,
    cpty_of_agr,
    margin_lag,
    default_weight,
):
    owners = lax.axis_size("trade")
    path_parts = lax.axis_size("path")
    tenors, dates, path_dev = shocks.shape
    path_total = float(path_dev * path_parts)
    rows = coefficient.shape[0]
    lines = rows // LANES
    plan = Plan(owners, rows, tenors, dates)
    cols = dates * path_dev
    me = lax.axis_index("trade").astype(jnp.int32).reshape(1)
    notional = notional.reshape(lines, LANES)

    message = jax.ShapeDtypeStruct((plan.height, LANES), BF16)
    if plan.direct:
        messages = [message] * owners
    else:
        messages = [jax.ShapeDtypeStruct((owners,) + message.shape, BF16)]
    place, *outgoing = pl.pallas_call(
        functools.partial(pack_kernel, plan),
        out_shape=[jax.ShapeDtypeStruct((SUBS, rows), F32)] + messages,
        in_specs=[SMEM] + [VMEM] * 3,
        out_specs=[VMEM] * (1 + len(messages)),
        name="pack",
        compiler_params=pltpu.CompilerParams(vmem_limit_bytes=24 << 20),
    )(me, ns_of_trade.reshape(owners * lines, LANES), coefficient.T, notional)
    if plan.direct:
        incoming = [outgoing[0]] + [
            permuted(outgoing[d], "trade", owners, d) for d in range(1, owners)
        ]
    else:
        incoming = [lax.all_to_all(outgoing[0], "trade", split_axis=0, concat_axis=0, tiled=True)]

    basis = pl.pallas_call(
        functools.partial(basis_kernel, plan),
        out_shape=jax.ShapeDtypeStruct((2 * LANES, cols), BF16),
        in_specs=[VMEM] * 3,
        out_specs=VMEM,
        scratch_shapes=[pltpu.VMEM((tenors * dates, path_dev), F32)],
        name="basis",
        compiler_params=pltpu.CompilerParams(vmem_limit_bytes=16 << 20),
        cost_estimate=pl.CostEstimate(
            flops=2 * 400 * tenors * cols, bytes_accessed=4 << 20, transcendentals=3 * tenors * cols
        ),
    )(shocks.reshape(tenors * dates, path_dev), forward_start.reshape(1, tenors), loading)

    need = 2 * plan.trades * cols + 16 * plan.trades * plan.width + (8 << 20)
    tile = pl.pallas_call(
        functools.partial(main_kernel, plan, path_total),
        out_shape=jax.ShapeDtypeStruct((plan.tile, LANES), F32),
        in_specs=[SMEM] * 4 + [VMEM] * (2 + len(incoming)),
        out_specs=VMEM,
        scratch_shapes=[pltpu.VMEM((cols // plan.width, plan.trades, plan.width), BF16)],
        name="value_and_allocate",
        compiler_params=pltpu.CompilerParams(vmem_limit_bytes=need),
    )(me, agr_of_ns, cpty_of_agr, margin_lag, default_weight, basis, *incoming)

    others = [permuted(tile, "path", path_parts, d) for d in range(1, path_parts)]
    for other in others:
        tile = tile + other
    if plan.direct:
        tiles = [tile] + [permuted(tile, "trade", owners, d) for d in range(1, owners)]
    else:
        tiles = [lax.all_gather(tile, "trade", axis=0, tiled=False)]
    allocation, cva = pl.pallas_call(
        functools.partial(finish_kernel, plan),
        out_shape=[
            jax.ShapeDtypeStruct((1, rows), F32),
            jax.ShapeDtypeStruct((1, default_weight.shape[0]), F32),
        ],
        in_specs=[SMEM] + [VMEM] * (3 + len(tiles)),
        out_specs=[VMEM, VMEM],
        name="finish",
        compiler_params=pltpu.CompilerParams(vmem_limit_bytes=32 << 20),
    )(me, place, notional, tile, *tiles)
    return (allocation.reshape(rows), cva.reshape(default_weight.shape[0]))


def solution(mesh):
    placed = (
        P(None, None, "path"),
        P(),
        P(),
        P("trade", None),
        P("trade"),
        P(),
        P("trade"),
        P("trade"),
        P("trade"),
        P("trade", None),
    )
    return jax.shard_map(
        body, mesh=mesh, in_specs=placed, out_specs=(P("trade"), P("trade")), check_vma=False
    )
```

time: 64.7 us -> 47.1 us (0.73)
  starting transfers between devices: 13.3 us -> 25.6 us
  local copies, waits for them, and re-layouts: 16 us -> 4.87 us
  other arithmetic: 10.5 us -> 0.01 us
  matrix products: 10.3 us -> 0 us
  Pallas kernels: 0 us -> 10.1 us
  blocking collectives: 6.24 us -> 0 us
  waiting for transfers between devices: 6.92 us -> 5.35 us
    ppermute x0 -> x17, starting transfers between devices: none -> 25.6 us  [permuted(): return lax.ppermute(x, axis, [(i, i ^ d) for i in range(size)])]
    all_to_all x2 -> x0, starting transfers between devices: 13.3 us -> none  [the longest x1 7.28 us: body(): lax.all_to_all(outgoing.astype(jnp.bfloat16), 'trade', split_axis=0, conc...]
    dot_general x10 -> x0, matrix products: 10.3 us -> none  [the longest x1 4.54 us: price_rows(): underlying = jnp.dot(coef_rows, basis, preferred_element_type=jnp.float32)]
    pallas_call x0 -> x4, Pallas kernels: none -> 10.1 us  [the longest x1 6.15 us: body(): pl.pallas_call(functools.partial(main_kernel, plan, path_total), out_shap...]
    all_to_all x2 -> x0, waiting for transfers between devices: 6.92 us -> none  [the longest x1 6.91 us: body(): lax.all_to_all(slot_grads, 'trade', split_axis=0, concat_axis=0, tiled=True)]
    psum x1 -> x0, blocking collectives: 6.24 us -> none  [body(): allocation = lax.psum(alloc_part, 'path')]
    dot_general x1 -> x0, other arithmetic: 5.81 us -> none  [body(): jnp.einsum('ic,ic->i', values, grad_rows, preferred_element_type=jnp.floa...]
    ppermute x0 -> x17, waiting for transfers between devices: none -> 5.35 us  [permuted(): return lax.ppermute(x, axis, [(i, i ^ d) for i in range(size)])]
  transfers between devices with their start and end apart: 2 -> 17, of which waited for: 1 -> 6; matrix products, arithmetic and copies ran while one was open for 16% -> 0% of each run, Pallas kernels for 0% -> 6%
where the time goes in v2:
time: 47.1 us; the launch traced here: 46.8 us
  starting transfers between devices  25.6 us (54%)
  Pallas kernels  10.1 us (21%)
  waiting for transfers between devices  5.35 us (11%)
  local copies, waits for them, and re-layouts  4.87 us (10%)
  between operations  0.77 us (2%)
    ppermute x17, starting transfers between devices, permuted(): return lax.ppermute(x, axis, [(i, i ^ d) for i in range(size)])  25.6 us
    pallas_call x1, Pallas kernels, body(): pl.pallas_call(functools.partial(main_kernel, plan, path_total), out_shap...  6.15 us
    ppermute x17, waiting for transfers between devices, permuted(): return lax.ppermute(x, axis, [(i, i ^ d) for i in range(size)])  5.35 us
    unnamed x22, local copies, waits for them, and re-layouts  4.87 us
    pallas_call x1, Pallas kernels, body(): pl.pallas_call(functools.partial(basis_kernel, plan), out_shape=jax.Shape...  2.61 us
  transfers between devices with their start and end apart: 17, of which 6 were waited for; matrix products, arithmetic and copies ran while one was open for 0% of the time, Pallas kernels for 6%

profile of v2, /device:TPU:0, one launch (start us, length us, event | category | flops | bytes accessed | tf_op | source)
XLA Modules:
  0.0 46.8 jit_solution(2336649721734689964)
XLA Ops:
  0.6 0.0 copy-start.6
  0.6 0.0 copy-start.10
  0.7 0.0 copy-start.9
  0.7 0.0 copy-start.8
  0.7 0.9 %copy-done.1 = bf16[512,160]{0,1:T(8,128)(2,1)S(1)} copy-done((bf16[512,160]{0,1:T(8,128)(2,1)S(1)}, bf16[512,160]{0,1:T(8,128)(2,1)}, u32[]{:S(2)}) %copy-start.1) | copy-done | bytes 163864
  1.6 0.7 %copy-done.3 = s32[4096]{0:T(1024)S(1)} copy-done((s32[4096]{0:T(1024)S(1)}, s32[4096]{0:T(1024)}, u32[]{:S(2)}) %copy-start.3) | copy-done | bytes 16408
  2.3 0.7 %copy-done.4 = f32[512]{0:T(512)S(1)} copy-done((f32[512]{0:T(512)S(1)}, f32[512]{0:T(512)}, u32[]{:S(2)}) %copy-start.4) | copy-done | bytes 2072
  3.0 0.6 %pack.1 = (f32[8,512]{1,0:T(8,128)S(1)}, bf16[128,128]{1,0:T(8,128)(2,1)S(1)}, bf16[128,128]{1,0:T(8,128)(2,1)S(1)}, bf16[128,128]{1,0:T(8,128)(2,1)S(1)}, bf16[...) custom-call(s32[1]{0:T(128)} %bitcast.me_ref, ...), custom_call_target="tpu_custom_call" | custom-call | tf_op jit(solution)/shard_map/pack/pallas_call | solution.py:302
  3.6 3.0 %collective-permute-start = (bf16[128,128]{1,0:T(8,128)(2,1)S(1)}, bf16[128,128]{1,0:T(8,128)(2,1)S(1)}, u32[]{:S(2)}, u32[]{:S(2)}) collective-permute-start(bf16[128,128]{1,0:T(8,128)(2,1)S(1)} %get-tuple-element.15), channel_id=1, source_target_pairs={{0,4},{4,0},{8,12},{12,8},{16,20},{20,16},{24,28},{28,24},{1,5},{5... | collective-permute-start | bytes 98312 | tf_op jit(solution)/shard_map/ppermute | solution.py:271
  6.6 1.6 %collective-permute-start.1 = (bf16[128,128]{1,0:T(8,128)(2,1)S(1)}, bf16[128,128]{1,0:T(8,128)(2,1)S(1)}, u32[]{:S(2)}, u32[]{:S(2)}) collective-permute-start(bf16[128,128]{1,0:T(8,128)(2,1)S(1)} %get-tuple-element.16), channel_id=1, source_target_pairs={{0,8},{4,12},{8,0},{12,4},{16,24},{20,28},{24,16},{28,20},{1,9},{5... | collective-permute-start | bytes 98312 | tf_op jit(solution)/shard_map/ppermute | solution.py:271
  8.2 0.0 collective-permute-start.2
  8.2 3.0 %collective-permute-start.3 = (bf16[128,128]{1,0:T(8,128)(2,1)S(1)}, bf16[128,128]{1,0:T(8,128)(2,1)S(1)}, u32[]{:S(2)}, u32[]{:S(2)}) collective-permute-start(bf16[128,128]{1,0:T(8,128)(2,1)S(1)} %get-tuple-element.18), channel_id=1, source_target_pairs={{0,16},{4,20},{8,24},{12,28},{16,0},{20,4},{24,8},{28,12},{1,17},{... | collective-permute-start | bytes 98312 | tf_op jit(solution)/shard_map/ppermute | solution.py:271
  11.2 1.3 %collective-permute-start.4 = (bf16[128,128]{1,0:T(8,128)(2,1)S(1)}, bf16[128,128]{1,0:T(8,128)(2,1)S(1)}, u32[]{:S(2)}, u32[]{:S(2)}) collective-permute-start(bf16[128,128]{1,0:T(8,128)(2,1)S(1)} %get-tuple-element.19), channel_id=1, source_target_pairs={{0,20},{4,16},{8,28},{12,24},{16,4},{20,0},{24,12},{28,8},{1,21},{... | collective-permute-start | bytes 98312 | tf_op jit(solution)/shard_map/ppermute | solution.py:271
  12.5 0.0 collective-permute-done.refs_1_
  12.5 3.6 %collective-permute-start.5 = (bf16[128,128]{1,0:T(8,128)(2,1)S(1)}, bf16[128,128]{1,0:T(8,128)(2,1)S(1)}, u32[]{:S(2)}, u32[]{:S(2)}) collective-permute-start(bf16[128,128]{1,0:T(8,128)(2,1)S(1)} %get-tuple-element.20), channel_id=1, source_target_pairs={{0,24},{4,28},{8,16},{12,20},{16,8},{20,12},{24,0},{28,4},{1,25},{... | collective-permute-start | bytes 98312 | tf_op jit(solution)/shard_map/ppermute | solution.py:271
  16.1 0.0 collective-permute-done.1.refs_2_
  16.1 0.0 collective-permute-start.6
  16.1 1.1 %copy-done = bf16[80,32,128]{2,1,0:T(8,128)(2,1)S(1)} copy-done((bf16[80,32,128]{2,1,0:T(8,128)(2,1)S(1)}, bf16[80,32,128]{2,1,0:T(8,128)(2,1)}, u32[]{:S(2)}) %copy-start) | copy-done | bytes 655384
  17.2 0.8 %copy-done.2 = f32[80,80]{1,0:T(8,128)S(1)} copy-done((f32[80,80]{1,0:T(8,128)S(1)}, f32[80,80]{1,0:T(8,128)}, u32[]{:S(2)}) %copy-start.2) | copy-done | bytes 25624
  18.0 0.7 %copy-done.7 = f32[80]{0:T(128)S(1)} copy-done((f32[80]{0:T(128)S(1)}, f32[80]{0:T(128)}, u32[]{:S(2)}) %copy-start.7) | copy-done | bytes 344
  18.6 2.6 %basis.1.basis_ref = bf16[256,4096]{1,0:T(8,128)(2,1)S(1)} custom-call(bf16[2560,128]{1,0:T(8,128)(2,1)S(1)} %bitcast.8, f32[1,80]{1,0:T(1,128)S(1)} %bitcast.13, f32[80,80]{1,0:T(8,128)S(1)} %copy-done.2), custom_call_target="tpu_custom_call" | custom-call | flops 262144000 | bytes 4194304 | tf_op jit(solution)/shard_map/basis/pallas_call | solution.py:317
  21.3 0.0 collective-permute-done.2.refs_3_
  21.3 0.0 collective-permute-done.3.refs_4_
  21.3 0.0 collective-permute-done.4.refs_5_
  21.3 0.0 collective-permute-done.5.refs_6_
  21.3 1.4 %collective-permute-done.6.refs_7_ = bf16[128,128]{1,0:T(8,128)(2,1)S(1)} collective-permute-done((bf16[128,128]{1,0:T(8,128)(2,1)S(1)}, bf16[128,128]{1,0:T(8,128)(2,1)S(1)}, u32[]{:S(2)}, u32[]{:S(2)}) %collective-permute-start.6) | collective-permute-done | bytes 32800 | tf_op jit(solution)/shard_map/ppermute | solution.py:271
  22.7 6.1 %value_and_allocate.1 = f32[8,128]{1,0:T(8,128)S(1)} custom-call(s32[1]{0:T(128)} %bitcast.me_ref, s32[8]{0:T(128)S(1)} %copy-done.8, s32[4]{0:T(128)S(1)} %copy-done.9, s32[4]{0:T(128)S(1)} %copy-done.10, f32[4,32]{1,0:T(4,128)S(1)} %copy-done.6, bf16[256,4096]{1,0:T(8,128)(2,1)S(1)} %basis.1.basis_ref, bf16[128,128]{1,0:T(8,128)(2,1)S(1)} %get-tuple-element.14.refs_0_, ...), custom_call_target="tpu_custom_call" | custom-call | tf_op jit(solution)/shard_map/value_and_allocate/pallas_call | solution.py:331
  28.9 0.1 collective-permute-start.9
  29.0 1.6 %collective-permute-start.8 = (f32[8,128]{1,0:T(8,128)S(1)}, f32[8,128]{1,0:T(8,128)S(1)}, u32[]{:S(2)}, u32[]{:S(2)}) collective-permute-start(f32[8,128]{1,0:T(8,128)S(1)} %value_and_allocate.1), channel_id=1, source_target_pairs={{0,2},{1,3},{2,0},{3,1},{4,6},{5,7},{6,4},{7,5},{8,10},{9,11},{10,... | collective-permute-start | bytes 12296 | tf_op jit(solution)/shard_map/ppermute | solution.py:271
  30.5 0.3 collective-permute-start.7
  30.8 1.2 %collective-permute-done.9 = f32[8,128]{1,0:T(8,128)S(1)} collective-permute-done((f32[8,128]{1,0:T(8,128)S(1)}, f32[8,128]{1,0:T(8,128)S(1)}, u32[]{:S(2)}, u32[]{:S(2)}) %collective-permute-start.9) | collective-permute-done | bytes 4128 | tf_op jit(solution)/shard_map/ppermute | solution.py:271
  32.0 0.7 %collective-permute-done.8 = f32[8,128]{1,0:T(8,128)S(1)} collective-permute-done((f32[8,128]{1,0:T(8,128)S(1)}, f32[8,128]{1,0:T(8,128)S(1)}, u32[]{:S(2)}, u32[]{:S(2)}) %collective-permute-start.8) | collective-permute-done | bytes 4128 | tf_op jit(solution)/shard_map/ppermute | solution.py:271
  32.6 0.0 collective-permute-done.7
  32.6 3.4 %collective-permute-start.16 = (f32[8,128]{1,0:T(8,128)S(1)}, f32[8,128]{1,0:T(8,128)S(1)}, u32[]{:S(2)}, u32[]{:S(2)}) collective-permute-start(f32[8,128]{1,0:T(8,128)S(1)} %add_add_fusion.own_ref.refs_0_), channel_id=1, source_target_pairs={{0,28},{4,24},{8,20},{12,16},{16,12},{20,8},{24,4},{28,0},{1,29},{... | collective-permute-start | bytes 12296 | tf_op jit(solution)/shard_map/ppermute | solution.py:271
  36.1 0.4 collective-permute-start.15
  36.5 0.0 collective-permute-start.14
  36.5 3.9 %collective-permute-start.13 = (f32[8,128]{1,0:T(8,128)S(1)}, f32[8,128]{1,0:T(8,128)S(1)}, u32[]{:S(2)}, u32[]{:S(2)}) collective-permute-start(f32[8,128]{1,0:T(8,128)S(1)} %add_add_fusion.own_ref.refs_0_), channel_id=1, source_target_pairs={{0,16},{4,20},{8,24},{12,28},{16,0},{20,4},{24,8},{28,12},{1,17},{... | collective-permute-start | bytes 12296 | tf_op jit(solution)/shard_map/ppermute | solution.py:271
  40.4 1.0 %collective-permute-start.12 = (f32[8,128]{1,0:T(8,128)S(1)}, f32[8,128]{1,0:T(8,128)S(1)}, u32[]{:S(2)}, u32[]{:S(2)}) collective-permute-start(f32[8,128]{1,0:T(8,128)S(1)} %add_add_fusion.own_ref.refs_0_), channel_id=1, source_target_pairs={{0,12},{4,8},{8,4},{12,0},{16,28},{20,24},{24,20},{28,16},{1,13},{... | collective-permute-start | bytes 12296 | tf_op jit(solution)/shard_map/ppermute | solution.py:271
  41.3 0.0 collective-permute-done.16.refs_7_
  41.3 1.0 %collective-permute-start.11 = (f32[8,128]{1,0:T(8,128)S(1)}, f32[8,128]{1,0:T(8,128)S(1)}, u32[]{:S(2)}, u32[]{:S(2)}) collective-permute-start(f32[8,128]{1,0:T(8,128)S(1)} %add_add_fusion.own_ref.refs_0_), channel_id=1, source_target_pairs={{0,8},{4,12},{8,0},{12,4},{16,24},{20,28},{24,16},{28,20},{1,9},{5... | collective-permute-start | bytes 12296 | tf_op jit(solution)/shard_map/ppermute | solution.py:271
  42.3 0.0 collective-permute-done.15.refs_6_
  42.4 1.5 %collective-permute-start.10 = (f32[8,128]{1,0:T(8,128)S(1)}, f32[8,128]{1,0:T(8,128)S(1)}, u32[]{:S(2)}, u32[]{:S(2)}) collective-permute-start(f32[8,128]{1,0:T(8,128)S(1)} %add_add_fusion.own_ref.refs_0_), channel_id=1, source_target_pairs={{0,4},{4,0},{8,12},{12,8},{16,20},{20,16},{24,28},{28,24},{1,5},{5... | collective-permute-start | bytes 12296 | tf_op jit(solution)/shard_map/ppermute | solution.py:271
  43.9 0.0 collective-permute-done.14.refs_5_
  43.9 0.0 collective-permute-done.13.refs_4_
  43.9 1.0 %collective-permute-done.12.refs_3_ = f32[8,128]{1,0:T(8,128)S(1)} collective-permute-done((f32[8,128]{1,0:T(8,128)S(1)}, f32[8,128]{1,0:T(8,128)S(1)}, u32[]{:S(2)}, u32[]{:S(2)}) %collective-permute-start.12) | collective-permute-done | bytes 4128 | tf_op jit(solution)/shard_map/ppermute | solution.py:271
  44.9 0.1 collective-permute-done.11.refs_2_
  45.0 1.0 %collective-permute-done.10.refs_1_ = f32[8,128]{1,0:T(8,128)S(1)} collective-permute-done((f32[8,128]{1,0:T(8,128)S(1)}, f32[8,128]{1,0:T(8,128)S(1)}, u32[]{:S(2)}, u32[]{:S(2)}) %collective-permute-start.10) | collective-permute-done | bytes 4128 | tf_op jit(solution)/shard_map/ppermute | solution.py:271
  46.0 0.8 %finish.1 = (f32[1,512]{1,0:T(1,128)}, f32[1,4]{1,0:T(1,128)}) custom-call(s32[1]{0:T(128)} %bitcast.me_ref, f32[8,512]{1,0:T(8,128)S(1)} %get-tuple-element.13.place_ref, f32[4,128]{1,0:T(4,128)S(1)} %bitcast.12, f32[8,128]{1,0:T(8,128)S(1)} %add_add_fusion.own_ref.refs_0_, f32[8,128]{1,0:T(8,128)S(1)} %add_add_fusion.own_ref.refs_0_, ...), custom_call_target="tpu_custom_call" | custom-call | tf_op jit(solution)/shard_map/finish/pallas_call | solution.py:348
  (13 shorter events, 0.0 us)
Async XLA Ops:
  0.6 22.1 %copy-start.6 = (f32[4,32]{1,0:T(4,128)S(1)}, f32[4,32]{1,0:T(4,128)}, u32[]{:S(2)}) copy-start(f32[4,32]{1,0:T(4,128)} %weight_ref.1) | copy-start | bytes 1540
  0.6 22.1 %copy-start.10 = (s32[4]{0:T(128)S(1)}, s32[4]{0:T(128)}, u32[]{:S(2)}) copy-start(s32[4]{0:T(128)} %lag_ref.1) | copy-start | bytes 52
  0.7 22.1 %copy-start.9 = (s32[4]{0:T(128)S(1)}, s32[4]{0:T(128)}, u32[]{:S(2)}) copy-start(s32[4]{0:T(128)} %cpty_ref.1) | copy-start | bytes 52
  0.7 22.1 %copy-start.8 = (s32[8]{0:T(128)S(1)}, s32[8]{0:T(128)}, u32[]{:S(2)}) copy-start(s32[8]{0:T(128)} %agr_ref.1) | copy-start | bytes 100
  0.7 0.9 %copy-start.1 = (bf16[512,160]{0,1:T(8,128)(2,1)S(1)}, bf16[512,160]{0,1:T(8,128)(2,1)}, u32[]{:S(2)}) copy-start(bf16[512,160]{0,1:T(8,128)(2,1)} %param.13) | copy-start | bytes 491524
  1.6 0.7 %copy-start.3 = (s32[4096]{0:T(1024)S(1)}, s32[4096]{0:T(1024)}, u32[]{:S(2)}) copy-start(s32[4096]{0:T(1024)} %param.15) | copy-start | bytes 49156
  2.3 0.7 %copy-start.4 = (f32[512]{0:T(512)S(1)}, f32[512]{0:T(512)}, u32[]{:S(2)}) copy-start(f32[512]{0:T(512)} %param.14) | copy-start | bytes 6148
  3.6 8.9 %collective-permute-start = (bf16[128,128]{1,0:T(8,128)(2,1)S(1)}, bf16[128,128]{1,0:T(8,128)(2,1)S(1)}, u32[]{:S(2)}, u32[]{:S(2)}) collective-permute-start(bf16[128,128]{1,0:T(8,128)(2,1)S(1)} %get-tuple-element.15), channel_id=1, source_target_pairs={{0,4},{4,0},{8,12},{12,8},{16,20},{20,16},{24,28},{28,24},{1,5},{5... | collective-permute-start | bytes 98312 | tf_op jit(solution)/shard_map/ppermute | solution.py:271
  6.6 9.5 %collective-permute-start.1 = (bf16[128,128]{1,0:T(8,128)(2,1)S(1)}, bf16[128,128]{1,0:T(8,128)(2,1)S(1)}, u32[]{:S(2)}, u32[]{:S(2)}) collective-permute-start(bf16[128,128]{1,0:T(8,128)(2,1)S(1)} %get-tuple-element.16), channel_id=1, source_target_pairs={{0,8},{4,12},{8,0},{12,4},{16,24},{20,28},{24,16},{28,20},{1,9},{5... | collective-permute-start | bytes 98312 | tf_op jit(solution)/shard_map/ppermute | solution.py:271
  8.2 13.0 %collective-permute-start.2 = (bf16[128,128]{1,0:T(8,128)(2,1)S(1)}, bf16[128,128]{1,0:T(8,128)(2,1)S(1)}, u32[]{:S(2)}, u32[]{:S(2)}) collective-permute-start(bf16[128,128]{1,0:T(8,128)(2,1)S(1)} %get-tuple-element.17), channel_id=1, source_target_pairs={{0,12},{4,8},{8,4},{12,0},{16,28},{20,24},{24,20},{28,16},{1,13},{... | collective-permute-start | bytes 98312 | tf_op jit(solution)/shard_map/ppermute | solution.py:271
  8.2 13.1 %collective-permute-start.3 = (bf16[128,128]{1,0:T(8,128)(2,1)S(1)}, bf16[128,128]{1,0:T(8,128)(2,1)S(1)}, u32[]{:S(2)}, u32[]{:S(2)}) collective-permute-start(bf16[128,128]{1,0:T(8,128)(2,1)S(1)} %get-tuple-element.18), channel_id=1, source_target_pairs={{0,16},{4,20},{8,24},{12,28},{16,0},{20,4},{24,8},{28,12},{1,17},{... | collective-permute-start | bytes 98312 | tf_op jit(solution)/shard_map/ppermute | solution.py:271
  11.2 10.1 %collective-permute-start.4 = (bf16[128,128]{1,0:T(8,128)(2,1)S(1)}, bf16[128,128]{1,0:T(8,128)(2,1)S(1)}, u32[]{:S(2)}, u32[]{:S(2)}) collective-permute-start(bf16[128,128]{1,0:T(8,128)(2,1)S(1)} %get-tuple-element.19), channel_id=1, source_target_pairs={{0,20},{4,16},{8,28},{12,24},{16,4},{20,0},{24,12},{28,8},{1,21},{... | collective-permute-start | bytes 98312 | tf_op jit(solution)/shard_map/ppermute | solution.py:271
  12.5 8.8 %collective-permute-start.5 = (bf16[128,128]{1,0:T(8,128)(2,1)S(1)}, bf16[128,128]{1,0:T(8,128)(2,1)S(1)}, u32[]{:S(2)}, u32[]{:S(2)}) collective-permute-start(bf16[128,128]{1,0:T(8,128)(2,1)S(1)} %get-tuple-element.20), channel_id=1, source_target_pairs={{0,24},{4,28},{8,16},{12,20},{16,8},{20,12},{24,0},{28,4},{1,25},{... | collective-permute-start | bytes 98312 | tf_op jit(solution)/shard_map/ppermute | solution.py:271
  16.1 6.6 %collective-permute-start.6 = (bf16[128,128]{1,0:T(8,128)(2,1)S(1)}, bf16[128,128]{1,0:T(8,128)(2,1)S(1)}, u32[]{:S(2)}, u32[]{:S(2)}) collective-permute-start(bf16[128,128]{1,0:T(8,128)(2,1)S(1)} %get-tuple-element.21), channel_id=1, source_target_pairs={{0,28},{4,24},{8,20},{12,16},{16,12},{20,8},{24,4},{28,0},{1,29},{... | collective-permute-start | bytes 98312 | tf_op jit(solution)/shard_map/ppermute | solution.py:271
  16.1 1.1 %copy-start = (bf16[80,32,128]{2,1,0:T(8,128)(2,1)S(1)}, bf16[80,32,128]{2,1,0:T(8,128)(2,1)}, u32[]{:S(2)}) copy-start(bf16[80,32,128]{2,1,0:T(8,128)(2,1)} %param.10) | copy-start | bytes 1966084
  17.2 0.8 %copy-start.2 = (f32[80,80]{1,0:T(8,128)S(1)}, f32[80,80]{1,0:T(8,128)}, u32[]{:S(2)}) copy-start(f32[80,80]{1,0:T(8,128)} %loading_ref.1) | copy-start | bytes 76804
  18.0 0.7 %copy-start.7 = (f32[80]{0:T(128)S(1)}, f32[80]{0:T(128)}, u32[]{:S(2)}) copy-start(f32[80]{0:T(128)} %param.11) | copy-start | bytes 964
  18.6 27.3 %copy-start.5 = (f32[512]{0:T(512)S(1)}, f32[512]{0:T(512)}, u32[]{:S(2)}) copy-start(f32[512]{0:T(512)} %param.14) | copy-start | bytes 6148
  28.9 3.1 %collective-permute-start.9 = (f32[8,128]{1,0:T(8,128)S(1)}, f32[8,128]{1,0:T(8,128)S(1)}, u32[]{:S(2)}, u32[]{:S(2)}) collective-permute-start(f32[8,128]{1,0:T(8,128)S(1)} %value_and_allocate.1), channel_id=1, source_target_pairs={{0,3},{1,2},{2,1},{3,0},{4,7},{5,6},{6,5},{7,4},{8,11},{9,10},{10,... | collective-permute-start | bytes 12296 | tf_op jit(solution)/shard_map/ppermute | solution.py:271
  29.0 3.7 %collective-permute-start.8 = (f32[8,128]{1,0:T(8,128)S(1)}, f32[8,128]{1,0:T(8,128)S(1)}, u32[]{:S(2)}, u32[]{:S(2)}) collective-permute-start(f32[8,128]{1,0:T(8,128)S(1)} %value_and_allocate.1), channel_id=1, source_target_pairs={{0,2},{1,3},{2,0},{3,1},{4,6},{5,7},{6,4},{7,5},{8,10},{9,11},{10,... | collective-permute-start | bytes 12296 | tf_op jit(solution)/shard_map/ppermute | solution.py:271
  30.5 2.1 %collective-permute-start.7 = (f32[8,128]{1,0:T(8,128)S(1)}, f32[8,128]{1,0:T(8,128)S(1)}, u32[]{:S(2)}, u32[]{:S(2)}) collective-permute-start(f32[8,128]{1,0:T(8,128)S(1)} %value_and_allocate.1), channel_id=1, source_target_pairs={{0,1},{1,0},{2,3},{3,2},{4,5},{5,4},{6,7},{7,6},{8,9},{9,8},{10,11... | collective-permute-start | bytes 12296 | tf_op jit(solution)/shard_map/ppermute | solution.py:271
  32.6 8.7 %collective-permute-start.16 = (f32[8,128]{1,0:T(8,128)S(1)}, f32[8,128]{1,0:T(8,128)S(1)}, u32[]{:S(2)}, u32[]{:S(2)}) collective-permute-start(f32[8,128]{1,0:T(8,128)S(1)} %add_add_fusion.own_ref.refs_0_), channel_id=1, source_target_pairs={{0,28},{4,24},{8,20},{12,16},{16,12},{20,8},{24,4},{28,0},{1,29},{... | collective-permute-start | bytes 12296 | tf_op jit(solution)/shard_map/ppermute | solution.py:271
  36.1 6.3 %collective-permute-start.15 = (f32[8,128]{1,0:T(8,128)S(1)}, f32[8,128]{1,0:T(8,128)S(1)}, u32[]{:S(2)}, u32[]{:S(2)}) collective-permute-start(f32[8,128]{1,0:T(8,128)S(1)} %add_add_fusion.own_ref.refs_0_), channel_id=1, source_target_pairs={{0,24},{4,28},{8,16},{12,20},{16,8},{20,12},{24,0},{28,4},{1,25},{... | collective-permute-start | bytes 12296 | tf_op jit(solution)/shard_map/ppermute | solution.py:271
  36.5 7.4 %collective-permute-start.14 = (f32[8,128]{1,0:T(8,128)S(1)}, f32[8,128]{1,0:T(8,128)S(1)}, u32[]{:S(2)}, u32[]{:S(2)}) collective-permute-start(f32[8,128]{1,0:T(8,128)S(1)} %add_add_fusion.own_ref.refs_0_), channel_id=1, source_target_pairs={{0,20},{4,16},{8,28},{12,24},{16,4},{20,0},{24,12},{28,8},{1,21},{... | collective-permute-start | bytes 12296 | tf_op jit(solution)/shard_map/ppermute | solution.py:271
  36.5 7.4 %collective-permute-start.13 = (f32[8,128]{1,0:T(8,128)S(1)}, f32[8,128]{1,0:T(8,128)S(1)}, u32[]{:S(2)}, u32[]{:S(2)}) collective-permute-start(f32[8,128]{1,0:T(8,128)S(1)} %add_add_fusion.own_ref.refs_0_), channel_id=1, source_target_pairs={{0,16},{4,20},{8,24},{12,28},{16,0},{20,4},{24,8},{28,12},{1,17},{... | collective-permute-start | bytes 12296 | tf_op jit(solution)/shard_map/ppermute | solution.py:271
  40.4 4.5 %collective-permute-start.12 = (f32[8,128]{1,0:T(8,128)S(1)}, f32[8,128]{1,0:T(8,128)S(1)}, u32[]{:S(2)}, u32[]{:S(2)}) collective-permute-start(f32[8,128]{1,0:T(8,128)S(1)} %add_add_fusion.own_ref.refs_0_), channel_id=1, source_target_pairs={{0,12},{4,8},{8,4},{12,0},{16,28},{20,24},{24,20},{28,16},{1,13},{... | collective-permute-start | bytes 12296 | tf_op jit(solution)/shard_map/ppermute | solution.py:271
  41.3 3.6 %collective-permute-start.11 = (f32[8,128]{1,0:T(8,128)S(1)}, f32[8,128]{1,0:T(8,128)S(1)}, u32[]{:S(2)}, u32[]{:S(2)}) collective-permute-start(f32[8,128]{1,0:T(8,128)S(1)} %add_add_fusion.own_ref.refs_0_), channel_id=1, source_target_pairs={{0,8},{4,12},{8,0},{12,4},{16,24},{20,28},{24,16},{28,20},{1,9},{5... | collective-permute-start | bytes 12296 | tf_op jit(solution)/shard_map/ppermute | solution.py:271
  42.4 3.6 %collective-permute-start.10 = (f32[8,128]{1,0:T(8,128)S(1)}, f32[8,128]{1,0:T(8,128)S(1)}, u32[]{:S(2)}, u32[]{:S(2)}) collective-permute-start(f32[8,128]{1,0:T(8,128)S(1)} %add_add_fusion.own_ref.refs_0_), channel_id=1, source_target_pairs={{0,4},{4,0},{8,12},{12,8},{16,20},{20,16},{24,28},{28,24},{1,5},{5... | collective-permute-start | bytes 12296 | tf_op jit(solution)/shard_map/ppermute | solution.py:271

commit v3 on v2

--- a/solution.py
+++ b/solution.py
@@ -12,7 +12,7 @@
 LAG_MAX = 4
 LANES = 128
 SUBS = 8
-DIRECT = 16
+DIRECT = 0
 
 RATE_UNIT = 0.03
 STEP = 0.25
@@ -22,6 +22,7 @@
 BF16 = jnp.bfloat16
 VMEM = pl.BlockSpec(memory_space=pltpu.VMEM)
 SMEM = pl.BlockSpec(memory_space=pltpu.SMEM)
+HBM = pl.BlockSpec(memory_space=pltpu.HBM)
 BOTH_LANES = (((1,), (1,)), ((), ()))
 
 
@@ -40,6 +41,13 @@
         pieces.append(piece)
         x = x - piece.astype(F32)
     return pieces
+
+
+def fetch(sources, targets, sems):
+    copies = [pltpu.make_async_copy(a, b, sems.at[n]) for n, (a, b) in enumerate(zip(sources, targets))]
+    for copy in copies:
+        copy.start()
+    return copies
 
 
 def in_a_row(x):
@@ -64,12 +72,17 @@
         self.width = 512
 
 
-def pack_kernel(plan, me_ref, sets_ref, coef_ref, notional_ref, place_ref, *out_refs):
+def pack_kernel(plan, me_ref, sets_hbm, coef_hbm, notional_hbm, place_ref, *refs):
+    *out_refs, sets_ref, coef_ref, notional_ref, sems = refs
+    copies = fetch(
+        [sets_hbm, notional_hbm, coef_hbm], [sets_ref, notional_ref, coef_ref], sems
+    )
     me = me_ref[0]
     owners, part, room, extra = plan.owners, plan.part, plan.room, plan.extra
     lines = notional_ref.shape[0]
     rows = lines * LANES
     shared = SUBS // lines
+    copies[0].wait()
     block = sets_ref[pl.ds(pl.multiple_of(me // shared * SUBS, SUBS), SUBS), :]
     own = block[0:lines]
     for b in range(1, shared):
@@ -88,11 +101,13 @@
     )
     spot = key * room + rank.astype(jnp.int32)
     chosen = mask_bf16(iota((owners * room, rows), 0) == spot)
+    copies[1].wait()
     notional = in_a_row(notional_ref[...])
     high = notional.astype(BF16).astype(F32)
     info = jnp.concatenate(
         [high, notional - high, local.astype(F32), jnp.zeros((13, rows), F32)], axis=0
     )
+    copies[2].wait()
     table = jnp.concatenate([coef_ref[...], info.astype(BF16)], axis=0)
     moved = lax.dot_general(chosen, table, BOTH_LANES, preferred_element_type=F32)
     ids = LANES + extra
@@ -109,10 +124,15 @@
         message[room:, :] = jnp.concatenate(lanes, axis=1).astype(BF16)
 
 
-def basis_kernel(plan, shocks_ref, start_ref, loading_ref, out_ref, wide_ref):
+def basis_kernel(plan, shocks_hbm, start_hbm, loading_hbm, out_ref, *refs):
+    shocks_ref, start_ref, loading_ref, wide_ref, sems = refs
+    copies = fetch(
+        [loading_hbm, start_hbm, shocks_hbm], [loading_ref, start_ref, shocks_ref], sems
+    )
     tenors = loading_ref.shape[0]
     dates = plan.dates
-    wide_ref[...] = shocks_ref[...].astype(F32)
+    copies[0].wait()
+    copies[1].wait()
     loading_t = jnp.transpose(loading_ref[...])
     drift = 0.5 * STEP * jnp.sum(loading_t * loading_t, axis=1, keepdims=True)
     diag = iota((tenors, tenors), 0) == iota((tenors, tenors), 1)
@@ -123,6 +143,8 @@
     log_fwd = jnp.broadcast_to(log_start, (tenors, LANES))
     drift = jnp.broadcast_to(drift, (tenors, LANES))
     head = LANES - tenors
+    copies[2].wait()
+    wide_ref[...] = shocks_ref[...].astype(F32)
     step = plan.width // LANES
     for c in range(dates // step):
         shock = jnp.concatenate(
@@ -302,10 +324,15 @@
     place, *outgoing = pl.pallas_call(
         functools.partial(pack_kernel, plan),
         out_shape=[jax.ShapeDtypeStruct((SUBS, rows), F32)] + messages,
-        in_specs=[SMEM] + [VMEM] * 3,
+        in_specs=[SMEM] + [HBM] * 3,
         out_specs=[VMEM] * (1 + len(messages)),
+        scratch_shapes=[
+            pltpu.VMEM((owners * lines, LANES), jnp.int32),
+            pltpu.VMEM((2 * tenors, rows), BF16),
+            pltpu.VMEM((lines, LANES), F32),
+            pltpu.SemaphoreType.DMA((3,)),
+        ],
         name="pack",
-        compiler_params=pltpu.CompilerParams(vmem_limit_bytes=24 << 20),
     )(me, ns_of_trade.reshape(owners * lines, LANES), coefficient.T, notional)
     if plan.direct:
         incoming = [outgoing[0]] + [
@@ -317,11 +344,16 @@
     basis = pl.pallas_call(
         functools.partial(basis_kernel, plan),
         out_shape=jax.ShapeDtypeStruct((2 * LANES, cols), BF16),
-        in_specs=[VMEM] * 3,
+        in_specs=[HBM] * 3,
         out_specs=VMEM,
-        scratch_shapes=[pltpu.VMEM((tenors * dates, path_dev), F32)],
+        scratch_shapes=[
+            pltpu.VMEM((tenors * dates, path_dev), BF16),
+            pltpu.VMEM((1, tenors), F32),
+            pltpu.VMEM((tenors, tenors), F32),
+            pltpu.VMEM((tenors * dates, path_dev), F32),
+            pltpu.SemaphoreType.DMA((3,)),
+        ],
         name="basis",
-        compiler_params=pltpu.CompilerParams(vmem_limit_bytes=16 << 20),
         cost_estimate=pl.CostEstimate(
             flops=2 * 400 * tenors * cols, bytes_accessed=4 << 20, transcendentals=3 * tenors * cols
         ),
@@ -344,7 +376,8 @@
     if plan.direct:
         tiles = [tile] + [permuted(tile, "trade", owners, d) for d in range(1, owners)]
     else:
-        tiles = [lax.all_gather(tile, "trade", axis=0, tiled=False)]
+        spread = jnp.broadcast_to(tile, (owners,) + tile.shape)
+        tiles = [lax.all_to_all(spread, "trade", split_axis=0, concat_axis=0, tiled=True)]
     allocation, cva = pl.pallas_call(
         functools.partial(finish_kernel, plan),
         out_shape=[

time: 47.1 us -> 42.4 us (0.900)
  starting transfers between devices: 25.6 us -> 9.21 us
  blocking collectives: 0 us -> 10.6 us
  Pallas kernels: 10.1 us -> 14.3 us
  local copies, waits for them, and re-layouts: 4.87 us -> 1.62 us
    ppermute x17 -> x3, starting transfers between devices: 25.6 us -> 1.92 us  [permuted(): return lax.ppermute(x, axis, [(i, i ^ d) for i in range(size)])]
    all_to_all x0 -> x1, blocking collectives: none -> 10.6 us  [body(): lax.all_to_all(spread, 'trade', split_axis=0, concat_axis=0, tiled=True)]
    all_to_all x0 -> x1, starting transfers between devices: none -> 7.29 us  [body(): lax.all_to_all(outgoing[0], 'trade', split_axis=0, concat_axis=0, tiled=T...]
    all_to_all x0 -> x1, waiting for transfers between devices: none -> 3.81 us  [body(): lax.all_to_all(outgoing[0], 'trade', split_axis=0, concat_axis=0, tiled=T...]
    ppermute x17 -> x3, waiting for transfers between devices: 5.35 us -> 1.83 us  [permuted(): return lax.ppermute(x, axis, [(i, i ^ d) for i in range(size)])]
    unnamed x22 -> x14, local copies, waits for them, and re-layouts: 4.87 us -> 1.61 us
    pallas_call x1, Pallas kernels: 2.61 us -> 5.08 us  [body(): pl.pallas_call(functools.partial(basis_kernel, plan), out_shape=jax.Shape...]
    pallas_call x1, Pallas kernels: 0.58 us -> 2.3 us  [body(): pl.pallas_call(functools.partial(pack_kernel, plan), out_shape=[jax.Shape...]
  transfers between devices with their start and end apart: 17 -> 4, of which waited for: 6 -> 3; matrix products, arithmetic and copies ran while one was open for 0% -> 0% of each run, Pallas kernels for 6% -> 12%
where the time goes in v3:
time: 42.4 us; the launch traced here: 42.1 us
  Pallas kernels  14.3 us (34%)
  blocking collectives  10.6 us (25%)
  starting transfers between devices  9.21 us (22%)
  waiting for transfers between devices  5.64 us (13%)
  local copies, waits for them, and re-layouts  1.62 us (4%)
  between operations  0.75 us (2%)
    all_to_all x1, blocking collectives, body(): lax.all_to_all(spread, 'trade', split_axis=0, concat_axis=0, tiled=True)  10.6 us
    all_to_all x1, starting transfers between devices, body(): lax.all_to_all(outgoing[0], 'trade', split_axis=0, concat_axis=0, tiled=T...  7.29 us
    pallas_call x1, Pallas kernels, body(): pl.pallas_call(functools.partial(main_kernel, plan, path_total), out_shap...  6.14 us
    pallas_call x1, Pallas kernels, body(): pl.pallas_call(functools.partial(basis_kernel, plan), out_shape=jax.Shape...  5.08 us
    all_to_all x1, waiting for transfers between devices, body(): lax.all_to_all(outgoing[0], 'trade', split_axis=0, concat_axis=0, tiled=T...  3.81 us
    pallas_call x1, Pallas kernels, body(): pl.pallas_call(functools.partial(pack_kernel, plan), out_shape=[jax.Shape...  2.3 us
    ppermute x3, starting transfers between devices, permuted(): return lax.ppermute(x, axis, [(i, i ^ d) for i in range(size)])  1.92 us
    ppermute x3, waiting for transfers between devices, permuted(): return lax.ppermute(x, axis, [(i, i ^ d) for i in range(size)])  1.83 us
  transfers between devices with their start and end apart: 4, of which 3 were waited for; matrix products, arithmetic and copies ran while one was open for 0% of the time, Pallas kernels for 12%

profile of v3, /device:TPU:0, one launch (start us, length us, event | category | flops | bytes accessed | tf_op | source)
XLA Modules:
  0.0 42.1 jit_solution(10131155690952522699)
XLA Ops:
  0.6 0.0 copy-start.3
  0.6 0.0 copy-start.6
  0.7 0.0 copy-start.5
  0.7 0.0 copy-start.4
  0.7 2.3 %pack.1 = (f32[8,512]{1,0:T(8,128)}, bf16[8,128,128]{2,1,0:T(8,128)(2,1)}) custom-call(s32[1]{0:T(128)} %bitcast.me_ref, s32[32,128]{1,0:T(8,128)} %bitcast.12, bf16[160,512]{1,0:T(8,128)(2,1)} %bitcast.11, f32[4,128]{1,0:T(4,128)} %bitcast.8), custom_call_target="tpu_custom_call" | custom-call | tf_op jit(solution)/shard_map/pack/pallas_call | solution.py:324
  3.0 7.3 %all-to-all-start = ((bf16[8,128,128]{2,1,0:T(8,128)(2,1)}), bf16[8,128,128]{2,1,0:T(8,128)(2,1)S(1)}, u32[]{:S(2)}, u32[]{:S(2)}) async-start(bf16[8,128,128]{2,1,0:T(8,128)(2,1)} %get-tuple-element.7), calls=%async_computation | async-start | bytes 524288 | tf_op jit(solution)/shard_map/all_to_all | solution.py:342
  10.3 0.0 copy-start.1
  10.3 0.0 copy-start.2
  10.3 5.1 %basis.1.basis_ref = bf16[256,4096]{1,0:T(8,128)(2,1)} custom-call(bf16[2560,128]{1,0:T(8,128)(2,1)} %bitcast.10, f32[1,80]{1,0:T(1,128)} %bitcast.13, f32[80,80]{1,0:T(8,128)} %loading_hbm.1), custom_call_target="tpu_custom_call" | custom-call | flops 262144000 | bytes 4194304 | tf_op jit(solution)/shard_map/basis/pallas_call | solution.py:344
  15.4 3.8 %all-to-all-done.refs_0_ = bf16[8,128,128]{2,1,0:T(8,128)(2,1)S(1)} async-done(((bf16[8,128,128]{2,1,0:T(8,128)(2,1)}), bf16[8,128,128]{2,1,0:T(8,128)(2,1)S(1)}, u32[]{:S(2)}, u32[]{:S(2)}) %all-to-all-start) | async-done | bytes 262176 | tf_op jit(solution)/shard_map/all_to_all | solution.py:342
  19.2 0.0 copy-done.3
  19.2 0.0 copy-done.6
  19.2 0.0 copy-done.5
  19.2 0.0 copy-done.4
  19.2 0.0 copy-start
  19.2 1.6 %copy-done = bf16[256,4096]{1,0:T(8,128)(2,1)S(1)} copy-done((bf16[256,4096]{1,0:T(8,128)(2,1)S(1)}, bf16[256,4096]{1,0:T(8,128)(2,1)}, u32[]{:S(2)}) %copy-start) | copy-done | bytes 2097176
  20.8 6.1 %value_and_allocate.1 = f32[8,128]{1,0:T(8,128)S(1)} custom-call(s32[1]{0:T(128)} %bitcast.me_ref, s32[8]{0:T(128)S(1)} %copy-done.4, s32[4]{0:T(128)S(1)} %copy-done.5, s32[4]{0:T(128)S(1)} %copy-done.6, f32[4,32]{1,0:T(4,128)S(1)} %copy-done.3, bf16[256,4096]{1,0:T(8,128)(2,1)S(1)} %copy-done, bf16[8,128,128]{2,1,0:T(8,128)(2,1)S(1)} %all-to-all-done.refs_0_), custom_call_target="tpu_custom_call" | custom-call | tf_op jit(solution)/shard_map/value_and_allocate/pallas_call | solution.py:363
  27.0 0.1 collective-permute-start.2
  27.0 1.6 %collective-permute-start.1 = (f32[8,128]{1,0:T(8,128)S(1)}, f32[8,128]{1,0:T(8,128)S(1)}, u32[]{:S(2)}, u32[]{:S(2)}) collective-permute-start(f32[8,128]{1,0:T(8,128)S(1)} %value_and_allocate.1), channel_id=1, source_target_pairs={{0,2},{1,3},{2,0},{3,1},{4,6},{5,7},{6,4},{7,5},{8,10},{9,11},{10,... | collective-permute-start | bytes 12296 | tf_op jit(solution)/shard_map/ppermute | solution.py:293
  28.6 0.3 collective-permute-start
  28.9 1.2 %collective-permute-done.2 = f32[8,128]{1,0:T(8,128)S(1)} collective-permute-done((f32[8,128]{1,0:T(8,128)S(1)}, f32[8,128]{1,0:T(8,128)S(1)}, u32[]{:S(2)}, u32[]{:S(2)}) %collective-permute-start.2) | collective-permute-done | bytes 4128 | tf_op jit(solution)/shard_map/ppermute | solution.py:293
  30.1 0.7 %collective-permute-done.1 = f32[8,128]{1,0:T(8,128)S(1)} collective-permute-done((f32[8,128]{1,0:T(8,128)S(1)}, f32[8,128]{1,0:T(8,128)S(1)}, u32[]{:S(2)}, u32[]{:S(2)}) %collective-permute-start.1) | collective-permute-done | bytes 4128 | tf_op jit(solution)/shard_map/ppermute | solution.py:293
  30.7 0.0 collective-permute-done
  30.7 10.6 %all_to_all.10.refs_0_ = f32[8,8,128]{2,1,0:T(8,128)S(1)} all-to-all(f32[8,8,128]{2,1,0:T(8,128)S(1)} %broadcast_in_dim.3), channel_id=1, replica_groups=mesh['trade'=8,'path'=4] {'trade'}, dimensions={0} | all-to-all | bytes 65536 | tf_op jit(solution)/shard_map/all_to_all | solution.py:380
  41.3 0.0 copy-done.1
  41.3 0.0 copy-done.2
  41.3 0.8 %finish.1 = (f32[1,512]{1,0:T(1,128)}, f32[1,4]{1,0:T(1,128)}) custom-call(s32[1]{0:T(128)} %bitcast.me_ref, f32[8,512]{1,0:T(8,128)S(1)} %copy-done.1, f32[4,128]{1,0:T(4,128)S(1)} %bitcast.9, f32[8,128]{1,0:T(8,128)S(1)} %add_add_fusion.own_ref, f32[8,8,128]{2,1,0:T(8,128)S(1)} %all_to_all.10.refs_0_), custom_call_target="tpu_custom_call" | custom-call | tf_op jit(solution)/shard_map/finish/pallas_call | solution.py:381
  (2 shorter events, 0.0 us)
Async XLA Ops:
  0.6 18.6 %copy-start.3 = (f32[4,32]{1,0:T(4,128)S(1)}, f32[4,32]{1,0:T(4,128)}, u32[]{:S(2)}) copy-start(f32[4,32]{1,0:T(4,128)} %weight_ref.1) | copy-start | bytes 1540
  0.6 18.6 %copy-start.6 = (s32[4]{0:T(128)S(1)}, s32[4]{0:T(128)}, u32[]{:S(2)}) copy-start(s32[4]{0:T(128)} %lag_ref.1) | copy-start | bytes 52
  0.7 18.6 %copy-start.5 = (s32[4]{0:T(128)S(1)}, s32[4]{0:T(128)}, u32[]{:S(2)}) copy-start(s32[4]{0:T(128)} %cpty_ref.1) | copy-start | bytes 52
  0.7 18.5 %copy-start.4 = (s32[8]{0:T(128)S(1)}, s32[8]{0:T(128)}, u32[]{:S(2)}) copy-start(s32[8]{0:T(128)} %agr_ref.1) | copy-start | bytes 100
  3.0 16.2 %all-to-all-start = ((bf16[8,128,128]{2,1,0:T(8,128)(2,1)}), bf16[8,128,128]{2,1,0:T(8,128)(2,1)S(1)}, u32[]{:S(2)}, u32[]{:S(2)}) async-start(bf16[8,128,128]{2,1,0:T(8,128)(2,1)} %get-tuple-element.7), calls=%async_computation | async-start | bytes 524288 | tf_op jit(solution)/shard_map/all_to_all | solution.py:342
  10.3 31.0 %copy-start.1 = (f32[8,512]{1,0:T(8,128)S(1)}, f32[8,512]{1,0:T(8,128)}, u32[]{:S(2)}) copy-start(f32[8,512]{1,0:T(8,128)} %get-tuple-element.6.place_ref) | copy-start | bytes 49156
  10.3 31.0 %copy-start.2 = (f32[512]{0:T(512)S(1)}, f32[512]{0:T(512)}, u32[]{:S(2)}) copy-start(f32[512]{0:T(512)} %param.14) | copy-start | bytes 6148
  19.2 1.6 %copy-start = (bf16[256,4096]{1,0:T(8,128)(2,1)S(1)}, bf16[256,4096]{1,0:T(8,128)(2,1)}, u32[]{:S(2)}) copy-start(bf16[256,4096]{1,0:T(8,128)(2,1)} %basis.1.basis_ref) | copy-start | bytes 6291460
  27.0 3.1 %collective-permute-start.2 = (f32[8,128]{1,0:T(8,128)S(1)}, f32[8,128]{1,0:T(8,128)S(1)}, u32[]{:S(2)}, u32[]{:S(2)}) collective-permute-start(f32[8,128]{1,0:T(8,128)S(1)} %value_and_allocate.1), channel_id=1, source_target_pairs={{0,3},{1,2},{2,1},{3,0},{4,7},{5,6},{6,5},{7,4},{8,11},{9,10},{10,... | collective-permute-start | bytes 12296 | tf_op jit(solution)/shard_map/ppermute | solution.py:293
  27.0 3.7 %collective-permute-start.1 = (f32[8,128]{1,0:T(8,128)S(1)}, f32[8,128]{1,0:T(8,128)S(1)}, u32[]{:S(2)}, u32[]{:S(2)}) collective-permute-start(f32[8,128]{1,0:T(8,128)S(1)} %value_and_allocate.1), channel_id=1, source_target_pairs={{0,2},{1,3},{2,0},{3,1},{4,6},{5,7},{6,4},{7,5},{8,10},{9,11},{10,... | collective-permute-start | bytes 12296 | tf_op jit(solution)/shard_map/ppermute | solution.py:293
  28.6 2.1 %collective-permute-start = (f32[8,128]{1,0:T(8,128)S(1)}, f32[8,128]{1,0:T(8,128)S(1)}, u32[]{:S(2)}, u32[]{:S(2)}) collective-permute-start(f32[8,128]{1,0:T(8,128)S(1)} %value_and_allocate.1), channel_id=1, source_target_pairs={{0,1},{1,0},{2,3},{3,2},{4,5},{5,4},{6,7},{7,6},{8,9},{9,8},{10,11... | collective-permute-start | bytes 12296 | tf_op jit(solution)/shard_map/ppermute | solution.py:293

commit v4 on v3

--- a/solution.py
+++ b/solution.py
@@ -12,7 +12,7 @@
 LAG_MAX = 4
 LANES = 128
 SUBS = 8
-DIRECT = 0
+DIRECT = 8
 
 RATE_UNIT = 0.03
 STEP = 0.25
@@ -72,8 +72,21 @@
         self.width = 512
 
 
-def pack_kernel(plan, me_ref, sets_hbm, coef_hbm, notional_hbm, place_ref, *refs):
-    *out_refs, sets_ref, coef_ref, notional_ref, sems = refs
+def pack_kernel(
+    plan,
+    me_ref,
+    sets_hbm,
+    coef_hbm,
+    notional_hbm,
+    place_ref,
+    out_hbm,
+    out_ref,
+    sets_ref,
+    coef_ref,
+    notional_ref,
+    sems,
+    out_sems,
+):
     copies = fetch(
         [sets_hbm, notional_hbm, coef_hbm], [sets_ref, notional_ref, coef_ref], sems
     )
@@ -90,8 +103,6 @@
     sets = in_a_row(own)
     key = lax.shift_right_logical(sets, 3)
     local = sets - key * NS_DEV
-    if plan.direct:
-        key = lax.bitwise_xor(key, me)
     hot = iota((owners, rows), 0) == key
     before = mask_bf16(iota((rows, rows), 0) < iota((rows, rows), 1))
     count = jnp.dot(mask_bf16(hot), before, preferred_element_type=F32)
@@ -112,7 +123,7 @@
     moved = lax.dot_general(chosen, table, BOTH_LANES, preferred_element_type=F32)
     ids = LANES + extra
     for d in range(owners):
-        message = out_refs[d] if plan.direct else out_refs[0].at[d]
+        message = out_ref.at[d]
         block = moved[d * room : (d + 1) * room]
         message[0:room, :] = block[:, 0:LANES].astype(BF16)
         split = [block[part * g : part * (g + 1)] for g in range(plan.groups)]
@@ -122,10 +133,13 @@
         lanes += [x[:, ids : ids + SUBS] for x in split]
         lanes.append(jnp.zeros((part, SUBS * (4 - plan.groups)), F32))
         message[room:, :] = jnp.concatenate(lanes, axis=1).astype(BF16)
-
-
-def basis_kernel(plan, shocks_hbm, start_hbm, loading_hbm, out_ref, *refs):
-    shocks_ref, start_ref, loading_ref, wide_ref, sems = refs
+        pltpu.make_async_copy(message, out_hbm.at[d], out_sems.at[d]).start()
+    for d in range(owners):
+        pltpu.make_async_copy(out_ref.at[d], out_hbm.at[d], out_sems.at[d]).wait()
+
+
+def basis_kernel(plan, shocks_hbm, start_hbm, loading_hbm, out_hbm, *refs):
+    out_ref, shocks_ref, start_ref, loading_ref, wide_ref, sems, out_sems = refs
     copies = fetch(
         [loading_hbm, start_hbm, shocks_hbm], [loading_ref, start_ref, shocks_ref], sems
     )
@@ -165,26 +179,43 @@
         growth = split_bf16(jnp.log(1.0 + STEP * fwd), 2)
         summed = jnp.dot(lower, jnp.concatenate(growth, axis=0), preferred_element_type=F32)
         bond = jnp.exp(-summed)
-        cols = slice(c * plan.width, (c + 1) * plan.width)
-        out_ref[0:tenors, cols] = (bond * fwd * (1.0 / RATE_UNIT)).astype(BF16)
+        out_ref[c, 0:tenors] = (bond * fwd * (1.0 / RATE_UNIT)).astype(BF16)
         bond = bond.astype(BF16)
-        out_ref[tenors:LANES, cols] = bond[0:head]
+        out_ref[c, tenors:LANES] = bond[0:head]
         for g in range(plan.groups):
-            out_ref[LANES + plan.extra * g : LANES + plan.extra * (g + 1), cols] = bond[head:]
+            out_ref[c, LANES + plan.extra * g : LANES + plan.extra * (g + 1)] = bond[head:]
         used = LANES + plan.extra * plan.groups
-        out_ref[used:, cols] = jnp.zeros((2 * LANES - used, plan.width), BF16)
-
-
-def main_kernel(plan, path_total, me_ref, agr_ref, cpty_ref, lag_ref, weight_ref, basis_ref, *refs):
-    *in_refs, out_ref, val_ref = refs
+        out_ref[c, used:] = jnp.zeros((2 * LANES - used, plan.width), BF16)
+        pltpu.make_async_copy(out_ref.at[c], out_hbm.at[c], out_sems.at[c]).start()
+    for c in range(dates // step):
+        pltpu.make_async_copy(out_ref.at[c], out_hbm.at[c], out_sems.at[c]).wait()
+
+
+def main_kernel(
+    plan,
+    path_total,
+    me_ref,
+    agr_ref,
+    cpty_ref,
+    lag_ref,
+    weight_ref,
+    in_ref,
+    basis_hbm,
+    out_ref,
+    val_ref,
+    basis_ref,
+    sems,
+):
+    chunks = basis_hbm.shape[0]
+    copies = fetch(
+        [basis_hbm.at[c] for c in range(chunks)], [basis_ref.at[c] for c in range(chunks)], sems
+    )
     me = me_ref[0]
     part, room, dates = plan.part, plan.room, plan.dates
     cpty_dev = weight_ref.shape[0]
 
     def rows_of(first):
-        if plan.direct:
-            return jnp.concatenate([ref[first : first + part, :] for ref in in_refs], axis=0)
-        return in_refs[0][:, first : first + part, :].reshape(plan.owners * part, LANES)
+        return in_ref[:, first : first + part, :].reshape(plan.owners * part, LANES)
 
     rest = rows_of(room)
     lane = iota((1, LANES), 1)
@@ -206,11 +237,9 @@
 
     owed = []
     width = plan.width
-    chunks = dates * LANES // width
     for c in range(chunks):
-        under = jnp.dot(
-            left, basis_ref[:, c * width : (c + 1) * width], preferred_element_type=F32
-        )
+        copies[c].wait()
+        under = jnp.dot(left, basis_ref[c], preferred_element_type=F32)
         value = jnp.maximum(under, 0.0).astype(BF16)
         val_ref[c] = value
         both = jnp.dot(netting, value, preferred_element_type=F32)
@@ -271,10 +300,10 @@
     key = place_ref[0:1, :].astype(jnp.int32)
     rank = place_ref[1:2, :].astype(jnp.int32)
     group = lax.div(rank, part)
-    slot = key if plan.direct else jnp.full_like(key, me)
-    line = group * plan.lines + lax.div(slot, per_line)
-    lane = lax.rem(slot, per_line) * part + (rank - group * part)
+    line = group * plan.lines + me // per_line
+    lane = lax.rem(me, per_line) * part + (rank - group * part)
     if plan.direct:
+        key = lax.bitwise_xor(key, me)
         tiles = jnp.concatenate([ref[...] for ref in in_refs], axis=0)
     else:
         tiles = in_refs[0][...].reshape(plan.owners * plan.tile, LANES)
@@ -313,45 +342,43 @@
     lines = rows // LANES
     plan = Plan(owners, rows, tenors, dates)
     cols = dates * path_dev
+    chunks = cols // plan.width
     me = lax.axis_index("trade").astype(jnp.int32).reshape(1)
     notional = notional.reshape(lines, LANES)
 
-    message = jax.ShapeDtypeStruct((plan.height, LANES), BF16)
-    if plan.direct:
-        messages = [message] * owners
-    else:
-        messages = [jax.ShapeDtypeStruct((owners,) + message.shape, BF16)]
-    place, *outgoing = pl.pallas_call(
+    place, outgoing = pl.pallas_call(
         functools.partial(pack_kernel, plan),
-        out_shape=[jax.ShapeDtypeStruct((SUBS, rows), F32)] + messages,
+        out_shape=[
+            jax.ShapeDtypeStruct((SUBS, rows), F32),
+            jax.ShapeDtypeStruct((owners, plan.height, LANES), BF16),
+        ],
         in_specs=[SMEM] + [HBM] * 3,
-        out_specs=[VMEM] * (1 + len(messages)),
+        out_specs=[VMEM, HBM],
         scratch_shapes=[
+            pltpu.VMEM((owners, plan.height, LANES), BF16),
             pltpu.VMEM((owners * lines, LANES), jnp.int32),
             pltpu.VMEM((2 * tenors, rows), BF16),
             pltpu.VMEM((lines, LANES), F32),
             pltpu.SemaphoreType.DMA((3,)),
+            pltpu.SemaphoreType.DMA((owners,)),
         ],
         name="pack",
     )(me, ns_of_trade.reshape(owners * lines, LANES), coefficient.T, notional)
-    if plan.direct:
-        incoming = [outgoing[0]] + [
-            permuted(outgoing[d], "trade", owners, d) for d in range(1, owners)
-        ]
-    else:
-        incoming = [lax.all_to_all(outgoing[0], "trade", split_axis=0, concat_axis=0, tiled=True)]
+    incoming = lax.all_to_all(outgoing, "trade", split_axis=0, concat_axis=0, tiled=True)
 
     basis = pl.pallas_call(
         functools.partial(basis_kernel, plan),
-        out_shape=jax.ShapeDtypeStruct((2 * LANES, cols), BF16),
+        out_shape=jax.ShapeDtypeStruct((chunks, 2 * LANES, plan.width), BF16),
         in_specs=[HBM] * 3,
-        out_specs=VMEM,
+        out_specs=HBM,
         scratch_shapes=[
+            pltpu.VMEM((chunks, 2 * LANES, plan.width), BF16),
             pltpu.VMEM((tenors * dates, path_dev), BF16),
             pltpu.VMEM((1, tenors), F32),
             pltpu.VMEM((tenors, tenors), F32),
             pltpu.VMEM((tenors * dates, path_dev), F32),
             pltpu.SemaphoreType.DMA((3,)),
+            pltpu.SemaphoreType.DMA((chunks,)),
         ],
         name="basis",
         cost_estimate=pl.CostEstimate(
@@ -359,22 +386,26 @@
         ),
     )(shocks.reshape(tenors * dates, path_dev), forward_start.reshape(1, tenors), loading)
 
-    need = 2 * plan.trades * cols + 16 * plan.trades * plan.width + (8 << 20)
     tile = pl.pallas_call(
         functools.partial(main_kernel, plan, path_total),
         out_shape=jax.ShapeDtypeStruct((plan.tile, LANES), F32),
-        in_specs=[SMEM] * 4 + [VMEM] * (2 + len(incoming)),
+        in_specs=[SMEM] * 4 + [VMEM] * 2 + [HBM],
         out_specs=VMEM,
-        scratch_shapes=[pltpu.VMEM((cols // plan.width, plan.trades, plan.width), BF16)],
+        scratch_shapes=[
+            pltpu.VMEM((chunks, plan.trades, plan.width), BF16),
+            pltpu.VMEM((chunks, 2 * LANES, plan.width), BF16),
+            pltpu.SemaphoreType.DMA((chunks,)),
+        ],
         name="value_and_allocate",
-        compiler_params=pltpu.CompilerParams(vmem_limit_bytes=need),
-    )(me, agr_of_ns, cpty_of_agr, margin_lag, default_weight, basis, *incoming)
+        compiler_params=pltpu.CompilerParams(vmem_limit_bytes=60 << 20),
+    )(me, agr_of_ns, cpty_of_agr, margin_lag, default_weight, incoming, basis)
 
     others = [permuted(tile, "path", path_parts, d) for d in range(1, path_parts)]
     for other in others:
         tile = tile + other
     if plan.direct:
-        tiles = [tile] + [permuted(tile, "trade", owners, d) for d in range(1, owners)]
+        pair = jnp.concatenate([tile, permuted(tile, "trade", owners, 1)], axis=0)
+        tiles = [pair] + [permuted(pair, "trade", owners, d) for d in range(2, owners, 2)]
     else:
         spread = jnp.broadcast_to(tile, (owners,) + tile.shape)
         tiles = [lax.all_to_all(spread, "trade", split_axis=0, concat_axis=0, tiled=True)]

time: 42.4 us -> 45.3 us (1.068)
  blocking collectives: 10.6 us -> 0 us
  starting transfers between devices: 9.21 us -> 15 us
  waiting for transfers between devices: 5.64 us -> 10.4 us
  Pallas kernels: 14.3 us -> 17.5 us
  local copies, waits for them, and re-layouts: 1.62 us -> 0.7 us
  other arithmetic: 0.01 us -> 0.69 us
    all_to_all x1 -> x0, blocking collectives: 10.6 us -> none  [body(): lax.all_to_all(spread, 'trade', split_axis=0, concat_axis=0, tiled=True)]
    ppermute x3 -> x7, starting transfers between devices: 1.92 us -> 7.75 us  [permuted(): return lax.ppermute(x, axis, [(i, i ^ d) for i in range(size)])]
    ppermute x3 -> x7, waiting for transfers between devices: 1.83 us -> 6.02 us  [permuted(): return lax.ppermute(x, axis, [(i, i ^ d) for i in range(size)])]
    pallas_call x1, Pallas kernels: 6.14 us -> 9.15 us  [body(): pl.pallas_call(functools.partial(main_kernel, plan, path_total), out_shap...]
    unnamed x14 -> x6, local copies, waits for them, and re-layouts: 1.61 us -> 0.7 us
    add x1, other arithmetic: 0.01 us -> 0.69 us  [body(): tile = tile + other]
    pallas_call x1, Pallas kernels: 2.3 us -> 2.96 us  [body(): pl.pallas_call(functools.partial(pack_kernel, plan), out_shape=[jax.Shape...]
    pallas_call x1, Pallas kernels: 5.08 us -> 4.54 us  [body(): pl.pallas_call(functools.partial(basis_kernel, plan), out_shape=jax.Shape...]
  transfers between devices with their start and end apart: 4 -> 8, of which waited for: 3 -> 7; matrix products, arithmetic and copies ran while one was open for 0% -> 0% of each run, Pallas kernels for 12% -> 10%
where the time goes in v4:
time: 45.3 us; the launch traced here: 44.9 us
  Pallas kernels  17.5 us (39%)
  starting transfers between devices  15 us (33%)
  waiting for transfers between devices  10.4 us (23%)
  local copies, waits for them, and re-layouts  0.7 us (2%)
  other arithmetic  0.69 us (2%)
  between operations  0.69 us (2%)
    pallas_call x1, Pallas kernels, body(): pl.pallas_call(functools.partial(main_kernel, plan, path_total), out_shap...  9.15 us
    ppermute x7, starting transfers between devices, permuted(): return lax.ppermute(x, axis, [(i, i ^ d) for i in range(size)])  7.75 us
    all_to_all x1, starting transfers between devices, body(): lax.all_to_all(outgoing, 'trade', split_axis=0, concat_axis=0, tiled=True)  7.29 us
    ppermute x7, waiting for transfers between devices, permuted(): return lax.ppermute(x, axis, [(i, i ^ d) for i in range(size)])  6.02 us
    pallas_call x1, Pallas kernels, body(): pl.pallas_call(functools.partial(basis_kernel, plan), out_shape=jax.Shape...  4.54 us
    all_to_all x1, waiting for transfers between devices, body(): lax.all_to_all(outgoing, 'trade', split_axis=0, concat_axis=0, tiled=True)  4.35 us
    pallas_call x1, Pallas kernels, body(): pl.pallas_call(functools.partial(pack_kernel, plan), out_shape=[jax.Shape...  2.96 us
  transfers between devices with their start and end apart: 8, of which 7 were waited for; matrix products, arithmetic and copies ran while one was open for 0% of the time, Pallas kernels for 10%

profile of v4, /device:TPU:0, one launch (start us, length us, event | category | flops | bytes accessed | tf_op | source)
XLA Modules:
  0.0 44.9 jit_solution(489188784410575290)
XLA Ops:
  0.6 3.0 %pack.1 = (f32[8,512]{1,0:T(8,128)}, bf16[8,128,128]{2,1,0:T(8,128)(2,1)}) custom-call(s32[1]{0:T(128)} %bitcast.me_ref, s32[32,128]{1,0:T(8,128)} %bitcast.12, bf16[160,512]{1,0:T(8,128)(2,1)} %bitcast.11, f32[4,128]{1,0:T(4,128)} %bitcast.8), custom_call_target="tpu_custom_call" | custom-call | tf_op jit(solution)/shard_map/pack/pallas_call | solution.py:349
  3.6 7.3 %all-to-all-start = ((bf16[8,128,128]{2,1,0:T(8,128)(2,1)}), bf16[8,128,128]{2,1,0:T(8,128)(2,1)S(1)}, u32[]{:S(2)}, u32[]{:S(2)}) async-start(bf16[8,128,128]{2,1,0:T(8,128)(2,1)} %get-tuple-element.7), calls=%async_computation | async-start | bytes 524288 | tf_op jit(solution)/shard_map/all_to_all | solution.py:367
  10.9 0.0 copy-start
  10.9 0.0 copy-start.1
  10.9 4.5 %basis.1.basis_hbm = bf16[8,256,512]{2,1,0:T(8,128)(2,1)} custom-call(bf16[2560,128]{1,0:T(8,128)(2,1)} %bitcast.10, f32[1,80]{1,0:T(1,128)} %bitcast.13, f32[80,80]{1,0:T(8,128)} %loading_hbm.1), custom_call_target="tpu_custom_call" | custom-call | flops 262144000 | bytes 4194304 | tf_op jit(solution)/shard_map/basis/pallas_call | solution.py:369
  15.5 4.4 %all-to-all-done.in_ref = bf16[8,128,128]{2,1,0:T(8,128)(2,1)S(1)} async-done(((bf16[8,128,128]{2,1,0:T(8,128)(2,1)}), bf16[8,128,128]{2,1,0:T(8,128)(2,1)S(1)}, u32[]{:S(2)}, u32[]{:S(2)}) %all-to-all-start) | async-done | bytes 262176 | tf_op jit(solution)/shard_map/all_to_all | solution.py:367
  19.8 0.0 copy-start.2
  19.8 0.7 %copy-done.2 = bf16[8,128,128]{2,1,0:T(8,128)(2,1)} copy-done((bf16[8,128,128]{2,1,0:T(8,128)(2,1)}, bf16[8,128,128]{2,1,0:T(8,128)(2,1)S(1)}, u32[]{:S(2)}) %copy-start.2) | copy-done | bytes 262168
  20.5 9.2 %value_and_allocate.1 = f32[8,128]{1,0:T(8,128)} custom-call(s32[1]{0:T(128)} %bitcast.me_ref, s32[8]{0:T(128)} %agr_ref.1, s32[4]{0:T(128)} %cpty_ref.1, s32[4]{0:T(128)} %lag_ref.1, f32[4,32]{1,0:T(4,128)} %weight_ref.1, bf16[8,128,128]{2,1,0:T(8,128)(2,1)} %copy-done.2, bf16[8,256,512]{2,1,0:T(8,128)(2,1)} %basis.1.basis_hbm), custom_call_target="tpu_custom_call" | custom-call | tf_op jit(solution)/shard_map/value_and_allocate/pallas_call | solution.py:389
  29.7 0.1 collective-permute-start.2
  29.7 1.6 %collective-permute-start.1 = (f32[8,128]{1,0:T(8,128)}, f32[8,128]{1,0:T(8,128)S(1)}, u32[]{:S(2)}, u32[]{:S(2)}) collective-permute-start(f32[8,128]{1,0:T(8,128)} %value_and_allocate.1), channel_id=1, source_target_pairs={{0,2},{1,3},{2,0},{3,1},{4,6},{5,7},{6,4},{7,5},{8,10},{9,11},{10,... | collective-permute-start | bytes 12296 | tf_op jit(solution)/shard_map/ppermute | solution.py:322
  31.3 0.3 collective-permute-start
  31.6 1.4 %collective-permute-done.2 = f32[8,128]{1,0:T(8,128)S(1)} collective-permute-done((f32[8,128]{1,0:T(8,128)}, f32[8,128]{1,0:T(8,128)S(1)}, u32[]{:S(2)}, u32[]{:S(2)}) %collective-permute-start.2) | collective-permute-done | bytes 4128 | tf_op jit(solution)/shard_map/ppermute | solution.py:322
  33.0 0.7 %collective-permute-done.1 = f32[8,128]{1,0:T(8,128)S(1)} collective-permute-done((f32[8,128]{1,0:T(8,128)}, f32[8,128]{1,0:T(8,128)S(1)}, u32[]{:S(2)}, u32[]{:S(2)}) %collective-permute-start.1) | collective-permute-done | bytes 4128 | tf_op jit(solution)/shard_map/ppermute | solution.py:322
  33.6 0.0 collective-permute-done
  33.6 0.7 %add_add_fusion.own_ref = f32[8,128]{1,0:T(8,128)S(1)} fusion(f32[8,128]{1,0:T(8,128)S(1)} %collective-permute-done.2, f32[8,128]{1,0:T(8,128)S(1)} %collective-permute-done.1, f32[8,128]{1,0:T(8,128)} %value_and_allocate.1, f32[8,128]{1,0:T(8,128)S(1)} %collective-permute-done), kind=kLoop, calls=%fused_computation.1 | loop fusion | flops 3072 | bytes 20480 | tf_op jit(solution)/shard_map/add | solution.py:405
  34.3 1.4 %collective-permute-start.3 = (f32[8,128]{1,0:T(8,128)S(1)}, f32[8,128]{1,0:T(8,128)S(1)}, u32[]{:S(2)}, u32[]{:S(2)}) collective-permute-start(f32[8,128]{1,0:T(8,128)S(1)} %add_add_fusion.own_ref), channel_id=1, source_target_pairs={{0,4},{4,0},{8,12},{12,8},{16,20},{20,16},{24,28},{28,24},{1,5},{5... | collective-permute-start | bytes 12296 | tf_op jit(solution)/shard_map/ppermute | solution.py:322
  35.8 2.2 %collective-permute-done.3 = f32[8,128]{1,0:T(8,128)S(1)} collective-permute-done((f32[8,128]{1,0:T(8,128)S(1)}, f32[8,128]{1,0:T(8,128)S(1)}, u32[]{:S(2)}, u32[]{:S(2)}) %collective-permute-start.3) | collective-permute-done | bytes 4128 | tf_op jit(solution)/shard_map/ppermute | solution.py:322
  38.0 1.4 %collective-permute-start.6 = (f32[16,128]{1,0:T(8,128)S(1)}, f32[16,128]{1,0:T(8,128)S(1)}, u32[]{:S(2)}, u32[]{:S(2)}) collective-permute-start(f32[16,128]{1,0:T(8,128)S(1)} %pad_maximum_fusion.refs_0_), channel_id=1, source_target_pairs={{0,24},{4,28},{8,16},{12,20},{16,8},{20,12},{24,0},{28,4},{1,25},{... | collective-permute-start | bytes 24584 | tf_op jit(solution)/shard_map/ppermute | solution.py:322
  39.4 1.1 %collective-permute-start.5 = (f32[16,128]{1,0:T(8,128)S(1)}, f32[16,128]{1,0:T(8,128)S(1)}, u32[]{:S(2)}, u32[]{:S(2)}) collective-permute-start(f32[16,128]{1,0:T(8,128)S(1)} %pad_maximum_fusion.refs_0_), channel_id=1, source_target_pairs={{0,16},{4,20},{8,24},{12,28},{16,0},{20,4},{24,8},{28,12},{1,17},{... | collective-permute-start | bytes 24584 | tf_op jit(solution)/shard_map/ppermute | solution.py:322
  40.5 1.9 %collective-permute-start.4 = (f32[16,128]{1,0:T(8,128)S(1)}, f32[16,128]{1,0:T(8,128)S(1)}, u32[]{:S(2)}, u32[]{:S(2)}) collective-permute-start(f32[16,128]{1,0:T(8,128)S(1)} %pad_maximum_fusion.refs_0_), channel_id=1, source_target_pairs={{0,8},{4,12},{8,0},{12,4},{16,24},{20,28},{24,16},{28,20},{1,9},{5... | collective-permute-start | bytes 24584 | tf_op jit(solution)/shard_map/ppermute | solution.py:322
  42.3 1.1 %collective-permute-done.6.refs_3_ = f32[16,128]{1,0:T(8,128)S(1)} collective-permute-done((f32[16,128]{1,0:T(8,128)S(1)}, f32[16,128]{1,0:T(8,128)S(1)}, u32[]{:S(2)}, u32[]{:S(2)}) %collective-permute-start.6) | collective-permute-done | bytes 8224 | tf_op jit(solution)/shard_map/ppermute | solution.py:322
  43.4 0.5 %collective-permute-done.5.refs_2_ = f32[16,128]{1,0:T(8,128)S(1)} collective-permute-done((f32[16,128]{1,0:T(8,128)S(1)}, f32[16,128]{1,0:T(8,128)S(1)}, u32[]{:S(2)}, u32[]{:S(2)}) %collective-permute-start.5) | collective-permute-done | bytes 8224 | tf_op jit(solution)/shard_map/ppermute | solution.py:322
  43.9 0.2 collective-permute-done.4.refs_1_
  44.1 0.0 copy-done
  44.1 0.0 copy-done.1
  44.1 0.8 %finish.1 = (f32[1,512]{1,0:T(1,128)}, f32[1,4]{1,0:T(1,128)}) custom-call(s32[1]{0:T(128)} %bitcast.me_ref, f32[8,512]{1,0:T(8,128)S(1)} %copy-done, f32[4,128]{1,0:T(4,128)S(1)} %bitcast.9, f32[8,128]{1,0:T(8,128)S(1)} %add_add_fusion.own_ref, f32[16,128]{1,0:T(8,128)S(1)} %pad_maximum_fusion.refs_0_, f32[16,128]{1,0:T(8,128)S(1)} %collective-permute-done.4.refs_1_, ...), custom_call_target="tpu_custom_call" | custom-call | tf_op jit(solution)/shard_map/finish/pallas_call | solution.py:412
  (1 shorter events, 0.0 us)
Async XLA Ops:
  3.6 16.2 %all-to-all-start = ((bf16[8,128,128]{2,1,0:T(8,128)(2,1)}), bf16[8,128,128]{2,1,0:T(8,128)(2,1)S(1)}, u32[]{:S(2)}, u32[]{:S(2)}) async-start(bf16[8,128,128]{2,1,0:T(8,128)(2,1)} %get-tuple-element.7), calls=%async_computation | async-start | bytes 524288 | tf_op jit(solution)/shard_map/all_to_all | solution.py:367
  10.9 33.2 %copy-start = (f32[8,512]{1,0:T(8,128)S(1)}, f32[8,512]{1,0:T(8,128)}, u32[]{:S(2)}) copy-start(f32[8,512]{1,0:T(8,128)} %get-tuple-element.6.place_ref) | copy-start | bytes 49156
  10.9 33.2 %copy-start.1 = (f32[512]{0:T(512)S(1)}, f32[512]{0:T(512)}, u32[]{:S(2)}) copy-start(f32[512]{0:T(512)} %param.14) | copy-start | bytes 6148
  19.8 0.7 %copy-start.2 = (bf16[8,128,128]{2,1,0:T(8,128)(2,1)}, bf16[8,128,128]{2,1,0:T(8,128)(2,1)S(1)}, u32[]{:S(2)}) copy-start(bf16[8,128,128]{2,1,0:T(8,128)(2,1)S(1)} %all-to-all-done.in_ref) | copy-start | bytes 786436
  29.7 3.3 %collective-permute-start.2 = (f32[8,128]{1,0:T(8,128)}, f32[8,128]{1,0:T(8,128)S(1)}, u32[]{:S(2)}, u32[]{:S(2)}) collective-permute-start(f32[8,128]{1,0:T(8,128)} %value_and_allocate.1), channel_id=1, source_target_pairs={{0,3},{1,2},{2,1},{3,0},{4,7},{5,6},{6,5},{7,4},{8,11},{9,10},{10,... | collective-permute-start | bytes 12296 | tf_op jit(solution)/shard_map/ppermute | solution.py:322
  29.7 3.9 %collective-permute-start.1 = (f32[8,128]{1,0:T(8,128)}, f32[8,128]{1,0:T(8,128)S(1)}, u32[]{:S(2)}, u32[]{:S(2)}) collective-permute-start(f32[8,128]{1,0:T(8,128)} %value_and_allocate.1), channel_id=1, source_target_pairs={{0,2},{1,3},{2,0},{3,1},{4,6},{5,7},{6,4},{7,5},{8,10},{9,11},{10,... | collective-permute-start | bytes 12296 | tf_op jit(solution)/shard_map/ppermute | solution.py:322
  31.3 2.3 %collective-permute-start = (f32[8,128]{1,0:T(8,128)}, f32[8,128]{1,0:T(8,128)S(1)}, u32[]{:S(2)}, u32[]{:S(2)}) collective-permute-start(f32[8,128]{1,0:T(8,128)} %value_and_allocate.1), channel_id=1, source_target_pairs={{0,1},{1,0},{2,3},{3,2},{4,5},{5,4},{6,7},{7,6},{8,9},{9,8},{10,11... | collective-permute-start | bytes 12296 | tf_op jit(solution)/shard_map/ppermute | solution.py:322
  34.3 3.6 %collective-permute-start.3 = (f32[8,128]{1,0:T(8,128)S(1)}, f32[8,128]{1,0:T(8,128)S(1)}, u32[]{:S(2)}, u32[]{:S(2)}) collective-permute-start(f32[8,128]{1,0:T(8,128)S(1)} %add_add_fusion.own_ref), channel_id=1, source_target_pairs={{0,4},{4,0},{8,12},{12,8},{16,20},{20,16},{24,28},{28,24},{1,5},{5... | collective-permute-start | bytes 12296 | tf_op jit(solution)/shard_map/ppermute | solution.py:322
  38.0 5.4 %collective-permute-start.6 = (f32[16,128]{1,0:T(8,128)S(1)}, f32[16,128]{1,0:T(8,128)S(1)}, u32[]{:S(2)}, u32[]{:S(2)}) collective-permute-start(f32[16,128]{1,0:T(8,128)S(1)} %pad_maximum_fusion.refs_0_), channel_id=1, source_target_pairs={{0,24},{4,28},{8,16},{12,20},{16,8},{20,12},{24,0},{28,4},{1,25},{... | collective-permute-start | bytes 24584 | tf_op jit(solution)/shard_map/ppermute | solution.py:322
  39.4 4.5 %collective-permute-start.5 = (f32[16,128]{1,0:T(8,128)S(1)}, f32[16,128]{1,0:T(8,128)S(1)}, u32[]{:S(2)}, u32[]{:S(2)}) collective-permute-start(f32[16,128]{1,0:T(8,128)S(1)} %pad_maximum_fusion.refs_0_), channel_id=1, source_target_pairs={{0,16},{4,20},{8,24},{12,28},{16,0},{20,4},{24,8},{28,12},{1,17},{... | collective-permute-start | bytes 24584 | tf_op jit(solution)/shard_map/ppermute | solution.py:322
  40.5 3.7 %collective-permute-start.4 = (f32[16,128]{1,0:T(8,128)S(1)}, f32[16,128]{1,0:T(8,128)S(1)}, u32[]{:S(2)}, u32[]{:S(2)}) collective-permute-start(f32[16,128]{1,0:T(8,128)S(1)} %pad_maximum_fusion.refs_0_), channel_id=1, source_target_pairs={{0,8},{4,12},{8,0},{12,4},{16,24},{20,28},{24,16},{28,20},{1,9},{5... | collective-permute-start | bytes 24584 | tf_op jit(solution)/shard_map/ppermute | solution.py:322

commit v5 on v3

--- a/solution.py
+++ b/solution.py
@@ -12,7 +12,7 @@
 LAG_MAX = 4
 LANES = 128
 SUBS = 8
-DIRECT = 0
+DIRECT = 8
 
 RATE_UNIT = 0.03
 STEP = 0.25
@@ -72,8 +72,8 @@
         self.width = 512
 
 
-def pack_kernel(plan, me_ref, sets_hbm, coef_hbm, notional_hbm, place_ref, *refs):
-    *out_refs, sets_ref, coef_ref, notional_ref, sems = refs
+def pack_kernel(plan, me_ref, sets_hbm, coef_hbm, notional_hbm, place_ref, out_ref, *refs):
+    sets_ref, coef_ref, notional_ref, sems = refs
     copies = fetch(
         [sets_hbm, notional_hbm, coef_hbm], [sets_ref, notional_ref, coef_ref], sems
     )
@@ -90,8 +90,6 @@
     sets = in_a_row(own)
     key = lax.shift_right_logical(sets, 3)
     local = sets - key * NS_DEV
-    if plan.direct:
-        key = lax.bitwise_xor(key, me)
     hot = iota((owners, rows), 0) == key
     before = mask_bf16(iota((rows, rows), 0) < iota((rows, rows), 1))
     count = jnp.dot(mask_bf16(hot), before, preferred_element_type=F32)
@@ -112,7 +110,7 @@
     moved = lax.dot_general(chosen, table, BOTH_LANES, preferred_element_type=F32)
     ids = LANES + extra
     for d in range(owners):
-        message = out_refs[d] if plan.direct else out_refs[0].at[d]
+        message = out_ref.at[d]
         block = moved[d * room : (d + 1) * room]
         message[0:room, :] = block[:, 0:LANES].astype(BF16)
         split = [block[part * g : part * (g + 1)] for g in range(plan.groups)]
@@ -176,15 +174,13 @@
 
 
 def main_kernel(plan, path_total, me_ref, agr_ref, cpty_ref, lag_ref, weight_ref, basis_ref, *refs):
-    *in_refs, out_ref, val_ref = refs
+    in_ref, out_ref, val_ref = refs
     me = me_ref[0]
     part, room, dates = plan.part, plan.room, plan.dates
     cpty_dev = weight_ref.shape[0]
 
     def rows_of(first):
-        if plan.direct:
-            return jnp.concatenate([ref[first : first + part, :] for ref in in_refs], axis=0)
-        return in_refs[0][:, first : first + part, :].reshape(plan.owners * part, LANES)
+        return in_ref[:, first : first + part, :].reshape(plan.owners * part, LANES)
 
     rest = rows_of(room)
     lane = iota((1, LANES), 1)
@@ -263,21 +259,20 @@
     out_ref[...] = jnp.concatenate(lines, axis=0)
 
 
-def finish_kernel(plan, me_ref, place_ref, notional_ref, own_ref, *refs):
-    *in_refs, alloc_ref, cva_ref = refs
+def finish_kernel(plan, me_ref, place_ref, notional_ref, in_ref, alloc_ref, cva_ref):
     me = me_ref[0]
     part, per_line = plan.part, plan.per_line
     rows = place_ref.shape[1]
     key = place_ref[0:1, :].astype(jnp.int32)
     rank = place_ref[1:2, :].astype(jnp.int32)
     group = lax.div(rank, part)
-    slot = key if plan.direct else jnp.full_like(key, me)
-    line = group * plan.lines + lax.div(slot, per_line)
-    lane = lax.rem(slot, per_line) * part + (rank - group * part)
-    if plan.direct:
-        tiles = jnp.concatenate([ref[...] for ref in in_refs], axis=0)
-    else:
-        tiles = in_refs[0][...].reshape(plan.owners * plan.tile, LANES)
+    line = group * plan.lines + me // per_line
+    lane = lax.rem(me, per_line) * part + (rank - group * part)
+    tiles, own = in_ref[:, 0], in_ref[me, 0]
+    for p in range(1, in_ref.shape[1]):
+        tiles = tiles + in_ref[:, p]
+        own = own + in_ref[me, p]
+    tiles = tiles.reshape(plan.owners * plan.tile, LANES)
     hot = mask_bf16(iota((LANES, rows), 0) == lane)
     found = jnp.zeros((tiles.shape[0], rows), F32)
     for piece in split_bf16(tiles, 3):
@@ -286,7 +281,7 @@
     share = jnp.sum(jnp.where(wanted, found, 0.0), axis=0, keepdims=True)
     alloc_ref[...] = share * in_a_row(notional_ref[...])
     last = plan.groups * plan.lines
-    cva_ref[...] = own_ref[last : last + 1, 0 : cva_ref.shape[1]]
+    cva_ref[...] = own[last : last + 1, 0 : cva_ref.shape[1]]
 
 
 def permuted(x, axis, size, d):
@@ -316,16 +311,14 @@
     me = lax.axis_index("trade").astype(jnp.int32).reshape(1)
     notional = notional.reshape(lines, LANES)
 
-    message = jax.ShapeDtypeStruct((plan.height, LANES), BF16)
-    if plan.direct:
-        messages = [message] * owners
-    else:
-        messages = [jax.ShapeDtypeStruct((owners,) + message.shape, BF16)]
-    place, *outgoing = pl.pallas_call(
+    place, outgoing = pl.pallas_call(
         functools.partial(pack_kernel, plan),
-        out_shape=[jax.ShapeDtypeStruct((SUBS, rows), F32)] + messages,
+        out_shape=[
+            jax.ShapeDtypeStruct((SUBS, rows), F32),
+            jax.ShapeDtypeStruct((owners, plan.height, LANES), BF16),
+        ],
         in_specs=[SMEM] + [HBM] * 3,
-        out_specs=[VMEM] * (1 + len(messages)),
+        out_specs=[VMEM, VMEM],
         scratch_shapes=[
             pltpu.VMEM((owners * lines, LANES), jnp.int32),
             pltpu.VMEM((2 * tenors, rows), BF16),
@@ -334,12 +327,7 @@
         ],
         name="pack",
     )(me, ns_of_trade.reshape(owners * lines, LANES), coefficient.T, notional)
-    if plan.direct:
-        incoming = [outgoing[0]] + [
-            permuted(outgoing[d], "trade", owners, d) for d in range(1, owners)
-        ]
-    else:
-        incoming = [lax.all_to_all(outgoing[0], "trade", split_axis=0, concat_axis=0, tiled=True)]
+    incoming = lax.all_to_all(outgoing, "trade", split_axis=0, concat_axis=0, tiled=True)
 
     basis = pl.pallas_call(
         functools.partial(basis_kernel, plan),
@@ -354,6 +342,7 @@
             pltpu.SemaphoreType.DMA((3,)),
         ],
         name="basis",
+        compiler_params=pltpu.CompilerParams(vmem_limit_bytes=16 << 20),
         cost_estimate=pl.CostEstimate(
             flops=2 * 400 * tenors * cols, bytes_accessed=4 << 20, transcendentals=3 * tenors * cols
         ),
@@ -363,32 +352,35 @@
     tile = pl.pallas_call(
         functools.partial(main_kernel, plan, path_total),
         out_shape=jax.ShapeDtypeStruct((plan.tile, LANES), F32),
-        in_specs=[SMEM] * 4 + [VMEM] * (2 + len(incoming)),
+        in_specs=[SMEM] * 4 + [VMEM] * 3,
         out_specs=VMEM,
         scratch_shapes=[pltpu.VMEM((cols // plan.width, plan.trades, plan.width), BF16)],
         name="value_and_allocate",
         compiler_params=pltpu.CompilerParams(vmem_limit_bytes=need),
-    )(me, agr_of_ns, cpty_of_agr, margin_lag, default_weight, basis, *incoming)
-
-    others = [permuted(tile, "path", path_parts, d) for d in range(1, path_parts)]
-    for other in others:
-        tile = tile + other
+    )(me, agr_of_ns, cpty_of_agr, margin_lag, default_weight, basis, incoming)
+
     if plan.direct:
-        tiles = [tile] + [permuted(tile, "trade", owners, d) for d in range(1, owners)]
+        spread = jnp.broadcast_to(tile, (owners * path_parts,) + tile.shape)
+        tiles = lax.all_to_all(spread, ("trade", "path"), split_axis=0, concat_axis=0, tiled=True)
+        tiles = tiles.reshape((owners, path_parts) + tile.shape)
     else:
+        others = [permuted(tile, "path", path_parts, d) for d in range(1, path_parts)]
+        for other in others:
+            tile = tile + other
         spread = jnp.broadcast_to(tile, (owners,) + tile.shape)
-        tiles = [lax.all_to_all(spread, "trade", split_axis=0, concat_axis=0, tiled=True)]
+        tiles = lax.all_to_all(spread, "trade", split_axis=0, concat_axis=0, tiled=True)
+        tiles = tiles[:, None]
     allocation, cva = pl.pallas_call(
         functools.partial(finish_kernel, plan),
         out_shape=[
             jax.ShapeDtypeStruct((1, rows), F32),
             jax.ShapeDtypeStruct((1, default_weight.shape[0]), F32),
         ],
-        in_specs=[SMEM] + [VMEM] * (3 + len(tiles)),
+        in_specs=[SMEM] + [VMEM] * 3,
         out_specs=[VMEM, VMEM],
         name="finish",
         compiler_params=pltpu.CompilerParams(vmem_limit_bytes=32 << 20),
-    )(me, place, notional, tile, *tiles)
+    )(me, place, notional, tiles)
     return (allocation.reshape(rows), cva.reshape(default_weight.shape[0]))
 
 

time: 42.4 us -> 38.2 us (0.901)
  waiting for transfers between devices: 5.64 us -> 3.24 us
  starting transfers between devices: 9.21 us -> 7.29 us
  Pallas kernels: 14.3 us -> 12.4 us
  blocking collectives: 10.6 us -> 11.6 us
  local copies, waits for them, and re-layouts: 1.62 us -> 2.55 us
    pallas_call x1, Pallas kernels: 5.08 us -> 3.14 us  [body(): pl.pallas_call(functools.partial(basis_kernel, plan), out_shape=jax.Shape...]
    ppermute x3 -> x0, starting transfers between devices: 1.92 us -> none  [permuted(): return lax.ppermute(x, axis, [(i, i ^ d) for i in range(size)])]
    ppermute x3 -> x0, waiting for transfers between devices: 1.83 us -> none  [permuted(): return lax.ppermute(x, axis, [(i, i ^ d) for i in range(size)])]
    all_to_all x1, blocking collectives: 10.6 us -> 11.6 us  [body(): lax.all_to_all(spread, ('trade', 'path'), split_axis=0, concat_axis=0, ti...]
    unnamed x14 -> x18, local copies, waits for them, and re-layouts: 1.61 us -> 2.54 us
    all_to_all x1, waiting for transfers between devices: 3.81 us -> 3.24 us  [body(): lax.all_to_all(outgoing, 'trade', split_axis=0, concat_axis=0, tiled=True)]
  transfers between devices with their start and end apart: 4 -> 1, of which waited for: 3 -> 1; matrix products, arithmetic and copies ran while one was open for 0% -> 0% of each run, Pallas kernels for 12% -> 8%
where the time goes in v5:
time: 38.2 us; the launch traced here: 37.9 us
  Pallas kernels  12.4 us (32%)
  blocking collectives  11.6 us (30%)
  starting transfers between devices  7.29 us (19%)
  waiting for transfers between devices  3.24 us (8%)
  local copies, waits for them, and re-layouts  2.55 us (7%)
  between operations  0.72 us (2%)
    all_to_all x1, blocking collectives, body(): lax.all_to_all(spread, ('trade', 'path'), split_axis=0, concat_axis=0, ti...  11.6 us
    all_to_all x1, starting transfers between devices, body(): lax.all_to_all(outgoing, 'trade', split_axis=0, concat_axis=0, tiled=True)  7.29 us
    pallas_call x1, Pallas kernels, body(): pl.pallas_call(functools.partial(main_kernel, plan, path_total), out_shap...  6.15 us
    all_to_all x1, waiting for transfers between devices, body(): lax.all_to_all(outgoing, 'trade', split_axis=0, concat_axis=0, tiled=True)  3.24 us
    pallas_call x1, Pallas kernels, body(): pl.pallas_call(functools.partial(basis_kernel, plan), out_shape=jax.Shape...  3.14 us
    unnamed x18, local copies, waits for them, and re-layouts  2.54 us
    pallas_call x1, Pallas kernels, body(): pl.pallas_call(functools.partial(pack_kernel, plan), out_shape=[jax.Shape...  2.31 us
    pallas_call x1, Pallas kernels, body(): pl.pallas_call(functools.partial(finish_kernel, plan), out_shape=[jax.Sha...  0.81 us
  transfers between devices with their start and end apart: 1, of which 1 were waited for; matrix products, arithmetic and copies ran while one was open for 0% of the time, Pallas kernels for 8%

profile of v5, /device:TPU:0, one launch (start us, length us, event | category | flops | bytes accessed | tf_op | source)
XLA Modules:
  0.0 37.9 jit_solution(7469698664568034462)
XLA Ops:
  0.6 0.0 copy-start.4
  0.6 0.0 copy-start.8
  0.7 0.0 copy-start.7
  0.7 0.0 copy-start.6
  0.7 2.3 %pack.1 = (f32[8,512]{1,0:T(8,128)}, bf16[8,128,128]{2,1,0:T(8,128)(2,1)}) custom-call(s32[1]{0:T(128)} %bitcast.me_ref, s32[32,128]{1,0:T(8,128)} %bitcast.15, bf16[160,512]{1,0:T(8,128)(2,1)} %bitcast.14, f32[4,128]{1,0:T(4,128)} %bitcast.11), custom_call_target="tpu_custom_call" | custom-call | tf_op jit(solution)/shard_map/pack/pallas_call | solution.py:314
  3.0 7.3 %all-to-all-start = ((bf16[8,128,128]{2,1,0:T(8,128)(2,1)}), bf16[8,128,128]{2,1,0:T(8,128)(2,1)S(1)}, u32[]{:S(2)}, u32[]{:S(2)}) async-start(bf16[8,128,128]{2,1,0:T(8,128)(2,1)} %get-tuple-element.7), calls=%async_computation | async-start | bytes 524288 | tf_op jit(solution)/shard_map/all_to_all | solution.py:330
  10.3 0.0 copy-start
  10.3 1.1 %copy-done = bf16[80,32,128]{2,1,0:T(8,128)(2,1)S(1)} copy-done((bf16[80,32,128]{2,1,0:T(8,128)(2,1)S(1)}, bf16[80,32,128]{2,1,0:T(8,128)(2,1)}, u32[]{:S(2)}) %copy-start) | copy-done | bytes 655384
  11.4 0.0 copy-start.1
  11.4 0.8 %copy-done.1 = f32[80,80]{1,0:T(8,128)S(1)} copy-done((f32[80,80]{1,0:T(8,128)S(1)}, f32[80,80]{1,0:T(8,128)}, u32[]{:S(2)}) %copy-start.1) | copy-done | bytes 25624
  12.2 0.0 copy-start.5
  12.2 0.7 %copy-done.5 = f32[80]{0:T(128)S(1)} copy-done((f32[80]{0:T(128)S(1)}, f32[80]{0:T(128)}, u32[]{:S(2)}) %copy-start.5) | copy-done | bytes 344
  12.8 0.0 copy-start.2
  12.8 0.0 copy-start.3
  12.8 3.1 %basis.1.basis_ref = bf16[256,4096]{1,0:T(8,128)(2,1)S(1)} custom-call(bf16[2560,128]{1,0:T(8,128)(2,1)S(1)} %bitcast.9, f32[1,80]{1,0:T(1,128)S(1)} %bitcast.13, f32[80,80]{1,0:T(8,128)S(1)} %copy-done.1), custom_call_target="tpu_custom_call" | custom-call | flops 262144000 | bytes 4194304 | tf_op jit(solution)/shard_map/basis/pallas_call | solution.py:332
  16.0 3.2 %all-to-all-done.refs_0_ = bf16[8,128,128]{2,1,0:T(8,128)(2,1)S(1)} async-done(((bf16[8,128,128]{2,1,0:T(8,128)(2,1)}), bf16[8,128,128]{2,1,0:T(8,128)(2,1)S(1)}, u32[]{:S(2)}, u32[]{:S(2)}) %all-to-all-start) | async-done | bytes 262176 | tf_op jit(solution)/shard_map/all_to_all | solution.py:330
  19.2 0.0 copy-done.4
  19.2 0.0 copy-done.8
  19.2 0.0 copy-done.7
  19.2 0.0 copy-done.6
  19.2 6.2 %value_and_allocate.1 = f32[8,128]{1,0:T(8,128)S(1)} custom-call(s32[1]{0:T(128)} %bitcast.me_ref, s32[8]{0:T(128)S(1)} %copy-done.6, s32[4]{0:T(128)S(1)} %copy-done.7, s32[4]{0:T(128)S(1)} %copy-done.8, f32[4,32]{1,0:T(4,128)S(1)} %copy-done.4, bf16[256,4096]{1,0:T(8,128)(2,1)S(1)} %basis.1.basis_ref, bf16[8,128,128]{2,1,0:T(8,128)(2,1)S(1)} %all-to-all-done.refs_0_), custom_call_target="tpu_custom_call" | custom-call | tf_op jit(solution)/shard_map/value_and_allocate/pallas_call | solution.py:352
  25.4 11.6 %all_to_all.10 = f32[32,8,128]{2,1,0:T(8,128)S(1)} all-to-all(f32[32,8,128]{2,1,0:T(8,128)S(1)} %broadcast_in_dim.3), channel_id=1, replica_groups=mesh['trade'=8,'path'=4] {'trade','path'}, dimensions={0} | all-to-all | bytes 262144 | tf_op jit(solution)/shard_map/all_to_all | solution.py:364
  37.0 0.0 copy-done.2
  37.0 0.0 copy-done.3
  37.1 0.8 %finish.1 = (f32[1,512]{1,0:T(1,128)}, f32[1,4]{1,0:T(1,128)}) custom-call(s32[1]{0:T(128)} %bitcast.me_ref, f32[8,512]{1,0:T(8,128)S(1)} %copy-done.2, f32[4,128]{1,0:T(4,128)S(1)} %bitcast.12, f32[8,4,8,128]{3,2,1,0:T(8,128)S(1)} %bitcast.10), custom_call_target="tpu_custom_call" | custom-call | tf_op jit(solution)/shard_map/finish/pallas_call | solution.py:373
  (1 shorter events, 0.0 us)
Async XLA Ops:
  0.6 18.6 %copy-start.4 = (f32[4,32]{1,0:T(4,128)S(1)}, f32[4,32]{1,0:T(4,128)}, u32[]{:S(2)}) copy-start(f32[4,32]{1,0:T(4,128)} %weight_ref.1) | copy-start | bytes 1540
  0.6 18.6 %copy-start.8 = (s32[4]{0:T(128)S(1)}, s32[4]{0:T(128)}, u32[]{:S(2)}) copy-start(s32[4]{0:T(128)} %lag_ref.1) | copy-start | bytes 52
  0.7 18.6 %copy-start.7 = (s32[4]{0:T(128)S(1)}, s32[4]{0:T(128)}, u32[]{:S(2)}) copy-start(s32[4]{0:T(128)} %cpty_ref.1) | copy-start | bytes 52
  0.7 18.6 %copy-start.6 = (s32[8]{0:T(128)S(1)}, s32[8]{0:T(128)}, u32[]{:S(2)}) copy-start(s32[8]{0:T(128)} %agr_ref.1) | copy-start | bytes 100
  3.0 16.2 %all-to-all-start = ((bf16[8,128,128]{2,1,0:T(8,128)(2,1)}), bf16[8,128,128]{2,1,0:T(8,128)(2,1)S(1)}, u32[]{:S(2)}, u32[]{:S(2)}) async-start(bf16[8,128,128]{2,1,0:T(8,128)(2,1)} %get-tuple-element.7), calls=%async_computation | async-start | bytes 524288 | tf_op jit(solution)/shard_map/all_to_all | solution.py:330
  10.3 1.1 %copy-start = (bf16[80,32,128]{2,1,0:T(8,128)(2,1)S(1)}, bf16[80,32,128]{2,1,0:T(8,128)(2,1)}, u32[]{:S(2)}) copy-start(bf16[80,32,128]{2,1,0:T(8,128)(2,1)} %param.10) | copy-start | bytes 1966084
  11.4 0.8 %copy-start.1 = (f32[80,80]{1,0:T(8,128)S(1)}, f32[80,80]{1,0:T(8,128)}, u32[]{:S(2)}) copy-start(f32[80,80]{1,0:T(8,128)} %loading_hbm.1) | copy-start | bytes 76804
  12.2 0.7 %copy-start.5 = (f32[80]{0:T(128)S(1)}, f32[80]{0:T(128)}, u32[]{:S(2)}) copy-start(f32[80]{0:T(128)} %param.11) | copy-start | bytes 964
  12.8 24.2 %copy-start.2 = (f32[8,512]{1,0:T(8,128)S(1)}, f32[8,512]{1,0:T(8,128)}, u32[]{:S(2)}) copy-start(f32[8,512]{1,0:T(8,128)} %get-tuple-element.6.place_ref) | copy-start | bytes 49156
  12.8 24.2 %copy-start.3 = (f32[512]{0:T(512)S(1)}, f32[512]{0:T(512)}, u32[]{:S(2)}) copy-start(f32[512]{0:T(512)} %param.14) | copy-start | bytes 6148

commit v6 on v5

--- a/solution.py
+++ b/solution.py
@@ -12,7 +12,6 @@
 LAG_MAX = 4
 LANES = 128
 SUBS = 8
-DIRECT = 8
 
 RATE_UNIT = 0.03
 STEP = 0.25
@@ -58,7 +57,6 @@
     def __init__(self, owners, rows, tenors, dates):
         most = 3 * rows // (2 * owners)
         self.owners = owners
-        self.direct = owners <= DIRECT
         self.groups = 3 if most % 48 == 0 else 1
         self.part = -(-most // (16 * self.groups)) * 16
         self.room = self.groups * self.part
@@ -67,9 +65,9 @@
         self.per_line = LANES // self.part
         self.lines = owners * self.part // LANES
         self.trades = owners * self.room
-        self.tile = -(-(self.groups * self.lines + 1) // SUBS) * SUBS
         self.dates = dates
         self.width = 512
+        self.step = 256
 
 
 def pack_kernel(plan, me_ref, sets_hbm, coef_hbm, notional_hbm, place_ref, out_ref, *refs):
@@ -201,7 +199,7 @@
     netting = jnp.where(hot, jnp.where(row < AG_DEV, info[0:1], info[1:2]), 0.0).astype(BF16)
 
     owed = []
-    width = plan.width
+    width = plan.step
     chunks = dates * LANES // width
     for c in range(chunks):
         under = jnp.dot(
@@ -250,42 +248,42 @@
             part_grads, val_ref[c], BOTH_LANES, preferred_element_type=F32
         )
     share = jnp.sum(jnp.where(hot & (row < AG_DEV), dots, 0.0), axis=0, keepdims=True)
-    lines = [share[:, LANES * k : LANES * (k + 1)] for k in range(plan.trades // LANES)]
     spent = jnp.sum(spent, axis=1, keepdims=True) * (1.0 / path_total)
-    mine = (lane == cpty) & (iota((SUBS, LANES), 0) < AG_DEV)
-    lines.append(jnp.sum(jnp.where(mine, spent, 0.0), axis=0, keepdims=True))
-    if len(lines) < plan.tile:
-        lines.append(jnp.zeros((plan.tile - len(lines), LANES), F32))
-    out_ref[...] = jnp.concatenate(lines, axis=0)
+    mine = (lane - room == cpty) & (iota((SUBS, LANES), 0) < AG_DEV)
+    cva = jnp.sum(jnp.where(mine, spent, 0.0), axis=0, keepdims=True)
+    block = lane // part
+    count = plan.groups * plan.lines
+    lines = jnp.concatenate([share[:, LANES * k : LANES * (k + 1)] for k in range(count)], axis=0)
+    moved = [lines if m == 0 else pltpu.roll(lines, part * m, 1) for m in range(plan.per_line)]
+    paths = out_ref.shape[0] // plan.owners
+    for k in range(plan.lines):
+        for s in range(plan.per_line):
+            line = cva
+            for g in range(plan.groups):
+                n = g * plan.lines + k
+                line = jnp.where(block == g, moved[(g - s) % plan.per_line][n : n + 1], line)
+            for p in range(paths):
+                out_ref[(k * plan.per_line + s) * paths + p] = line
 
 
 def finish_kernel(plan, me_ref, place_ref, notional_ref, in_ref, alloc_ref, cva_ref):
     me = me_ref[0]
-    part, per_line = plan.part, plan.per_line
     rows = place_ref.shape[1]
     key = place_ref[0:1, :].astype(jnp.int32)
     rank = place_ref[1:2, :].astype(jnp.int32)
-    group = lax.div(rank, part)
-    line = group * plan.lines + me // per_line
-    lane = lax.rem(me, per_line) * part + (rank - group * part)
-    tiles, own = in_ref[:, 0], in_ref[me, 0]
-    for p in range(1, in_ref.shape[1]):
-        tiles = tiles + in_ref[:, p]
-        own = own + in_ref[me, p]
-    tiles = tiles.reshape(plan.owners * plan.tile, LANES)
-    hot = mask_bf16(iota((LANES, rows), 0) == lane)
-    found = jnp.zeros((tiles.shape[0], rows), F32)
-    for piece in split_bf16(tiles, 3):
+    lines = in_ref[...]
+    count = lines.shape[0]
+    paths = count // plan.owners
+    hot = mask_bf16(iota((LANES, rows), 0) == rank)
+    found = jnp.zeros((count, rows), F32)
+    for piece in split_bf16(lines, 3):
         found = found + jnp.dot(piece, hot, preferred_element_type=F32)
-    wanted = iota(found.shape, 0) == key * plan.tile + line
+    wanted = iota(found.shape, 0) // paths == key
     share = jnp.sum(jnp.where(wanted, found, 0.0), axis=0, keepdims=True)
     alloc_ref[...] = share * in_a_row(notional_ref[...])
-    last = plan.groups * plan.lines
-    cva_ref[...] = own[last : last + 1, 0 : cva_ref.shape[1]]
-
-
-def permuted(x, axis, size, d):
-    return lax.ppermute(x, axis, [(i, i ^ d) for i in range(size)])
+    own = iota(lines.shape, 0) // paths == me
+    cva = jnp.sum(jnp.where(own, lines, 0.0), axis=0, keepdims=True)
+    cva_ref[...] = cva[:, plan.room : plan.room + cva_ref.shape[1]]
 
 
 def body(
@@ -349,27 +347,18 @@
     )(shocks.reshape(tenors * dates, path_dev), forward_start.reshape(1, tenors), loading)
 
     need = 2 * plan.trades * cols + 16 * plan.trades * plan.width + (8 << 20)
-    tile = pl.pallas_call(
+    lines_out = pl.pallas_call(
         functools.partial(main_kernel, plan, path_total),
-        out_shape=jax.ShapeDtypeStruct((plan.tile, LANES), F32),
+        out_shape=jax.ShapeDtypeStruct((owners * path_parts, 1, LANES), F32),
         in_specs=[SMEM] * 4 + [VMEM] * 3,
         out_specs=VMEM,
-        scratch_shapes=[pltpu.VMEM((cols // plan.width, plan.trades, plan.width), BF16)],
+        scratch_shapes=[pltpu.VMEM((cols // plan.step, plan.trades, plan.step), BF16)],
         name="value_and_allocate",
         compiler_params=pltpu.CompilerParams(vmem_limit_bytes=need),
     )(me, agr_of_ns, cpty_of_agr, margin_lag, default_weight, basis, incoming)
 
-    if plan.direct:
-        spread = jnp.broadcast_to(tile, (owners * path_parts,) + tile.shape)
-        tiles = lax.all_to_all(spread, ("trade", "path"), split_axis=0, concat_axis=0, tiled=True)
-        tiles = tiles.reshape((owners, path_parts) + tile.shape)
-    else:
-        others = [permuted(tile, "path", path_parts, d) for d in range(1, path_parts)]
-        for other in others:
-            tile = tile + other
-        spread = jnp.broadcast_to(tile, (owners,) + tile.shape)
-        tiles = lax.all_to_all(spread, "trade", split_axis=0, concat_axis=0, tiled=True)
-        tiles = tiles[:, None]
+    lines_in = lax.all_to_all(lines_out, ("trade", "path"), split_axis=0, concat_axis=0, tiled=True)
+    lines_in = lines_in.reshape(owners * path_parts, LANES)
     allocation, cva = pl.pallas_call(
         functools.partial(finish_kernel, plan),
         out_shape=[
@@ -380,7 +369,7 @@
         out_specs=[VMEM, VMEM],
         name="finish",
         compiler_params=pltpu.CompilerParams(vmem_limit_bytes=32 << 20),
-    )(me, place, notional, tiles)
+    )(me, place, notional, lines_in)
     return (allocation.reshape(rows), cva.reshape(default_weight.shape[0]))
 
 

time: 38.2 us -> 39 us (1.021)
  Pallas kernels: 12.4 us -> 14.3 us
  blocking collectives: 11.6 us -> 10.6 us
    pallas_call x1, Pallas kernels: 6.15 us -> 8.07 us  [body(): pl.pallas_call(functools.partial(main_kernel, plan, path_total), out_shap...]
    all_to_all x1, blocking collectives: 11.6 us -> 10.6 us  [body(): lax.all_to_all(lines_out, ('trade', 'path'), split_axis=0, concat_axis=0,...]
where the time goes in v6:
time: 39 us; the launch traced here: 38.7 us
  Pallas kernels  14.3 us (37%)
  blocking collectives  10.6 us (27%)
  starting transfers between devices  7.29 us (19%)
  waiting for transfers between devices  3.24 us (8%)
  local copies, waits for them, and re-layouts  2.54 us (7%)
  between operations  0.71 us (2%)
    all_to_all x1, blocking collectives, body(): lax.all_to_all(lines_out, ('trade', 'path'), split_axis=0, concat_axis=0,...  10.6 us
    pallas_call x1, Pallas kernels, body(): pl.pallas_call(functools.partial(main_kernel, plan, path_total), out_shap...  8.07 us
    all_to_all x1, starting transfers between devices, body(): lax.all_to_all(outgoing, 'trade', split_axis=0, concat_axis=0, tiled=True)  7.29 us
    all_to_all x1, waiting for transfers between devices, body(): lax.all_to_all(outgoing, 'trade', split_axis=0, concat_axis=0, tiled=True)  3.24 us
    pallas_call x1, Pallas kernels, body(): pl.pallas_call(functools.partial(basis_kernel, plan), out_shape=jax.Shape...  3.14 us
    unnamed x18, local copies, waits for them, and re-layouts  2.54 us
    pallas_call x1, Pallas kernels, body(): pl.pallas_call(functools.partial(pack_kernel, plan), out_shape=[jax.Shape...  2.31 us
    pallas_call x1, Pallas kernels, body(): pl.pallas_call(functools.partial(finish_kernel, plan), out_shape=[jax.Sha...  0.79 us
  transfers between devices with their start and end apart: 1, of which 1 were waited for; matrix products, arithmetic and copies ran while one was open for 0% of the time, Pallas kernels for 8%

profile of v6, /device:TPU:0, one launch (start us, length us, event | category | flops | bytes accessed | tf_op | source)
XLA Modules:
  0.0 38.7 jit_solution(153925926311584654)
XLA Ops:
  0.6 0.0 copy-start.4
  0.6 0.0 copy-start.8
  0.7 0.0 copy-start.7
  0.7 0.0 copy-start.6
  0.7 2.3 %pack.1 = (f32[8,512]{1,0:T(8,128)}, bf16[8,128,128]{2,1,0:T(8,128)(2,1)}) custom-call(s32[1]{0:T(128)} %bitcast.me_ref, s32[32,128]{1,0:T(8,128)} %bitcast.15, bf16[160,512]{1,0:T(8,128)(2,1)} %bitcast.14, f32[4,128]{1,0:T(4,128)} %bitcast.11), custom_call_target="tpu_custom_call" | custom-call | tf_op jit(solution)/shard_map/pack/pallas_call | solution.py:312
  3.0 7.3 %all-to-all-start = ((bf16[8,128,128]{2,1,0:T(8,128)(2,1)}), bf16[8,128,128]{2,1,0:T(8,128)(2,1)S(1)}, u32[]{:S(2)}, u32[]{:S(2)}) async-start(bf16[8,128,128]{2,1,0:T(8,128)(2,1)} %get-tuple-element.7), calls=%async_computation | async-start | bytes 524288 | tf_op jit(solution)/shard_map/all_to_all | solution.py:328
  10.3 0.0 copy-start
  10.3 1.1 %copy-done = bf16[80,32,128]{2,1,0:T(8,128)(2,1)S(1)} copy-done((bf16[80,32,128]{2,1,0:T(8,128)(2,1)S(1)}, bf16[80,32,128]{2,1,0:T(8,128)(2,1)}, u32[]{:S(2)}) %copy-start) | copy-done | bytes 655384
  11.4 0.0 copy-start.1
  11.4 0.8 %copy-done.1 = f32[80,80]{1,0:T(8,128)S(1)} copy-done((f32[80,80]{1,0:T(8,128)S(1)}, f32[80,80]{1,0:T(8,128)}, u32[]{:S(2)}) %copy-start.1) | copy-done | bytes 25624
  12.2 0.0 copy-start.5
  12.2 0.7 %copy-done.5 = f32[80]{0:T(128)S(1)} copy-done((f32[80]{0:T(128)S(1)}, f32[80]{0:T(128)}, u32[]{:S(2)}) %copy-start.5) | copy-done | bytes 344
  12.8 0.0 copy-start.2
  12.8 0.0 copy-start.3
  12.8 3.1 %basis.1.basis_ref = bf16[256,4096]{1,0:T(8,128)(2,1)S(1)} custom-call(bf16[2560,128]{1,0:T(8,128)(2,1)S(1)} %bitcast.9, f32[1,80]{1,0:T(1,128)S(1)} %bitcast.13, f32[80,80]{1,0:T(8,128)S(1)} %copy-done.1), custom_call_target="tpu_custom_call" | custom-call | flops 262144000 | bytes 4194304 | tf_op jit(solution)/shard_map/basis/pallas_call | solution.py:330
  16.0 3.2 %all-to-all-done.refs_0_ = bf16[8,128,128]{2,1,0:T(8,128)(2,1)S(1)} async-done(((bf16[8,128,128]{2,1,0:T(8,128)(2,1)}), bf16[8,128,128]{2,1,0:T(8,128)(2,1)S(1)}, u32[]{:S(2)}, u32[]{:S(2)}) %all-to-all-start) | async-done | bytes 262176 | tf_op jit(solution)/shard_map/all_to_all | solution.py:328
  19.2 0.0 copy-done.4
  19.2 0.0 copy-done.8
  19.2 0.0 copy-done.7
  19.2 0.0 copy-done.6
  19.2 8.1 %value_and_allocate.1 = f32[32,1,128]{2,1,0:T(1,128)S(1)} custom-call(s32[1]{0:T(128)} %bitcast.me_ref, s32[8]{0:T(128)S(1)} %copy-done.6, s32[4]{0:T(128)S(1)} %copy-done.7, s32[4]{0:T(128)S(1)} %copy-done.8, f32[4,32]{1,0:T(4,128)S(1)} %copy-done.4, bf16[256,4096]{1,0:T(8,128)(2,1)S(1)} %basis.1.basis_ref, bf16[8,128,128]{2,1,0:T(8,128)(2,1)S(1)} %all-to-all-done.refs_0_), custom_call_target="tpu_custom_call" | custom-call | tf_op jit(solution)/shard_map/value_and_allocate/pallas_call | solution.py:350
  27.3 10.6 %all_to_all.10 = f32[32,1,128]{2,1,0:T(1,128)S(1)} all-to-all(f32[32,1,128]{2,1,0:T(1,128)S(1)} %value_and_allocate.1), channel_id=1, replica_groups=mesh['trade'=8,'path'=4] {'trade','path'}, dimensions={0} | all-to-all | bytes 32768 | tf_op jit(solution)/shard_map/all_to_all | solution.py:360
  37.9 0.0 copy-done.2
  37.9 0.0 copy-done.3
  37.9 0.8 %finish.1 = (f32[1,512]{1,0:T(1,128)}, f32[1,4]{1,0:T(1,128)}) custom-call(s32[1]{0:T(128)} %bitcast.me_ref, f32[8,512]{1,0:T(8,128)S(1)} %copy-done.2, f32[4,128]{1,0:T(4,128)S(1)} %bitcast.12, f32[32,128]{1,0:T(8,128)S(1)} %bitcast.10), custom_call_target="tpu_custom_call" | custom-call | tf_op jit(solution)/shard_map/finish/pallas_call | solution.py:362
Async XLA Ops:
  0.6 18.6 %copy-start.4 = (f32[4,32]{1,0:T(4,128)S(1)}, f32[4,32]{1,0:T(4,128)}, u32[]{:S(2)}) copy-start(f32[4,32]{1,0:T(4,128)} %weight_ref.1) | copy-start | bytes 1540
  0.6 18.6 %copy-start.8 = (s32[4]{0:T(128)S(1)}, s32[4]{0:T(128)}, u32[]{:S(2)}) copy-start(s32[4]{0:T(128)} %lag_ref.1) | copy-start | bytes 52
  0.7 18.6 %copy-start.7 = (s32[4]{0:T(128)S(1)}, s32[4]{0:T(128)}, u32[]{:S(2)}) copy-start(s32[4]{0:T(128)} %cpty_ref.1) | copy-start | bytes 52
  0.7 18.6 %copy-start.6 = (s32[8]{0:T(128)S(1)}, s32[8]{0:T(128)}, u32[]{:S(2)}) copy-start(s32[8]{0:T(128)} %agr_ref.1) | copy-start | bytes 100
  3.0 16.2 %all-to-all-start = ((bf16[8,128,128]{2,1,0:T(8,128)(2,1)}), bf16[8,128,128]{2,1,0:T(8,128)(2,1)S(1)}, u32[]{:S(2)}, u32[]{:S(2)}) async-start(bf16[8,128,128]{2,1,0:T(8,128)(2,1)} %get-tuple-element.7), calls=%async_computation | async-start | bytes 524288 | tf_op jit(solution)/shard_map/all_to_all | solution.py:328
  10.3 1.1 %copy-start = (bf16[80,32,128]{2,1,0:T(8,128)(2,1)S(1)}, bf16[80,32,128]{2,1,0:T(8,128)(2,1)}, u32[]{:S(2)}) copy-start(bf16[80,32,128]{2,1,0:T(8,128)(2,1)} %param.10) | copy-start | bytes 1966084
  11.4 0.8 %copy-start.1 = (f32[80,80]{1,0:T(8,128)S(1)}, f32[80,80]{1,0:T(8,128)}, u32[]{:S(2)}) copy-start(f32[80,80]{1,0:T(8,128)} %loading_hbm.1) | copy-start | bytes 76804
  12.2 0.7 %copy-start.5 = (f32[80]{0:T(128)S(1)}, f32[80]{0:T(128)}, u32[]{:S(2)}) copy-start(f32[80]{0:T(128)} %param.11) | copy-start | bytes 964
  12.8 25.1 %copy-start.2 = (f32[8,512]{1,0:T(8,128)S(1)}, f32[8,512]{1,0:T(8,128)}, u32[]{:S(2)}) copy-start(f32[8,512]{1,0:T(8,128)} %get-tuple-element.6.place_ref) | copy-start | bytes 49156
  12.8 25.1 %copy-start.3 = (f32[512]{0:T(512)S(1)}, f32[512]{0:T(512)}, u32[]{:S(2)}) copy-start(f32[512]{0:T(512)} %param.14) | copy-start | bytes 6148

commit v7 on v6

--- a/solution.py
+++ b/solution.py
@@ -67,7 +67,7 @@
         self.trades = owners * self.room
         self.dates = dates
         self.width = 512
-        self.step = 256
+        self.step = 1024
 
 
 def pack_kernel(plan, me_ref, sets_hbm, coef_hbm, notional_hbm, place_ref, out_ref, *refs):
@@ -206,7 +206,7 @@
             left, basis_ref[:, c * width : (c + 1) * width], preferred_element_type=F32
         )
         value = jnp.maximum(under, 0.0).astype(BF16)
-        val_ref[c] = value
+        val_ref[:, c * width : (c + 1) * width] = value
         both = jnp.dot(netting, value, preferred_element_type=F32)
         both = both + pltpu.roll(both, AG_DEV, 0)
         owed += [both[:, LANES * j : LANES * (j + 1)] for j in range(width // LANES)]
@@ -240,13 +240,9 @@
             after = jnp.where(lags[s - 1], slopes[t + s], after)
         grads.append(((slopes[t] - after) * (1.0 / path_total)).astype(BF16))
 
-    dots = jnp.zeros((SUBS, plan.trades), F32)
-    step = width // LANES
-    for c in range(chunks):
-        part_grads = jnp.concatenate(grads[c * step : (c + 1) * step], axis=1)
-        dots = dots + lax.dot_general(
-            part_grads, val_ref[c], BOTH_LANES, preferred_element_type=F32
-        )
+    dots = lax.dot_general(
+        jnp.concatenate(grads, axis=1), val_ref[...], BOTH_LANES, preferred_element_type=F32
+    )
     share = jnp.sum(jnp.where(hot & (row < AG_DEV), dots, 0.0), axis=0, keepdims=True)
     spent = jnp.sum(spent, axis=1, keepdims=True) * (1.0 / path_total)
     mine = (lane - room == cpty) & (iota((SUBS, LANES), 0) < AG_DEV)
@@ -346,13 +342,13 @@
         ),
     )(shocks.reshape(tenors * dates, path_dev), forward_start.reshape(1, tenors), loading)
 
-    need = 2 * plan.trades * cols + 16 * plan.trades * plan.width + (8 << 20)
+    need = 2 * plan.trades * cols + 8 * plan.trades * plan.step + (8 << 20)
     lines_out = pl.pallas_call(
         functools.partial(main_kernel, plan, path_total),
         out_shape=jax.ShapeDtypeStruct((owners * path_parts, 1, LANES), F32),
         in_specs=[SMEM] * 4 + [VMEM] * 3,
         out_specs=VMEM,
-        scratch_shapes=[pltpu.VMEM((cols // plan.step, plan.trades, plan.step), BF16)],
+        scratch_shapes=[pltpu.VMEM((plan.trades, cols), BF16)],
         name="value_and_allocate",
         compiler_params=pltpu.CompilerParams(vmem_limit_bytes=need),
     )(me, agr_of_ns, cpty_of_agr, margin_lag, default_weight, basis, incoming)

time: 39 us -> 36.7 us (0.941)
  Pallas kernels: 14.3 us -> 11.9 us
    pallas_call x1, Pallas kernels: 8.07 us -> 5.7 us  [body(): pl.pallas_call(functools.partial(main_kernel, plan, path_total), out_shap...]
  transfers between devices with their start and end apart: 1 -> 1, of which waited for: 1 -> 1; matrix products, arithmetic and copies ran while one was open for 0% -> 0% of each run, Pallas kernels for 8% -> 9%
where the time goes in v7:
time: 36.7 us; the launch traced here: 36.3 us
  Pallas kernels  11.9 us (32%)
  blocking collectives  10.6 us (29%)
  starting transfers between devices  7.29 us (20%)
  waiting for transfers between devices  3.24 us (9%)
  local copies, waits for them, and re-layouts  2.54 us (7%)
  between operations  0.71 us (2%)
    all_to_all x1, blocking collectives, body(): lax.all_to_all(lines_out, ('trade', 'path'), split_axis=0, concat_axis=0,...  10.6 us
    all_to_all x1, starting transfers between devices, body(): lax.all_to_all(outgoing, 'trade', split_axis=0, concat_axis=0, tiled=True)  7.29 us
    pallas_call x1, Pallas kernels, body(): pl.pallas_call(functools.partial(main_kernel, plan, path_total), out_shap...  5.7 us
    all_to_all x1, waiting for transfers between devices, body(): lax.all_to_all(outgoing, 'trade', split_axis=0, concat_axis=0, tiled=True)  3.24 us
    pallas_call x1, Pallas kernels, body(): pl.pallas_call(functools.partial(basis_kernel, plan), out_shape=jax.Shape...  3.14 us
    unnamed x18, local copies, waits for them, and re-layouts  2.54 us
    pallas_call x1, Pallas kernels, body(): pl.pallas_call(functools.partial(pack_kernel, plan), out_shape=[jax.Shape...  2.31 us
    pallas_call x1, Pallas kernels, body(): pl.pallas_call(functools.partial(finish_kernel, plan), out_shape=[jax.Sha...  0.79 us
  transfers between devices with their start and end apart: 1, of which 1 were waited for; matrix products, arithmetic and copies ran while one was open for 0% of the time, Pallas kernels for 9%

profile of v7, /device:TPU:0, one launch (start us, length us, event | category | flops | bytes accessed | tf_op | source)
XLA Modules:
  0.0 36.3 jit_solution(6987870313153915872)
XLA Ops:
  0.6 0.0 copy-start.4
  0.6 0.0 copy-start.8
  0.7 0.0 copy-start.7
  0.7 0.0 copy-start.6
  0.7 2.3 %pack.1 = (f32[8,512]{1,0:T(8,128)}, bf16[8,128,128]{2,1,0:T(8,128)(2,1)}) custom-call(s32[1]{0:T(128)} %bitcast.me_ref, s32[32,128]{1,0:T(8,128)} %bitcast.15, bf16[160,512]{1,0:T(8,128)(2,1)} %bitcast.14, f32[4,128]{1,0:T(4,128)} %bitcast.11), custom_call_target="tpu_custom_call" | custom-call | tf_op jit(solution)/shard_map/pack/pallas_call | solution.py:308
  3.0 7.3 %all-to-all-start = ((bf16[8,128,128]{2,1,0:T(8,128)(2,1)}), bf16[8,128,128]{2,1,0:T(8,128)(2,1)S(1)}, u32[]{:S(2)}, u32[]{:S(2)}) async-start(bf16[8,128,128]{2,1,0:T(8,128)(2,1)} %get-tuple-element.7), calls=%async_computation | async-start | bytes 524288 | tf_op jit(solution)/shard_map/all_to_all | solution.py:324
  10.3 0.0 copy-start
  10.3 1.1 %copy-done = bf16[80,32,128]{2,1,0:T(8,128)(2,1)S(1)} copy-done((bf16[80,32,128]{2,1,0:T(8,128)(2,1)S(1)}, bf16[80,32,128]{2,1,0:T(8,128)(2,1)}, u32[]{:S(2)}) %copy-start) | copy-done | bytes 655384
  11.4 0.0 copy-start.1
  11.4 0.8 %copy-done.1 = f32[80,80]{1,0:T(8,128)S(1)} copy-done((f32[80,80]{1,0:T(8,128)S(1)}, f32[80,80]{1,0:T(8,128)}, u32[]{:S(2)}) %copy-start.1) | copy-done | bytes 25624
  12.2 0.0 copy-start.5
  12.2 0.7 %copy-done.5 = f32[80]{0:T(128)S(1)} copy-done((f32[80]{0:T(128)S(1)}, f32[80]{0:T(128)}, u32[]{:S(2)}) %copy-start.5) | copy-done | bytes 344
  12.8 0.0 copy-start.2
  12.8 0.0 copy-start.3
  12.8 3.1 %basis.1.basis_ref = bf16[256,4096]{1,0:T(8,128)(2,1)S(1)} custom-call(bf16[2560,128]{1,0:T(8,128)(2,1)S(1)} %bitcast.9, f32[1,80]{1,0:T(1,128)S(1)} %bitcast.13, f32[80,80]{1,0:T(8,128)S(1)} %copy-done.1), custom_call_target="tpu_custom_call" | custom-call | flops 262144000 | bytes 4194304 | tf_op jit(solution)/shard_map/basis/pallas_call | solution.py:326
  16.0 3.2 %all-to-all-done.refs_0_ = bf16[8,128,128]{2,1,0:T(8,128)(2,1)S(1)} async-done(((bf16[8,128,128]{2,1,0:T(8,128)(2,1)}), bf16[8,128,128]{2,1,0:T(8,128)(2,1)S(1)}, u32[]{:S(2)}, u32[]{:S(2)}) %all-to-all-start) | async-done | bytes 262176 | tf_op jit(solution)/shard_map/all_to_all | solution.py:324
  19.2 0.0 copy-done.4
  19.2 0.0 copy-done.8
  19.2 0.0 copy-done.7
  19.2 0.0 copy-done.6
  19.2 5.7 %value_and_allocate.1 = f32[32,1,128]{2,1,0:T(1,128)S(1)} custom-call(s32[1]{0:T(128)} %bitcast.me_ref, s32[8]{0:T(128)S(1)} %copy-done.6, s32[4]{0:T(128)S(1)} %copy-done.7, s32[4]{0:T(128)S(1)} %copy-done.8, f32[4,32]{1,0:T(4,128)S(1)} %copy-done.4, bf16[256,4096]{1,0:T(8,128)(2,1)S(1)} %basis.1.basis_ref, bf16[8,128,128]{2,1,0:T(8,128)(2,1)S(1)} %all-to-all-done.refs_0_), custom_call_target="tpu_custom_call" | custom-call | tf_op jit(solution)/shard_map/value_and_allocate/pallas_call | solution.py:346
  24.9 10.6 %all_to_all.10 = f32[32,1,128]{2,1,0:T(1,128)S(1)} all-to-all(f32[32,1,128]{2,1,0:T(1,128)S(1)} %value_and_allocate.1), channel_id=1, replica_groups=mesh['trade'=8,'path'=4] {'trade','path'}, dimensions={0} | all-to-all | bytes 32768 | tf_op jit(solution)/shard_map/all_to_all | solution.py:356
  35.5 0.0 copy-done.2
  35.5 0.0 copy-done.3
  35.5 0.8 %finish.1 = (f32[1,512]{1,0:T(1,128)}, f32[1,4]{1,0:T(1,128)}) custom-call(s32[1]{0:T(128)} %bitcast.me_ref, f32[8,512]{1,0:T(8,128)S(1)} %copy-done.2, f32[4,128]{1,0:T(4,128)S(1)} %bitcast.12, f32[32,128]{1,0:T(8,128)S(1)} %bitcast.10), custom_call_target="tpu_custom_call" | custom-call | tf_op jit(solution)/shard_map/finish/pallas_call | solution.py:358
Async XLA Ops:
  0.6 18.6 %copy-start.4 = (f32[4,32]{1,0:T(4,128)S(1)}, f32[4,32]{1,0:T(4,128)}, u32[]{:S(2)}) copy-start(f32[4,32]{1,0:T(4,128)} %weight_ref.1) | copy-start | bytes 1540
  0.6 18.6 %copy-start.8 = (s32[4]{0:T(128)S(1)}, s32[4]{0:T(128)}, u32[]{:S(2)}) copy-start(s32[4]{0:T(128)} %lag_ref.1) | copy-start | bytes 52
  0.7 18.6 %copy-start.7 = (s32[4]{0:T(128)S(1)}, s32[4]{0:T(128)}, u32[]{:S(2)}) copy-start(s32[4]{0:T(128)} %cpty_ref.1) | copy-start | bytes 52
  0.7 18.6 %copy-start.6 = (s32[8]{0:T(128)S(1)}, s32[8]{0:T(128)}, u32[]{:S(2)}) copy-start(s32[8]{0:T(128)} %agr_ref.1) | copy-start | bytes 100
  3.0 16.2 %all-to-all-start = ((bf16[8,128,128]{2,1,0:T(8,128)(2,1)}), bf16[8,128,128]{2,1,0:T(8,128)(2,1)S(1)}, u32[]{:S(2)}, u32[]{:S(2)}) async-start(bf16[8,128,128]{2,1,0:T(8,128)(2,1)} %get-tuple-element.7), calls=%async_computation | async-start | bytes 524288 | tf_op jit(solution)/shard_map/all_to_all | solution.py:324
  10.3 1.1 %copy-start = (bf16[80,32,128]{2,1,0:T(8,128)(2,1)S(1)}, bf16[80,32,128]{2,1,0:T(8,128)(2,1)}, u32[]{:S(2)}) copy-start(bf16[80,32,128]{2,1,0:T(8,128)(2,1)} %param.10) | copy-start | bytes 1966084
  11.4 0.8 %copy-start.1 = (f32[80,80]{1,0:T(8,128)S(1)}, f32[80,80]{1,0:T(8,128)}, u32[]{:S(2)}) copy-start(f32[80,80]{1,0:T(8,128)} %loading_hbm.1) | copy-start | bytes 76804
  12.2 0.7 %copy-start.5 = (f32[80]{0:T(128)S(1)}, f32[80]{0:T(128)}, u32[]{:S(2)}) copy-start(f32[80]{0:T(128)} %param.11) | copy-start | bytes 964
  12.8 22.7 %copy-start.2 = (f32[8,512]{1,0:T(8,128)S(1)}, f32[8,512]{1,0:T(8,128)}, u32[]{:S(2)}) copy-start(f32[8,512]{1,0:T(8,128)} %get-tuple-element.6.place_ref) | copy-start | bytes 49156
  12.8 22.7 %copy-start.3 = (f32[512]{0:T(512)S(1)}, f32[512]{0:T(512)}, u32[]{:S(2)}) copy-start(f32[512]{0:T(512)} %param.14) | copy-start | bytes 6148

commit v8 on v7

--- a/solution.py
+++ b/solution.py
@@ -67,7 +67,7 @@
         self.trades = owners * self.room
         self.dates = dates
         self.width = 512
-        self.step = 1024
+        self.step = 2048 if self.trades <= 1024 else 512
 
 
 def pack_kernel(plan, me_ref, sets_hbm, coef_hbm, notional_hbm, place_ref, out_ref, *refs):
@@ -198,18 +198,14 @@
     hot = lax.rem(row, AG_DEV) == agr
     netting = jnp.where(hot, jnp.where(row < AG_DEV, info[0:1], info[1:2]), 0.0).astype(BF16)
 
-    owed = []
     width = plan.step
-    chunks = dates * LANES // width
-    for c in range(chunks):
-        under = jnp.dot(
-            left, basis_ref[:, c * width : (c + 1) * width], preferred_element_type=F32
-        )
-        value = jnp.maximum(under, 0.0).astype(BF16)
-        val_ref[:, c * width : (c + 1) * width] = value
-        both = jnp.dot(netting, value, preferred_element_type=F32)
-        both = both + pltpu.roll(both, AG_DEV, 0)
-        owed += [both[:, LANES * j : LANES * (j + 1)] for j in range(width // LANES)]
+    for c in range(dates * LANES // width):
+        cols = slice(c * width, (c + 1) * width)
+        under = jnp.dot(left, basis_ref[:, cols], preferred_element_type=F32)
+        val_ref[:, cols] = jnp.maximum(under.astype(BF16), 0)
+    both = jnp.dot(netting, val_ref[...], preferred_element_type=F32)
+    both = both + pltpu.roll(both, AG_DEV, 0)
+    owed = [both[:, LANES * t : LANES * (t + 1)] for t in range(dates)]
 
     member = lax.rem(iota((SUBS, LANES), 0), AG_DEV)
     lag = jnp.zeros((SUBS, LANES), jnp.int32)
@@ -229,10 +225,10 @@
             before = jnp.where(lags[s - 1], owed[t - s], before)
         excess = owed[t] - before
         square = excess * excess + SMOOTH * SMOOTH
-        root = jnp.sqrt(square)
+        inverse = lax.rsqrt(square)
         due = weight[:, t : t + 1]
-        spent = spent + due * (0.5 * (excess + root))
-        slopes.append(due * (0.5 * (1.0 + excess / root)))
+        spent = spent + due * (0.5 * (excess + square * inverse))
+        slopes.append(due * (0.5 * (1.0 + excess * inverse)))
     grads = []
     for t in range(dates):
         after = zero
@@ -271,10 +267,9 @@
     count = lines.shape[0]
     paths = count // plan.owners
     hot = mask_bf16(iota((LANES, rows), 0) == rank)
-    found = jnp.zeros((count, rows), F32)
-    for piece in split_bf16(lines, 3):
-        found = found + jnp.dot(piece, hot, preferred_element_type=F32)
-    wanted = iota(found.shape, 0) // paths == key
+    pieces = jnp.concatenate(split_bf16(lines, 3), axis=0)
+    found = jnp.dot(pieces, hot, preferred_element_type=F32)
+    wanted = lax.rem(iota(found.shape, 0), count) // paths == key
     share = jnp.sum(jnp.where(wanted, found, 0.0), axis=0, keepdims=True)
     alloc_ref[...] = share * in_a_row(notional_ref[...])
     own = iota(lines.shape, 0) // paths == me

time: 36.7 us -> 36.4 us (level)
  no operation moved by 1% of the time
where the time goes in v8:
time: 36.4 us; the launch traced here: 36 us
  Pallas kernels  11.6 us (32%)
  blocking collectives  10.6 us (29%)
  starting transfers between devices  7.29 us (20%)
  waiting for transfers between devices  3.24 us (9%)
  local copies, waits for them, and re-layouts  2.54 us (7%)
  between operations  0.71 us (2%)
    all_to_all x1, blocking collectives, body(): lax.all_to_all(lines_out, ('trade', 'path'), split_axis=0, concat_axis=0,...  10.6 us
    all_to_all x1, starting transfers between devices, body(): lax.all_to_all(outgoing, 'trade', split_axis=0, concat_axis=0, tiled=True)  7.29 us
    pallas_call x1, Pallas kernels, body(): pl.pallas_call(functools.partial(main_kernel, plan, path_total), out_shap...  5.42 us
    all_to_all x1, waiting for transfers between devices, body(): lax.all_to_all(outgoing, 'trade', split_axis=0, concat_axis=0, tiled=True)  3.24 us
    pallas_call x1, Pallas kernels, body(): pl.pallas_call(functools.partial(basis_kernel, plan), out_shape=jax.Shape...  3.14 us
    unnamed x18, local copies, waits for them, and re-layouts  2.54 us
    pallas_call x1, Pallas kernels, body(): pl.pallas_call(functools.partial(pack_kernel, plan), out_shape=[jax.Shape...  2.31 us
    pallas_call x1, Pallas kernels, body(): pl.pallas_call(functools.partial(finish_kernel, plan), out_shape=[jax.Sha...  0.76 us
  transfers between devices with their start and end apart: 1, of which 1 were waited for; matrix products, arithmetic and copies ran while one was open for 0% of the time, Pallas kernels for 9%

profile of v8, /device:TPU:0, one launch (start us, length us, event | category | flops | bytes accessed | tf_op | source)
XLA Modules:
  0.0 36.0 jit_solution(5505071811441371010)
XLA Ops:
  0.6 0.0 copy-start.4
  0.6 0.0 copy-start.8
  0.7 0.0 copy-start.7
  0.7 0.0 copy-start.6
  0.7 2.3 %pack.1 = (f32[8,512]{1,0:T(8,128)}, bf16[8,128,128]{2,1,0:T(8,128)(2,1)}) custom-call(s32[1]{0:T(128)} %bitcast.me_ref, s32[32,128]{1,0:T(8,128)} %bitcast.15, bf16[160,512]{1,0:T(8,128)(2,1)} %bitcast.14, f32[4,128]{1,0:T(4,128)} %bitcast.11), custom_call_target="tpu_custom_call" | custom-call | tf_op jit(solution)/shard_map/pack/pallas_call | solution.py:303
  3.0 7.3 %all-to-all-start = ((bf16[8,128,128]{2,1,0:T(8,128)(2,1)}), bf16[8,128,128]{2,1,0:T(8,128)(2,1)S(1)}, u32[]{:S(2)}, u32[]{:S(2)}) async-start(bf16[8,128,128]{2,1,0:T(8,128)(2,1)} %get-tuple-element.7), calls=%async_computation | async-start | bytes 524288 | tf_op jit(solution)/shard_map/all_to_all | solution.py:319
  10.3 0.0 copy-start
  10.3 1.1 %copy-done = bf16[80,32,128]{2,1,0:T(8,128)(2,1)S(1)} copy-done((bf16[80,32,128]{2,1,0:T(8,128)(2,1)S(1)}, bf16[80,32,128]{2,1,0:T(8,128)(2,1)}, u32[]{:S(2)}) %copy-start) | copy-done | bytes 655384
  11.4 0.0 copy-start.1
  11.4 0.8 %copy-done.1 = f32[80,80]{1,0:T(8,128)S(1)} copy-done((f32[80,80]{1,0:T(8,128)S(1)}, f32[80,80]{1,0:T(8,128)}, u32[]{:S(2)}) %copy-start.1) | copy-done | bytes 25624
  12.2 0.0 copy-start.5
  12.2 0.7 %copy-done.5 = f32[80]{0:T(128)S(1)} copy-done((f32[80]{0:T(128)S(1)}, f32[80]{0:T(128)}, u32[]{:S(2)}) %copy-start.5) | copy-done | bytes 344
  12.8 0.0 copy-start.2
  12.8 0.0 copy-start.3
  12.8 3.1 %basis.1.basis_ref = bf16[256,4096]{1,0:T(8,128)(2,1)S(1)} custom-call(bf16[2560,128]{1,0:T(8,128)(2,1)S(1)} %bitcast.9, f32[1,80]{1,0:T(1,128)S(1)} %bitcast.13, f32[80,80]{1,0:T(8,128)S(1)} %copy-done.1), custom_call_target="tpu_custom_call" | custom-call | flops 262144000 | bytes 4194304 | tf_op jit(solution)/shard_map/basis/pallas_call | solution.py:321
  16.0 3.2 %all-to-all-done.refs_0_ = bf16[8,128,128]{2,1,0:T(8,128)(2,1)S(1)} async-done(((bf16[8,128,128]{2,1,0:T(8,128)(2,1)}), bf16[8,128,128]{2,1,0:T(8,128)(2,1)S(1)}, u32[]{:S(2)}, u32[]{:S(2)}) %all-to-all-start) | async-done | bytes 262176 | tf_op jit(solution)/shard_map/all_to_all | solution.py:319
  19.2 0.0 copy-done.4
  19.2 0.0 copy-done.8
  19.2 0.0 copy-done.7
  19.2 0.0 copy-done.6
  19.2 5.4 %value_and_allocate.1 = f32[32,1,128]{2,1,0:T(1,128)S(1)} custom-call(s32[1]{0:T(128)} %bitcast.me_ref, s32[8]{0:T(128)S(1)} %copy-done.6, s32[4]{0:T(128)S(1)} %copy-done.7, s32[4]{0:T(128)S(1)} %copy-done.8, f32[4,32]{1,0:T(4,128)S(1)} %copy-done.4, bf16[256,4096]{1,0:T(8,128)(2,1)S(1)} %basis.1.basis_ref, bf16[8,128,128]{2,1,0:T(8,128)(2,1)S(1)} %all-to-all-done.refs_0_), custom_call_target="tpu_custom_call" | custom-call | tf_op jit(solution)/shard_map/value_and_allocate/pallas_call | solution.py:341
  24.7 10.6 %all_to_all.10 = f32[32,1,128]{2,1,0:T(1,128)S(1)} all-to-all(f32[32,1,128]{2,1,0:T(1,128)S(1)} %value_and_allocate.1), channel_id=1, replica_groups=mesh['trade'=8,'path'=4] {'trade','path'}, dimensions={0} | all-to-all | bytes 32768 | tf_op jit(solution)/shard_map/all_to_all | solution.py:351
  35.2 0.0 copy-done.2
  35.2 0.0 copy-done.3
  35.2 0.8 %finish.1 = (f32[1,512]{1,0:T(1,128)}, f32[1,4]{1,0:T(1,128)}) custom-call(s32[1]{0:T(128)} %bitcast.me_ref, f32[8,512]{1,0:T(8,128)S(1)} %copy-done.2, f32[4,128]{1,0:T(4,128)S(1)} %bitcast.12, f32[32,128]{1,0:T(8,128)S(1)} %bitcast.10), custom_call_target="tpu_custom_call" | custom-call | tf_op jit(solution)/shard_map/finish/pallas_call | solution.py:353
Async XLA Ops:
  0.6 18.6 %copy-start.4 = (f32[4,32]{1,0:T(4,128)S(1)}, f32[4,32]{1,0:T(4,128)}, u32[]{:S(2)}) copy-start(f32[4,32]{1,0:T(4,128)} %weight_ref.1) | copy-start | bytes 1540
  0.6 18.6 %copy-start.8 = (s32[4]{0:T(128)S(1)}, s32[4]{0:T(128)}, u32[]{:S(2)}) copy-start(s32[4]{0:T(128)} %lag_ref.1) | copy-start | bytes 52
  0.7 18.6 %copy-start.7 = (s32[4]{0:T(128)S(1)}, s32[4]{0:T(128)}, u32[]{:S(2)}) copy-start(s32[4]{0:T(128)} %cpty_ref.1) | copy-start | bytes 52
  0.7 18.6 %copy-start.6 = (s32[8]{0:T(128)S(1)}, s32[8]{0:T(128)}, u32[]{:S(2)}) copy-start(s32[8]{0:T(128)} %agr_ref.1) | copy-start | bytes 100
  3.0 16.2 %all-to-all-start = ((bf16[8,128,128]{2,1,0:T(8,128)(2,1)}), bf16[8,128,128]{2,1,0:T(8,128)(2,1)S(1)}, u32[]{:S(2)}, u32[]{:S(2)}) async-start(bf16[8,128,128]{2,1,0:T(8,128)(2,1)} %get-tuple-element.7), calls=%async_computation | async-start | bytes 524288 | tf_op jit(solution)/shard_map/all_to_all | solution.py:319
  10.3 1.1 %copy-start = (bf16[80,32,128]{2,1,0:T(8,128)(2,1)S(1)}, bf16[80,32,128]{2,1,0:T(8,128)(2,1)}, u32[]{:S(2)}) copy-start(bf16[80,32,128]{2,1,0:T(8,128)(2,1)} %param.10) | copy-start | bytes 1966084
  11.4 0.8 %copy-start.1 = (f32[80,80]{1,0:T(8,128)S(1)}, f32[80,80]{1,0:T(8,128)}, u32[]{:S(2)}) copy-start(f32[80,80]{1,0:T(8,128)} %loading_hbm.1) | copy-start | bytes 76804
  12.2 0.7 %copy-start.5 = (f32[80]{0:T(128)S(1)}, f32[80]{0:T(128)}, u32[]{:S(2)}) copy-start(f32[80]{0:T(128)} %param.11) | copy-start | bytes 964
  12.8 22.4 %copy-start.2 = (f32[8,512]{1,0:T(8,128)S(1)}, f32[8,512]{1,0:T(8,128)}, u32[]{:S(2)}) copy-start(f32[8,512]{1,0:T(8,128)} %get-tuple-element.6.place_ref) | copy-start | bytes 49156
  12.8 22.4 %copy-start.3 = (f32[512]{0:T(512)S(1)}, f32[512]{0:T(512)}, u32[]{:S(2)}) copy-start(f32[512]{0:T(512)} %param.14) | copy-start | bytes 6148

commit v9 on v8

--- a/solution.py
+++ b/solution.py
@@ -315,6 +315,7 @@
             pltpu.SemaphoreType.DMA((3,)),
         ],
         name="pack",
+        cost_estimate=pl.CostEstimate(flops=1 << 32, bytes_accessed=1 << 19, transcendentals=0),
     )(me, ns_of_trade.reshape(owners * lines, LANES), coefficient.T, notional)
     incoming = lax.all_to_all(outgoing, "trade", split_axis=0, concat_axis=0, tiled=True)
 

time: 36.4 us -> 36.4 us (level)
  local copies, waits for them, and re-layouts: 2.54 us -> 0.05 us
  waiting for transfers between devices: 3.24 us -> 5.7 us
    unnamed x18, local copies, waits for them, and re-layouts: 2.54 us -> 0.05 us
    all_to_all x1, waiting for transfers between devices: 3.24 us -> 5.7 us  [body(): lax.all_to_all(outgoing, 'trade', split_axis=0, concat_axis=0, tiled=True)]
where the time goes in v9:
time: 36.4 us; the launch traced here: 36.2 us
  Pallas kernels  11.7 us (32%)
  blocking collectives  10.6 us (29%)
  starting transfers between devices  7.43 us (20%)
  waiting for transfers between devices  5.7 us (16%)
  between operations  0.76 us (2%)
    all_to_all x1, blocking collectives, body(): lax.all_to_all(lines_out, ('trade', 'path'), split_axis=0, concat_axis=0,...  10.6 us
    all_to_all x1, starting transfers between devices, body(): lax.all_to_all(outgoing, 'trade', split_axis=0, concat_axis=0, tiled=True)  7.43 us
    all_to_all x1, waiting for transfers between devices, body(): lax.all_to_all(outgoing, 'trade', split_axis=0, concat_axis=0, tiled=True)  5.7 us
    pallas_call x1, Pallas kernels, body(): pl.pallas_call(functools.partial(main_kernel, plan, path_total), out_shap...  5.39 us
    pallas_call x1, Pallas kernels, body(): pl.pallas_call(functools.partial(basis_kernel, plan), out_shape=jax.Shape...  3.16 us
    pallas_call x1, Pallas kernels, body(): pl.pallas_call(functools.partial(pack_kernel, plan), out_shape=[jax.Shape...  2.35 us
    pallas_call x1, Pallas kernels, body(): pl.pallas_call(functools.partial(finish_kernel, plan), out_shape=[jax.Sha...  0.76 us
  transfers between devices with their start and end apart: 1, of which 1 were waited for; matrix products, arithmetic and copies ran while one was open for 0% of the time, Pallas kernels for 9%

profile of v9, /device:TPU:0, one launch (start us, length us, event | category | flops | bytes accessed | tf_op | source)
XLA Modules:
  0.0 36.2 jit_solution(14688740397869373707)
XLA Ops:
  0.6 0.0 copy-start
  0.6 0.0 copy-start.1
  0.7 0.0 copy-start.5
  0.7 2.4 %pack.1 = (f32[8,512]{1,0:T(8,128)}, bf16[8,128,128]{2,1,0:T(8,128)(2,1)}) custom-call(s32[1]{0:T(128)} %bitcast.me_ref, s32[32,128]{1,0:T(8,128)} %bitcast.15, bf16[160,512]{1,0:T(8,128)(2,1)} %bitcast.14, f32[4,128]{1,0:T(4,128)} %bitcast.11), custom_call_target="tpu_custom_call" | custom-call | flops 4294967296 | bytes 524288 | tf_op jit(solution)/shard_map/pack/pallas_call | solution.py:303
  3.0 0.0 copy-start.3
  3.0 0.0 copy-start.6
  3.1 0.0 copy-start.7
  3.1 0.0 copy-start.8
  3.1 7.4 %all-to-all-start = ((bf16[8,128,128]{2,1,0:T(8,128)(2,1)}), bf16[8,128,128]{2,1,0:T(8,128)(2,1)S(1)}, u32[]{:S(2)}, u32[]{:S(2)}) async-start(bf16[8,128,128]{2,1,0:T(8,128)(2,1)} %get-tuple-element.7), calls=%async_computation | async-start | bytes 524288 | tf_op jit(solution)/shard_map/all_to_all | solution.py:320
  10.5 0.0 copy-done
  10.5 0.0 copy-done.1
  10.5 0.0 copy-done.5
  10.5 0.0 copy-start.2
  10.5 0.0 copy-start.4
  10.5 3.2 %basis.1.basis_ref = bf16[256,4096]{1,0:T(8,128)(2,1)S(1)} custom-call(bf16[2560,128]{1,0:T(8,128)(2,1)S(1)} %bitcast.9, f32[1,80]{1,0:T(1,128)S(1)} %bitcast.13, f32[80,80]{1,0:T(8,128)S(1)} %copy-done.1), custom_call_target="tpu_custom_call" | custom-call | flops 262144000 | bytes 4194304 | tf_op jit(solution)/shard_map/basis/pallas_call | solution.py:322
  13.7 5.7 %all-to-all-done.refs_0_ = bf16[8,128,128]{2,1,0:T(8,128)(2,1)S(1)} async-done(((bf16[8,128,128]{2,1,0:T(8,128)(2,1)}), bf16[8,128,128]{2,1,0:T(8,128)(2,1)S(1)}, u32[]{:S(2)}, u32[]{:S(2)}) %all-to-all-start) | async-done | bytes 262176 | tf_op jit(solution)/shard_map/all_to_all | solution.py:320
  19.4 0.0 copy-done.3
  19.4 0.0 copy-done.6
  19.4 0.0 copy-done.7
  19.4 0.0 copy-done.8
  19.4 5.4 %value_and_allocate.1 = f32[32,1,128]{2,1,0:T(1,128)S(1)} custom-call(s32[1]{0:T(128)} %bitcast.me_ref, s32[8]{0:T(128)S(1)} %copy-done.6, s32[4]{0:T(128)S(1)} %copy-done.7, s32[4]{0:T(128)S(1)} %copy-done.8, f32[4,32]{1,0:T(4,128)S(1)} %copy-done.3, bf16[256,4096]{1,0:T(8,128)(2,1)S(1)} %basis.1.basis_ref, bf16[8,128,128]{2,1,0:T(8,128)(2,1)S(1)} %all-to-all-done.refs_0_), custom_call_target="tpu_custom_call" | custom-call | tf_op jit(solution)/shard_map/value_and_allocate/pallas_call | solution.py:342
  24.8 10.6 %all_to_all.10 = f32[32,1,128]{2,1,0:T(1,128)S(1)} all-to-all(f32[32,1,128]{2,1,0:T(1,128)S(1)} %value_and_allocate.1), channel_id=1, replica_groups=mesh['trade'=8,'path'=4] {'trade','path'}, dimensions={0} | all-to-all | bytes 32768 | tf_op jit(solution)/shard_map/all_to_all | solution.py:352
  35.4 0.0 copy-done.2
  35.4 0.0 copy-done.4
  35.4 0.8 %finish.1 = (f32[1,512]{1,0:T(1,128)}, f32[1,4]{1,0:T(1,128)}) custom-call(s32[1]{0:T(128)} %bitcast.me_ref, f32[8,512]{1,0:T(8,128)S(1)} %copy-done.2, f32[4,128]{1,0:T(4,128)S(1)} %bitcast.12, f32[32,128]{1,0:T(8,128)S(1)} %bitcast.10), custom_call_target="tpu_custom_call" | custom-call | tf_op jit(solution)/shard_map/finish/pallas_call | solution.py:354
Async XLA Ops:
  0.6 9.9 %copy-start = (bf16[80,32,128]{2,1,0:T(8,128)(2,1)S(1)}, bf16[80,32,128]{2,1,0:T(8,128)(2,1)}, u32[]{:S(2)}) copy-start(bf16[80,32,128]{2,1,0:T(8,128)(2,1)} %param.10) | copy-start | bytes 1966084
  0.6 9.9 %copy-start.1 = (f32[80,80]{1,0:T(8,128)S(1)}, f32[80,80]{1,0:T(8,128)}, u32[]{:S(2)}) copy-start(f32[80,80]{1,0:T(8,128)} %loading_hbm.1) | copy-start | bytes 76804
  0.7 9.9 %copy-start.5 = (f32[80]{0:T(128)S(1)}, f32[80]{0:T(128)}, u32[]{:S(2)}) copy-start(f32[80]{0:T(128)} %param.11) | copy-start | bytes 964
  3.0 16.4 %copy-start.3 = (f32[4,32]{1,0:T(4,128)S(1)}, f32[4,32]{1,0:T(4,128)}, u32[]{:S(2)}) copy-start(f32[4,32]{1,0:T(4,128)} %weight_ref.1) | copy-start | bytes 1540
  3.0 16.4 %copy-start.6 = (s32[8]{0:T(128)S(1)}, s32[8]{0:T(128)}, u32[]{:S(2)}) copy-start(s32[8]{0:T(128)} %agr_ref.1) | copy-start | bytes 100
  3.1 16.4 %copy-start.7 = (s32[4]{0:T(128)S(1)}, s32[4]{0:T(128)}, u32[]{:S(2)}) copy-start(s32[4]{0:T(128)} %cpty_ref.1) | copy-start | bytes 52
  3.1 16.4 %copy-start.8 = (s32[4]{0:T(128)S(1)}, s32[4]{0:T(128)}, u32[]{:S(2)}) copy-start(s32[4]{0:T(128)} %lag_ref.1) | copy-start | bytes 52
  3.1 16.3 %all-to-all-start = ((bf16[8,128,128]{2,1,0:T(8,128)(2,1)}), bf16[8,128,128]{2,1,0:T(8,128)(2,1)S(1)}, u32[]{:S(2)}, u32[]{:S(2)}) async-start(bf16[8,128,128]{2,1,0:T(8,128)(2,1)} %get-tuple-element.7), calls=%async_computation | async-start | bytes 524288 | tf_op jit(solution)/shard_map/all_to_all | solution.py:320
  10.5 24.9 %copy-start.2 = (f32[8,512]{1,0:T(8,128)S(1)}, f32[8,512]{1,0:T(8,128)}, u32[]{:S(2)}) copy-start(f32[8,512]{1,0:T(8,128)} %get-tuple-element.6.place_ref) | copy-start | bytes 49156
  10.5 24.9 %copy-start.4 = (f32[512]{0:T(512)S(1)}, f32[512]{0:T(512)}, u32[]{:S(2)}) copy-start(f32[512]{0:T(512)} %param.14) | copy-start | bytes 6148

commit v10 on v9

--- a/solution.py
+++ b/solution.py
@@ -57,6 +57,8 @@
     def __init__(self, owners, rows, tenors, dates):
         most = 3 * rows // (2 * owners)
         self.owners = owners
+        self.halves = 2 if most % 96 == 0 else 1
+        most = most // self.halves
         self.groups = 3 if most % 48 == 0 else 1
         self.part = -(-most // (16 * self.groups)) * 16
         self.room = self.groups * self.part
@@ -64,13 +66,14 @@
         self.extra = 2 * tenors - LANES
         self.per_line = LANES // self.part
         self.lines = owners * self.part // LANES
-        self.trades = owners * self.room
+        self.slots = self.halves * self.room
+        self.trades = owners * self.slots
         self.dates = dates
         self.width = 512
         self.step = 2048 if self.trades <= 1024 else 512
 
 
-def pack_kernel(plan, me_ref, sets_hbm, coef_hbm, notional_hbm, place_ref, out_ref, *refs):
+def pack_kernel(plan, me_ref, half_ref, sets_hbm, coef_hbm, notional_hbm, place_ref, out_ref, *refs):
     sets_ref, coef_ref, notional_ref, sems = refs
     copies = fetch(
         [sets_hbm, notional_hbm, coef_hbm], [sets_ref, notional_ref, coef_ref], sems
@@ -95,7 +98,8 @@
     place_ref[...] = jnp.concatenate(
         [key.astype(F32), rank, jnp.zeros((SUBS - 2, rows), F32)], axis=0
     )
-    spot = key * room + rank.astype(jnp.int32)
+    mine = rank.astype(jnp.int32) - room * half_ref[0]
+    spot = jnp.where((mine >= 0) & (mine < room), key * room + mine, -1)
     chosen = mask_bf16(iota((owners * room, rows), 0) == spot)
     copies[1].wait()
     notional = in_a_row(notional_ref[...])
@@ -172,22 +176,22 @@
 
 
 def main_kernel(plan, path_total, me_ref, agr_ref, cpty_ref, lag_ref, weight_ref, basis_ref, *refs):
-    in_ref, out_ref, val_ref = refs
+    *in_refs, out_ref, val_ref = refs
     me = me_ref[0]
     part, room, dates = plan.part, plan.room, plan.dates
     cpty_dev = weight_ref.shape[0]
 
-    def rows_of(first):
-        return in_ref[:, first : first + part, :].reshape(plan.owners * part, LANES)
-
-    rest = rows_of(room)
     lane = iota((1, LANES), 1)
     left, info = [], []
-    for g in range(plan.groups):
-        keep = mask_bf16((lane >= plan.extra * g) & (lane < plan.extra * (g + 1)))
-        left.append(jnp.concatenate([rows_of(part * g), rest * keep], axis=1))
-        pick = mask_bf16(iota((SUBS, LANES), 1) == 3 * plan.extra + SUBS * g + iota((SUBS, LANES), 0))
-        info.append(lax.dot_general(pick, rest, BOTH_LANES, preferred_element_type=F32))
+    for in_ref in in_refs:
+        rest = in_ref[:, room:, :].reshape(plan.owners * part, LANES)
+        for g in range(plan.groups):
+            main = in_ref[:, part * g : part * (g + 1), :].reshape(plan.owners * part, LANES)
+            keep = mask_bf16((lane >= plan.extra * g) & (lane < plan.extra * (g + 1)))
+            left.append(jnp.concatenate([main, rest * keep], axis=1))
+            first = 3 * plan.extra + SUBS * g
+            pick = mask_bf16(iota((SUBS, LANES), 1) == first + iota((SUBS, LANES), 0))
+            info.append(lax.dot_general(pick, rest, BOTH_LANES, preferred_element_type=F32))
     left = jnp.concatenate(left, axis=0)
     info = jnp.concatenate(info, axis=1)
     local = info[2:3].astype(jnp.int32)
@@ -241,17 +245,18 @@
     )
     share = jnp.sum(jnp.where(hot & (row < AG_DEV), dots, 0.0), axis=0, keepdims=True)
     spent = jnp.sum(spent, axis=1, keepdims=True) * (1.0 / path_total)
-    mine = (lane - room == cpty) & (iota((SUBS, LANES), 0) < AG_DEV)
+    mine = (lane - plan.slots == cpty) & (iota((SUBS, LANES), 0) < AG_DEV)
     cva = jnp.sum(jnp.where(mine, spent, 0.0), axis=0, keepdims=True)
     block = lane // part
-    count = plan.groups * plan.lines
+    parts = plan.slots // part
+    count = parts * plan.lines
     lines = jnp.concatenate([share[:, LANES * k : LANES * (k + 1)] for k in range(count)], axis=0)
     moved = [lines if m == 0 else pltpu.roll(lines, part * m, 1) for m in range(plan.per_line)]
     paths = out_ref.shape[0] // plan.owners
     for k in range(plan.lines):
         for s in range(plan.per_line):
             line = cva
-            for g in range(plan.groups):
+            for g in range(parts):
                 n = g * plan.lines + k
                 line = jnp.where(block == g, moved[(g - s) % plan.per_line][n : n + 1], line)
             for p in range(paths):
@@ -266,15 +271,19 @@
     lines = in_ref[...]
     count = lines.shape[0]
     paths = count // plan.owners
-    hot = mask_bf16(iota((LANES, rows), 0) == rank)
     pieces = jnp.concatenate(split_bf16(lines, 3), axis=0)
-    found = jnp.dot(pieces, hot, preferred_element_type=F32)
+    half = lax.rem(lax.rem(iota((pieces.shape[0], rows), 0), paths), plan.halves)
+    found = jnp.zeros(half.shape, F32)
+    for h in range(plan.halves):
+        slot = lax.rem(rank + plan.room * h, plan.slots)
+        hot = mask_bf16(iota((LANES, rows), 0) == slot)
+        found = jnp.where(half == h, jnp.dot(pieces, hot, preferred_element_type=F32), found)
     wanted = lax.rem(iota(found.shape, 0), count) // paths == key
     share = jnp.sum(jnp.where(wanted, found, 0.0), axis=0, keepdims=True)
     alloc_ref[...] = share * in_a_row(notional_ref[...])
     own = iota(lines.shape, 0) // paths == me
     cva = jnp.sum(jnp.where(own, lines, 0.0), axis=0, keepdims=True)
-    cva_ref[...] = cva[:, plan.room : plan.room + cva_ref.shape[1]]
+    cva_ref[...] = cva[:, plan.slots : plan.slots + cva_ref.shape[1]]
 
 
 def body(
@@ -298,6 +307,7 @@
     plan = Plan(owners, rows, tenors, dates)
     cols = dates * path_dev
     me = lax.axis_index("trade").astype(jnp.int32).reshape(1)
+    half = lax.rem(lax.axis_index("path").astype(jnp.int32), plan.halves).reshape(1)
     notional = notional.reshape(lines, LANES)
 
     place, outgoing = pl.pallas_call(
@@ -306,7 +316,7 @@
             jax.ShapeDtypeStruct((SUBS, rows), F32),
             jax.ShapeDtypeStruct((owners, plan.height, LANES), BF16),
         ],
-        in_specs=[SMEM] + [HBM] * 3,
+        in_specs=[SMEM] * 2 + [HBM] * 3,
         out_specs=[VMEM, VMEM],
         scratch_shapes=[
             pltpu.VMEM((owners * lines, LANES), jnp.int32),
@@ -316,8 +326,11 @@
         ],
         name="pack",
         cost_estimate=pl.CostEstimate(flops=1 << 32, bytes_accessed=1 << 19, transcendentals=0),
-    )(me, ns_of_trade.reshape(owners * lines, LANES), coefficient.T, notional)
-    incoming = lax.all_to_all(outgoing, "trade", split_axis=0, concat_axis=0, tiled=True)
+    )(me, half, ns_of_trade.reshape(owners * lines, LANES), coefficient.T, notional)
+    incoming = [lax.all_to_all(outgoing, "trade", split_axis=0, concat_axis=0, tiled=True)]
+    if plan.halves == 2:
+        pairs = [(p, p ^ 1) for p in range(path_parts)]
+        incoming.append(lax.ppermute(incoming[0], "path", pairs))
 
     basis = pl.pallas_call(
         functools.partial(basis_kernel, plan),
@@ -342,12 +355,12 @@
     lines_out = pl.pallas_call(
         functools.partial(main_kernel, plan, path_total),
         out_shape=jax.ShapeDtypeStruct((owners * path_parts, 1, LANES), F32),
-        in_specs=[SMEM] * 4 + [VMEM] * 3,
+        in_specs=[SMEM] * 4 + [VMEM] * (2 + len(incoming)),
         out_specs=VMEM,
         scratch_shapes=[pltpu.VMEM((plan.trades, cols), BF16)],
         name="value_and_allocate",
         compiler_params=pltpu.CompilerParams(vmem_limit_bytes=need),
-    )(me, agr_of_ns, cpty_of_agr, margin_lag, default_weight, basis, incoming)
+    )(me, agr_of_ns, cpty_of_agr, margin_lag, default_weight, basis, *incoming)
 
     lines_in = lax.all_to_all(lines_out, ("trade", "path"), split_axis=0, concat_axis=0, tiled=True)
     lines_in = lines_in.reshape(owners * path_parts, LANES)

time: 36.4 us -> 36.9 us (1.014)
  blocking collectives: 10.6 us -> 24.2 us
  starting transfers between devices: 7.43 us -> 0.01 us
  waiting for transfers between devices: 5.7 us -> 0.01 us
    all_to_all x0 -> x1, blocking collectives: none -> 14.8 us  [body(): lax.all_to_all(outgoing, 'trade', split_axis=0, concat_axis=0, tiled=True)]
    all_to_all x1 -> x0, starting transfers between devices: 7.43 us -> none  [body(): lax.all_to_all(outgoing, 'trade', split_axis=0, concat_axis=0, tiled=True)]
    all_to_all x1 -> x0, waiting for transfers between devices: 5.7 us -> none  [body(): lax.all_to_all(outgoing, 'trade', split_axis=0, concat_axis=0, tiled=True)]
    all_to_all x1, blocking collectives: 10.6 us -> 9.44 us  [body(): lax.all_to_all(lines_out, ('trade', 'path'), split_axis=0, concat_axis=0,...]
  transfers between devices with their start and end apart: 1 -> 1, of which waited for: 1 -> 0; matrix products, arithmetic and copies ran while one was open for 0% -> 0% of each run, Pallas kernels for 9% -> 9%
where the time goes in v10:
time: 36.9 us; the launch traced here: 36.6 us
  blocking collectives  24.2 us (66%)
  Pallas kernels  11.5 us (31%)
  between operations  0.79 us (2%)
    all_to_all x1, blocking collectives, body(): lax.all_to_all(outgoing, 'trade', split_axis=0, concat_axis=0, tiled=True)  14.8 us
    all_to_all x1, blocking collectives, body(): lax.all_to_all(lines_out, ('trade', 'path'), split_axis=0, concat_axis=0,...  9.44 us
    pallas_call x1, Pallas kernels, body(): pl.pallas_call(functools.partial(main_kernel, plan, path_total), out_shap...  5.47 us
    pallas_call x1, Pallas kernels, body(): pl.pallas_call(functools.partial(basis_kernel, plan), out_shape=jax.Shape...  3.16 us
    pallas_call x1, Pallas kernels, body(): pl.pallas_call(functools.partial(pack_kernel, plan), out_shape=[jax.Shape...  2.09 us
    pallas_call x1, Pallas kernels, body(): pl.pallas_call(functools.partial(finish_kernel, plan), out_shape=[jax.Sha...  0.81 us
  transfers between devices with their start and end apart: 1, of which 0 were waited for; matrix products, arithmetic and copies ran while one was open for 0% of the time, Pallas kernels for 9%

profile of v10, /device:TPU:0, one launch (start us, length us, event | category | flops | bytes accessed | tf_op | source)
XLA Modules:
  0.0 36.6 jit_solution(7417931631683930121)
XLA Ops:
  0.6 0.0 copy-start
  0.6 0.0 copy-start.1
  0.7 0.0 copy-start.5
  0.7 2.1 %pack.1 = (f32[8,512]{1,0:T(8,128)}, bf16[8,64,128]{2,1,0:T(8,128)(2,1)}) custom-call(s32[1]{0:T(128)} %bitcast.me_ref, s32[1]{0:T(128)} %bitcast.1.half_ref, s32[32,128]{1,0:T(8,128)} %bitcast.16, bf16[160,512]{1,0:T(8,128)(2,1)} %bitcast.15, f32[4,128]{1,0:T(4,128)} %bitcast.12), custom_call_target="tpu_custom_call" | custom-call | flops 4294967296 | bytes 524288 | tf_op jit(solution)/shard_map/pack/pallas_call | solution.py:313
  2.8 0.0 copy-start.3
  2.8 0.0 copy-start.6
  2.8 0.0 copy-start.7
  2.8 0.0 copy-start.8
  2.8 14.8 %all_to_all.10.refs_0_ = bf16[8,64,128]{2,1,0:T(8,128)(2,1)S(1)} all-to-all(bf16[8,64,128]{2,1,0:T(8,128)(2,1)} %get-tuple-element.7), channel_id=1, replica_groups=mesh['trade'=8,'path'=4] {'trade'}, dimensions={0} | all-to-all | bytes 262144 | tf_op jit(solution)/shard_map/all_to_all | solution.py:330
  17.6 0.0 collective-permute-start
  17.6 0.0 copy-done
  17.6 0.0 copy-done.1
  17.6 0.0 copy-done.5
  17.6 0.0 copy-start.2
  17.6 0.0 copy-start.4
  17.6 3.2 %basis.1.basis_ref = bf16[256,4096]{1,0:T(8,128)(2,1)S(1)} custom-call(bf16[2560,128]{1,0:T(8,128)(2,1)S(1)} %bitcast.10, f32[1,80]{1,0:T(1,128)S(1)} %bitcast.14, f32[80,80]{1,0:T(8,128)S(1)} %copy-done.1), custom_call_target="tpu_custom_call" | custom-call | flops 262144000 | bytes 4194304 | tf_op jit(solution)/shard_map/basis/pallas_call | solution.py:335
  20.8 0.0 collective-permute-done.refs_1_
  20.8 0.0 copy-done.3
  20.8 0.0 copy-done.6
  20.8 0.0 copy-done.7
  20.8 0.0 copy-done.8
  20.8 5.5 %value_and_allocate.1 = f32[32,1,128]{2,1,0:T(1,128)S(1)} custom-call(s32[1]{0:T(128)} %bitcast.me_ref, s32[8]{0:T(128)S(1)} %copy-done.6, s32[4]{0:T(128)S(1)} %copy-done.7, s32[4]{0:T(128)S(1)} %copy-done.8, f32[4,32]{1,0:T(4,128)S(1)} %copy-done.3, bf16[256,4096]{1,0:T(8,128)(2,1)S(1)} %basis.1.basis_ref, bf16[8,64,128]{2,1,0:T(8,128)(2,1)S(1)} %all_to_all.10.refs_0_, ...), custom_call_target="tpu_custom_call" | custom-call | tf_op jit(solution)/shard_map/value_and_allocate/pallas_call | solution.py:355
  26.3 9.4 %all_to_all.11 = f32[32,1,128]{2,1,0:T(1,128)S(1)} all-to-all(f32[32,1,128]{2,1,0:T(1,128)S(1)} %value_and_allocate.1), channel_id=1, replica_groups=mesh['trade'=8,'path'=4] {'trade','path'}, dimensions={0} | all-to-all | bytes 32768 | tf_op jit(solution)/shard_map/all_to_all | solution.py:365
  35.8 0.0 copy-done.2
  35.8 0.0 copy-done.4
  35.8 0.8 %finish.1 = (f32[1,512]{1,0:T(1,128)}, f32[1,4]{1,0:T(1,128)}) custom-call(s32[1]{0:T(128)} %bitcast.me_ref, f32[8,512]{1,0:T(8,128)S(1)} %copy-done.2, f32[4,128]{1,0:T(4,128)S(1)} %bitcast.13, f32[32,128]{1,0:T(8,128)S(1)} %bitcast.11), custom_call_target="tpu_custom_call" | custom-call | tf_op jit(solution)/shard_map/finish/pallas_call | solution.py:367
Async XLA Ops:
  0.6 16.9 %copy-start = (bf16[80,32,128]{2,1,0:T(8,128)(2,1)S(1)}, bf16[80,32,128]{2,1,0:T(8,128)(2,1)}, u32[]{:S(2)}) copy-start(bf16[80,32,128]{2,1,0:T(8,128)(2,1)} %param.10) | copy-start | bytes 1966084
  0.6 16.9 %copy-start.1 = (f32[80,80]{1,0:T(8,128)S(1)}, f32[80,80]{1,0:T(8,128)}, u32[]{:S(2)}) copy-start(f32[80,80]{1,0:T(8,128)} %loading_hbm.1) | copy-start | bytes 76804
  0.7 16.9 %copy-start.5 = (f32[80]{0:T(128)S(1)}, f32[80]{0:T(128)}, u32[]{:S(2)}) copy-start(f32[80]{0:T(128)} %param.11) | copy-start | bytes 964
  2.8 18.0 %copy-start.3 = (f32[4,32]{1,0:T(4,128)S(1)}, f32[4,32]{1,0:T(4,128)}, u32[]{:S(2)}) copy-start(f32[4,32]{1,0:T(4,128)} %weight_ref.1) | copy-start | bytes 1540
  2.8 18.0 %copy-start.6 = (s32[8]{0:T(128)S(1)}, s32[8]{0:T(128)}, u32[]{:S(2)}) copy-start(s32[8]{0:T(128)} %agr_ref.1) | copy-start | bytes 100
  2.8 18.0 %copy-start.7 = (s32[4]{0:T(128)S(1)}, s32[4]{0:T(128)}, u32[]{:S(2)}) copy-start(s32[4]{0:T(128)} %cpty_ref.1) | copy-start | bytes 52
  2.8 18.0 %copy-start.8 = (s32[4]{0:T(128)S(1)}, s32[4]{0:T(128)}, u32[]{:S(2)}) copy-start(s32[4]{0:T(128)} %lag_ref.1) | copy-start | bytes 52
  17.6 3.2 %collective-permute-start = (bf16[8,64,128]{2,1,0:T(8,128)(2,1)S(1)}, bf16[8,64,128]{2,1,0:T(8,128)(2,1)S(1)}, u32[]{:S(2)}, u32[]{:S(2)}) collective-permute-start(bf16[8,64,128]{2,1,0:T(8,128)(2,1)S(1)} %all_to_all.10.refs_0_), channel_id=1, source_target_pairs={{0,1},{1,0},{2,3},{3,2},{4,5},{5,4},{6,7},{7,6},{8,9},{9,8},{10,11... | collective-permute-start | bytes 393224 | tf_op jit(solution)/shard_map/ppermute | solution.py:333
  17.6 18.2 %copy-start.2 = (f32[8,512]{1,0:T(8,128)S(1)}, f32[8,512]{1,0:T(8,128)}, u32[]{:S(2)}) copy-start(f32[8,512]{1,0:T(8,128)} %get-tuple-element.6.place_ref) | copy-start | bytes 49156
  17.6 18.2 %copy-start.4 = (f32[512]{0:T(512)S(1)}, f32[512]{0:T(512)}, u32[]{:S(2)}) copy-start(f32[512]{0:T(512)} %param.14) | copy-start | bytes 6148

commit v11 on v10

--- a/solution.py
+++ b/solution.py
@@ -328,10 +328,6 @@
         cost_estimate=pl.CostEstimate(flops=1 << 32, bytes_accessed=1 << 19, transcendentals=0),
     )(me, half, ns_of_trade.reshape(owners * lines, LANES), coefficient.T, notional)
     incoming = [lax.all_to_all(outgoing, "trade", split_axis=0, concat_axis=0, tiled=True)]
-    if plan.halves == 2:
-        pairs = [(p, p ^ 1) for p in range(path_parts)]
-        incoming.append(lax.ppermute(incoming[0], "path", pairs))
-
     basis = pl.pallas_call(
         functools.partial(basis_kernel, plan),
         out_shape=jax.ShapeDtypeStruct((2 * LANES, cols), BF16),
@@ -351,6 +347,11 @@
         ),
     )(shocks.reshape(tenors * dates, path_dev), forward_start.reshape(1, tenors), loading)
 
+    if plan.halves == 2:
+        incoming[0], basis = lax.optimization_barrier((incoming[0], basis))
+        pairs = [(p, p ^ 1) for p in range(path_parts)]
+        incoming.append(lax.ppermute(incoming[0], "path", pairs))
+
     need = 2 * plan.trades * cols + 8 * plan.trades * plan.step + (8 << 20)
     lines_out = pl.pallas_call(
         functools.partial(main_kernel, plan, path_total),

time: 36.9 us -> 34.9 us (0.946)
  blocking collectives: 24.2 us -> 9.34 us
  starting transfers between devices: 0.01 us -> 7.42 us
  waiting for transfers between devices: 0.01 us -> 5.47 us
    all_to_all x1 -> x0, blocking collectives: 14.8 us -> none  [body(): lax.all_to_all(outgoing, 'trade', split_axis=0, concat_axis=0, tiled=True)]
    all_to_all x0 -> x1, starting transfers between devices: none -> 7.42 us  [body(): lax.all_to_all(outgoing, 'trade', split_axis=0, concat_axis=0, tiled=True)]
    all_to_all x0 -> x1, waiting for transfers between devices: none -> 4.13 us  [body(): lax.all_to_all(outgoing, 'trade', split_axis=0, concat_axis=0, tiled=True)]
    ppermute x1, waiting for transfers between devices: 0.01 us -> 1.35 us  [body(): incoming.append(lax.ppermute(incoming[0], 'path', pairs))]
  transfers between devices with their start and end apart: 1 -> 2, of which waited for: 0 -> 2; matrix products, arithmetic and copies ran while one was open for 0% -> 0% of each run, Pallas kernels for 9% -> 9%
where the time goes in v11:
time: 34.9 us; the launch traced here: 34.6 us
  Pallas kernels  11.5 us (33%)
  blocking collectives  9.34 us (27%)
  starting transfers between devices  7.42 us (21%)
  waiting for transfers between devices  5.47 us (16%)
  between operations  0.77 us (2%)
    all_to_all x1, blocking collectives, body(): lax.all_to_all(lines_out, ('trade', 'path'), split_axis=0, concat_axis=0,...  9.34 us
    all_to_all x1, starting transfers between devices, body(): lax.all_to_all(outgoing, 'trade', split_axis=0, concat_axis=0, tiled=True)  7.42 us
    pallas_call x1, Pallas kernels, body(): pl.pallas_call(functools.partial(main_kernel, plan, path_total), out_shap...  5.47 us
    all_to_all x1, waiting for transfers between devices, body(): lax.all_to_all(outgoing, 'trade', split_axis=0, concat_axis=0, tiled=True)  4.13 us
    pallas_call x1, Pallas kernels, body(): pl.pallas_call(functools.partial(basis_kernel, plan), out_shape=jax.Shape...  3.16 us
    pallas_call x1, Pallas kernels, body(): pl.pallas_call(functools.partial(pack_kernel, plan), out_shape=[jax.Shape...  2.1 us
    ppermute x1, waiting for transfers between devices, body(): incoming.append(lax.ppermute(incoming[0], 'path', pairs))  1.35 us
    pallas_call x1, Pallas kernels, body(): pl.pallas_call(functools.partial(finish_kernel, plan), out_shape=[jax.Sha...  0.81 us
  transfers between devices with their start and end apart: 2, of which 2 were waited for; matrix products, arithmetic and copies ran while one was open for 0% of the time, Pallas kernels for 9%

profile of v11, /device:TPU:0, one launch (start us, length us, event | category | flops | bytes accessed | tf_op | source)
XLA Modules:
  0.0 34.6 jit_solution(7369481804466766665)
XLA Ops:
  0.6 0.0 copy-start
  0.6 0.0 copy-start.1
  0.7 0.0 copy-start.5
  0.7 2.1 %pack.1 = (f32[8,512]{1,0:T(8,128)}, bf16[8,64,128]{2,1,0:T(8,128)(2,1)}) custom-call(s32[1]{0:T(128)} %bitcast.me_ref, s32[1]{0:T(128)} %bitcast.1.half_ref, s32[32,128]{1,0:T(8,128)} %bitcast.16, bf16[160,512]{1,0:T(8,128)(2,1)} %bitcast.15, f32[4,128]{1,0:T(4,128)} %bitcast.12), custom_call_target="tpu_custom_call" | custom-call | flops 4294967296 | bytes 524288 | tf_op jit(solution)/shard_map/pack/pallas_call | solution.py:313
  2.8 0.0 copy-start.3
  2.8 0.0 copy-start.6
  2.8 0.0 copy-start.7
  2.8 0.0 copy-start.8
  2.8 7.4 %all-to-all-start = ((bf16[8,64,128]{2,1,0:T(8,128)(2,1)}), bf16[8,64,128]{2,1,0:T(8,128)(2,1)S(1)}, u32[]{:S(2)}, u32[]{:S(2)}) async-start(bf16[8,64,128]{2,1,0:T(8,128)(2,1)} %get-tuple-element.9), calls=%async_computation | async-start | bytes 262144 | tf_op jit(solution)/shard_map/all_to_all | solution.py:330
  10.2 0.0 copy-done
  10.2 0.0 copy-done.1
  10.3 0.0 copy-done.5
  10.3 0.0 copy-start.2
  10.3 0.0 copy-start.4
  10.3 3.2 %basis.1.basis_ref = bf16[256,4096]{1,0:T(8,128)(2,1)S(1)} custom-call(bf16[2560,128]{1,0:T(8,128)(2,1)S(1)} %bitcast.10, f32[1,80]{1,0:T(1,128)S(1)} %bitcast.14, f32[80,80]{1,0:T(8,128)S(1)} %copy-done.1), custom_call_target="tpu_custom_call" | custom-call | flops 262144000 | bytes 4194304 | tf_op jit(solution)/shard_map/basis/pallas_call | solution.py:331
  13.5 4.1 %all-to-all-done.refs_0_ = bf16[8,64,128]{2,1,0:T(8,128)(2,1)S(1)} async-done(((bf16[8,64,128]{2,1,0:T(8,128)(2,1)}), bf16[8,64,128]{2,1,0:T(8,128)(2,1)S(1)}, u32[]{:S(2)}, u32[]{:S(2)}) %all-to-all-start) | async-done | bytes 131104 | tf_op jit(solution)/shard_map/all_to_all | solution.py:330
  17.6 0.0 collective-permute-start
  17.6 1.3 %collective-permute-done.refs_1_ = bf16[8,64,128]{2,1,0:T(8,128)(2,1)S(1)} collective-permute-done((bf16[8,64,128]{2,1,0:T(8,128)(2,1)S(1)}, bf16[8,64,128]{2,1,0:T(8,128)(2,1)S(1)}, u32[]{:S(2)}, u32[]{:S(2)}) %collective-permute-start) | collective-permute-done | bytes 131104 | tf_op jit(solution)/shard_map/ppermute | solution.py:353
  18.9 0.0 copy-done.3
  18.9 0.0 copy-done.6
  18.9 0.0 copy-done.7
  18.9 0.0 copy-done.8
  19.0 5.5 %value_and_allocate.1 = f32[32,1,128]{2,1,0:T(1,128)S(1)} custom-call(s32[1]{0:T(128)} %bitcast.me_ref, s32[8]{0:T(128)S(1)} %copy-done.6, s32[4]{0:T(128)S(1)} %copy-done.7, s32[4]{0:T(128)S(1)} %copy-done.8, f32[4,32]{1,0:T(4,128)S(1)} %copy-done.3, bf16[256,4096]{1,0:T(8,128)(2,1)S(1)} %basis.1.basis_ref, bf16[8,64,128]{2,1,0:T(8,128)(2,1)S(1)} %all-to-all-done.refs_0_, ...), custom_call_target="tpu_custom_call" | custom-call | tf_op jit(solution)/shard_map/value_and_allocate/pallas_call | solution.py:356
  24.4 9.3 %all_to_all.10 = f32[32,1,128]{2,1,0:T(1,128)S(1)} all-to-all(f32[32,1,128]{2,1,0:T(1,128)S(1)} %value_and_allocate.1), channel_id=1, replica_groups=mesh['trade'=8,'path'=4] {'trade','path'}, dimensions={0} | all-to-all | bytes 32768 | tf_op jit(solution)/shard_map/all_to_all | solution.py:366
  33.8 0.0 copy-done.2
  33.8 0.0 copy-done.4
  33.8 0.8 %finish.1 = (f32[1,512]{1,0:T(1,128)}, f32[1,4]{1,0:T(1,128)}) custom-call(s32[1]{0:T(128)} %bitcast.me_ref, f32[8,512]{1,0:T(8,128)S(1)} %copy-done.2, f32[4,128]{1,0:T(4,128)S(1)} %bitcast.13, f32[32,128]{1,0:T(8,128)S(1)} %bitcast.11), custom_call_target="tpu_custom_call" | custom-call | tf_op jit(solution)/shard_map/finish/pallas_call | solution.py:368
Async XLA Ops:
  0.6 9.6 %copy-start = (bf16[80,32,128]{2,1,0:T(8,128)(2,1)S(1)}, bf16[80,32,128]{2,1,0:T(8,128)(2,1)}, u32[]{:S(2)}) copy-start(bf16[80,32,128]{2,1,0:T(8,128)(2,1)} %param.10) | copy-start | bytes 1966084
  0.6 9.6 %copy-start.1 = (f32[80,80]{1,0:T(8,128)S(1)}, f32[80,80]{1,0:T(8,128)}, u32[]{:S(2)}) copy-start(f32[80,80]{1,0:T(8,128)} %loading_hbm.1) | copy-start | bytes 76804
  0.7 9.6 %copy-start.5 = (f32[80]{0:T(128)S(1)}, f32[80]{0:T(128)}, u32[]{:S(2)}) copy-start(f32[80]{0:T(128)} %param.11) | copy-start | bytes 964
  2.8 16.2 %copy-start.3 = (f32[4,32]{1,0:T(4,128)S(1)}, f32[4,32]{1,0:T(4,128)}, u32[]{:S(2)}) copy-start(f32[4,32]{1,0:T(4,128)} %weight_ref.1) | copy-start | bytes 1540
  2.8 16.2 %copy-start.6 = (s32[8]{0:T(128)S(1)}, s32[8]{0:T(128)}, u32[]{:S(2)}) copy-start(s32[8]{0:T(128)} %agr_ref.1) | copy-start | bytes 100
  2.8 16.1 %copy-start.7 = (s32[4]{0:T(128)S(1)}, s32[4]{0:T(128)}, u32[]{:S(2)}) copy-start(s32[4]{0:T(128)} %cpty_ref.1) | copy-start | bytes 52
  2.8 16.1 %copy-start.8 = (s32[4]{0:T(128)S(1)}, s32[4]{0:T(128)}, u32[]{:S(2)}) copy-start(s32[4]{0:T(128)} %lag_ref.1) | copy-start | bytes 52
  2.8 14.8 %all-to-all-start = ((bf16[8,64,128]{2,1,0:T(8,128)(2,1)}), bf16[8,64,128]{2,1,0:T(8,128)(2,1)S(1)}, u32[]{:S(2)}, u32[]{:S(2)}) async-start(bf16[8,64,128]{2,1,0:T(8,128)(2,1)} %get-tuple-element.9), calls=%async_computation | async-start | bytes 262144 | tf_op jit(solution)/shard_map/all_to_all | solution.py:330
  10.3 23.5 %copy-start.2 = (f32[8,512]{1,0:T(8,128)S(1)}, f32[8,512]{1,0:T(8,128)}, u32[]{:S(2)}) copy-start(f32[8,512]{1,0:T(8,128)} %get-tuple-element.8.place_ref) | copy-start | bytes 49156
  10.3 23.5 %copy-start.4 = (f32[512]{0:T(512)S(1)}, f32[512]{0:T(512)}, u32[]{:S(2)}) copy-start(f32[512]{0:T(512)} %param.14) | copy-start | bytes 6148
  17.6 1.3 %collective-permute-start = (bf16[8,64,128]{2,1,0:T(8,128)(2,1)S(1)}, bf16[8,64,128]{2,1,0:T(8,128)(2,1)S(1)}, u32[]{:S(2)}, u32[]{:S(2)}) collective-permute-start(bf16[8,64,128]{2,1,0:T(8,128)(2,1)S(1)} %all-to-all-done.refs_0_), channel_id=1, source_target_pairs={{0,1},{1,0},{2,3},{3,2},{4,5},{5,4},{6,7},{7,6},{8,9},{9,8},{10,11... | collective-permute-start | bytes 393224 | tf_op jit(solution)/shard_map/ppermute | solution.py:353

commit v12 on v11

--- a/solution.py
+++ b/solution.py
@@ -175,24 +175,47 @@
         out_ref[used:, cols] = jnp.zeros((2 * LANES - used, plan.width), BF16)
 
 
+def left_side(plan, in_ref):
+    part, extra = plan.part, plan.extra
+    rest = in_ref[:, plan.room :, :].reshape(plan.owners * part, LANES)
+    lane = iota((1, LANES), 1)
+    left = []
+    for g in range(plan.groups):
+        main = in_ref[:, part * g : part * (g + 1), :].reshape(plan.owners * part, LANES)
+        keep = mask_bf16((lane >= extra * g) & (lane < extra * (g + 1)))
+        left.append(jnp.concatenate([main, rest * keep], axis=1))
+    return jnp.concatenate(left, axis=0), rest
+
+
+def price(plan, left, basis_ref, val_ref):
+    width = plan.step
+    for c in range(basis_ref.shape[1] // width):
+        cols = slice(c * width, (c + 1) * width)
+        under = jnp.dot(left, basis_ref[:, cols], preferred_element_type=F32)
+        val_ref[:, cols] = jnp.maximum(under.astype(BF16), 0)
+
+
+def price_kernel(plan, basis_ref, in_ref, val_ref):
+    price(plan, left_side(plan, in_ref)[0], basis_ref, val_ref)
+
+
 def main_kernel(plan, path_total, me_ref, agr_ref, cpty_ref, lag_ref, weight_ref, basis_ref, *refs):
     *in_refs, out_ref, val_ref = refs
+    val_refs = [val_ref]
+    if plan.halves == 2:
+        val_refs = [in_refs.pop(), val_ref]
     me = me_ref[0]
     part, room, dates = plan.part, plan.room, plan.dates
     cpty_dev = weight_ref.shape[0]
 
     lane = iota((1, LANES), 1)
-    left, info = [], []
+    info = []
     for in_ref in in_refs:
-        rest = in_ref[:, room:, :].reshape(plan.owners * part, LANES)
+        left, rest = left_side(plan, in_ref)
         for g in range(plan.groups):
-            main = in_ref[:, part * g : part * (g + 1), :].reshape(plan.owners * part, LANES)
-            keep = mask_bf16((lane >= plan.extra * g) & (lane < plan.extra * (g + 1)))
-            left.append(jnp.concatenate([main, rest * keep], axis=1))
             first = 3 * plan.extra + SUBS * g
             pick = mask_bf16(iota((SUBS, LANES), 1) == first + iota((SUBS, LANES), 0))
             info.append(lax.dot_general(pick, rest, BOTH_LANES, preferred_element_type=F32))
-    left = jnp.concatenate(left, axis=0)
     info = jnp.concatenate(info, axis=1)
     local = info[2:3].astype(jnp.int32)
     agr = jnp.zeros_like(local)
@@ -202,12 +225,13 @@
     hot = lax.rem(row, AG_DEV) == agr
     netting = jnp.where(hot, jnp.where(row < AG_DEV, info[0:1], info[1:2]), 0.0).astype(BF16)
 
-    width = plan.step
-    for c in range(dates * LANES // width):
-        cols = slice(c * width, (c + 1) * width)
-        under = jnp.dot(left, basis_ref[:, cols], preferred_element_type=F32)
-        val_ref[:, cols] = jnp.maximum(under.astype(BF16), 0)
-    both = jnp.dot(netting, val_ref[...], preferred_element_type=F32)
+    price(plan, left, basis_ref, val_ref)
+    size = val_ref.shape[0]
+    both = jnp.zeros((SUBS, val_ref.shape[1]), F32)
+    for h, values in enumerate(val_refs):
+        both = both + jnp.dot(
+            netting[:, size * h : size * (h + 1)], values[...], preferred_element_type=F32
+        )
     both = both + pltpu.roll(both, AG_DEV, 0)
     owed = [both[:, LANES * t : LANES * (t + 1)] for t in range(dates)]
 
@@ -240,9 +264,12 @@
             after = jnp.where(lags[s - 1], slopes[t + s], after)
         grads.append(((slopes[t] - after) * (1.0 / path_total)).astype(BF16))
 
-    dots = lax.dot_general(
-        jnp.concatenate(grads, axis=1), val_ref[...], BOTH_LANES, preferred_element_type=F32
-    )
+    grads = jnp.concatenate(grads, axis=1)
+    dots = [
+        lax.dot_general(grads, values[...], BOTH_LANES, preferred_element_type=F32)
+        for values in val_refs
+    ]
+    dots = jnp.concatenate(dots, axis=1)
     share = jnp.sum(jnp.where(hot & (row < AG_DEV), dots, 0.0), axis=0, keepdims=True)
     spent = jnp.sum(spent, axis=1, keepdims=True) * (1.0 / path_total)
     mine = (lane - plan.slots == cpty) & (iota((SUBS, LANES), 0) < AG_DEV)
@@ -347,10 +374,24 @@
         ),
     )(shocks.reshape(tenors * dates, path_dev), forward_start.reshape(1, tenors), loading)
 
+    half_trades = plan.trades // plan.halves
     if plan.halves == 2:
         incoming[0], basis = lax.optimization_barrier((incoming[0], basis))
         pairs = [(p, p ^ 1) for p in range(path_parts)]
         incoming.append(lax.ppermute(incoming[0], "path", pairs))
+        incoming.append(
+            pl.pallas_call(
+                functools.partial(price_kernel, plan),
+                out_shape=jax.ShapeDtypeStruct((half_trades, cols), BF16),
+                in_specs=[VMEM] * 2,
+                out_specs=VMEM,
+                name="price_own_half",
+                compiler_params=pltpu.CompilerParams(vmem_limit_bytes=24 << 20),
+                cost_estimate=pl.CostEstimate(
+                    flops=4 * half_trades * LANES * cols, bytes_accessed=6 << 20, transcendentals=0
+                ),
+            )(basis, incoming[0])
+        )
 
     need = 2 * plan.trades * cols + 8 * plan.trades * plan.step + (8 << 20)
     lines_out = pl.pallas_call(
@@ -358,7 +399,7 @@
         out_shape=jax.ShapeDtypeStruct((owners * path_parts, 1, LANES), F32),
         in_specs=[SMEM] * 4 + [VMEM] * (2 + len(incoming)),
         out_specs=VMEM,
-        scratch_shapes=[pltpu.VMEM((plan.trades, cols), BF16)],
+        scratch_shapes=[pltpu.VMEM((half_trades, cols), BF16)],
         name="value_and_allocate",
         compiler_params=pltpu.CompilerParams(vmem_limit_bytes=need),
     )(me, agr_of_ns, cpty_of_agr, margin_lag, default_weight, basis, *incoming)

time: 34.9 us -> 33.4 us (0.957)
  waiting for transfers between devices: 5.47 us -> 4.42 us
    pallas_call x1, Pallas kernels: 5.47 us -> 4.16 us  [body(): pl.pallas_call(functools.partial(main_kernel, plan, path_total), out_shap...]
    ppermute x1, waiting for transfers between devices: 1.35 us -> 0.32 us  [body(): incoming.append(lax.ppermute(incoming[0], 'path', pairs))]
    pallas_call x0 -> x1, Pallas kernels: none -> 1 us  [body(): pl.pallas_call(functools.partial(price_kernel, plan), out_shape=jax.Shape...]
  transfers between devices with their start and end apart: 2 -> 2, of which waited for: 2 -> 2; matrix products, arithmetic and copies ran while one was open for 0% -> 0% of each run, Pallas kernels for 9% -> 13%
where the time goes in v12:
time: 33.4 us; the launch traced here: 33.1 us
  Pallas kernels  11.2 us (34%)
  blocking collectives  9.34 us (28%)
  starting transfers between devices  7.29 us (22%)
  waiting for transfers between devices  4.42 us (13%)
  between operations  0.77 us (2%)
    all_to_all x1, blocking collectives, body(): lax.all_to_all(lines_out, ('trade', 'path'), split_axis=0, concat_axis=0,...  9.34 us
    all_to_all x1, starting transfers between devices, body(): lax.all_to_all(outgoing, 'trade', split_axis=0, concat_axis=0, tiled=True)  7.29 us
    pallas_call x1, Pallas kernels, body(): pl.pallas_call(functools.partial(main_kernel, plan, path_total), out_shap...  4.16 us
    all_to_all x1, waiting for transfers between devices, body(): lax.all_to_all(outgoing, 'trade', split_axis=0, concat_axis=0, tiled=True)  4.1 us
    pallas_call x1, Pallas kernels, body(): pl.pallas_call(functools.partial(basis_kernel, plan), out_shape=jax.Shape...  3.16 us
    pallas_call x1, Pallas kernels, body(): pl.pallas_call(functools.partial(pack_kernel, plan), out_shape=[jax.Shape...  2.1 us
    pallas_call x1, Pallas kernels, body(): pl.pallas_call(functools.partial(price_kernel, plan), out_shape=jax.Shape...  1 us
    pallas_call x1, Pallas kernels, body(): pl.pallas_call(functools.partial(finish_kernel, plan), out_shape=[jax.Sha...  0.81 us
  transfers between devices with their start and end apart: 2, of which 2 were waited for; matrix products, arithmetic and copies ran while one was open for 0% of the time, Pallas kernels for 13%

profile of v12, /device:TPU:0, one launch (start us, length us, event | category | flops | bytes accessed | tf_op | source)
XLA Modules:
  0.0 33.1 jit_solution(15297857452437245432)
XLA Ops:
  0.6 0.0 copy-start
  0.6 0.0 copy-start.1
  0.7 0.0 copy-start.5
  0.7 2.1 %pack.1 = (f32[8,512]{1,0:T(8,128)}, bf16[8,64,128]{2,1,0:T(8,128)(2,1)}) custom-call(s32[1]{0:T(128)} %bitcast.me_ref, s32[1]{0:T(128)} %bitcast.1.half_ref, s32[32,128]{1,0:T(8,128)} %bitcast.16, bf16[160,512]{1,0:T(8,128)(2,1)} %bitcast.15, f32[4,128]{1,0:T(4,128)} %bitcast.12), custom_call_target="tpu_custom_call" | custom-call | flops 4294967296 | bytes 524288 | tf_op jit(solution)/shard_map/pack/pallas_call | solution.py:340
  2.8 7.3 %all-to-all-start = ((bf16[8,64,128]{2,1,0:T(8,128)(2,1)}), bf16[8,64,128]{2,1,0:T(8,128)(2,1)S(1)}, u32[]{:S(2)}, u32[]{:S(2)}) async-start(bf16[8,64,128]{2,1,0:T(8,128)(2,1)} %get-tuple-element.9), calls=%async_computation | async-start | bytes 262144 | tf_op jit(solution)/shard_map/all_to_all | solution.py:357
  10.1 0.0 copy-done
  10.1 0.0 copy-done.1
  10.1 0.0 copy-done.5
  10.1 3.2 %basis.1.basis_ref = bf16[256,4096]{1,0:T(8,128)(2,1)S(1)} custom-call(bf16[2560,128]{1,0:T(8,128)(2,1)S(1)} %bitcast.10, f32[1,80]{1,0:T(1,128)S(1)} %bitcast.14, f32[80,80]{1,0:T(8,128)S(1)} %copy-done.1), custom_call_target="tpu_custom_call" | custom-call | flops 262144000 | bytes 4194304 | tf_op jit(solution)/shard_map/basis/pallas_call | solution.py:358
  13.3 0.0 copy-start.3
  13.3 0.0 copy-start.6
  13.3 0.0 copy-start.7
  13.3 0.0 copy-start.8
  13.3 4.1 %all-to-all-done.in_ref.refs_0_ = bf16[8,64,128]{2,1,0:T(8,128)(2,1)S(1)} async-done(((bf16[8,64,128]{2,1,0:T(8,128)(2,1)}), bf16[8,64,128]{2,1,0:T(8,128)(2,1)S(1)}, u32[]{:S(2)}, u32[]{:S(2)}) %all-to-all-start) | async-done | bytes 131104 | tf_op jit(solution)/shard_map/all_to_all | solution.py:357
  17.4 0.0 collective-permute-start
  17.4 1.0 %price_own_half.1.refs_2_ = bf16[384,4096]{1,0:T(8,128)(2,1)S(1)} custom-call(bf16[256,4096]{1,0:T(8,128)(2,1)S(1)} %basis.1.basis_ref, bf16[8,64,128]{2,1,0:T(8,128)(2,1)S(1)} %all-to-all-done.in_ref.refs_0_), custom_call_target="tpu_custom_call" | custom-call | flops 805306368 | bytes 6291456 | tf_op jit(solution)/shard_map/price_own_half/pallas_call | solution.py:383
  18.4 0.0 copy-start.2
  18.4 0.0 copy-start.4
  18.4 0.3 collective-permute-done.refs_1_
  18.8 0.0 copy-done.3
  18.8 0.0 copy-done.6
  18.8 0.0 copy-done.7
  18.8 0.0 copy-done.8
  18.8 4.2 %value_and_allocate.1 = f32[32,1,128]{2,1,0:T(1,128)S(1)} custom-call(s32[1]{0:T(128)} %bitcast.me_ref, s32[8]{0:T(128)S(1)} %copy-done.6, s32[4]{0:T(128)S(1)} %copy-done.7, s32[4]{0:T(128)S(1)} %copy-done.8, f32[4,32]{1,0:T(4,128)S(1)} %copy-done.3, bf16[256,4096]{1,0:T(8,128)(2,1)S(1)} %basis.1.basis_ref, ...), custom_call_target="tpu_custom_call" | custom-call | tf_op jit(solution)/shard_map/value_and_allocate/pallas_call | solution.py:397
  22.9 9.3 %all_to_all.10 = f32[32,1,128]{2,1,0:T(1,128)S(1)} all-to-all(f32[32,1,128]{2,1,0:T(1,128)S(1)} %value_and_allocate.1), channel_id=1, replica_groups=mesh['trade'=8,'path'=4] {'trade','path'}, dimensions={0} | all-to-all | bytes 32768 | tf_op jit(solution)/shard_map/all_to_all | solution.py:407
  32.3 0.0 copy-done.2
  32.3 0.0 copy-done.4
  32.3 0.8 %finish.1 = (f32[1,512]{1,0:T(1,128)}, f32[1,4]{1,0:T(1,128)}) custom-call(s32[1]{0:T(128)} %bitcast.me_ref, f32[8,512]{1,0:T(8,128)S(1)} %copy-done.2, f32[4,128]{1,0:T(4,128)S(1)} %bitcast.13, f32[32,128]{1,0:T(8,128)S(1)} %bitcast.11), custom_call_target="tpu_custom_call" | custom-call | tf_op jit(solution)/shard_map/finish/pallas_call | solution.py:409
Async XLA Ops:
  0.6 9.4 %copy-start = (bf16[80,32,128]{2,1,0:T(8,128)(2,1)S(1)}, bf16[80,32,128]{2,1,0:T(8,128)(2,1)}, u32[]{:S(2)}) copy-start(bf16[80,32,128]{2,1,0:T(8,128)(2,1)} %param.10) | copy-start | bytes 1966084
  0.6 9.4 %copy-start.1 = (f32[80,80]{1,0:T(8,128)S(1)}, f32[80,80]{1,0:T(8,128)}, u32[]{:S(2)}) copy-start(f32[80,80]{1,0:T(8,128)} %loading_hbm.1) | copy-start | bytes 76804
  0.7 9.4 %copy-start.5 = (f32[80]{0:T(128)S(1)}, f32[80]{0:T(128)}, u32[]{:S(2)}) copy-start(f32[80]{0:T(128)} %param.11) | copy-start | bytes 964
  2.8 14.6 %all-to-all-start = ((bf16[8,64,128]{2,1,0:T(8,128)(2,1)}), bf16[8,64,128]{2,1,0:T(8,128)(2,1)S(1)}, u32[]{:S(2)}, u32[]{:S(2)}) async-start(bf16[8,64,128]{2,1,0:T(8,128)(2,1)} %get-tuple-element.9), calls=%async_computation | async-start | bytes 262144 | tf_op jit(solution)/shard_map/all_to_all | solution.py:357
  13.3 5.5 %copy-start.3 = (f32[4,32]{1,0:T(4,128)S(1)}, f32[4,32]{1,0:T(4,128)}, u32[]{:S(2)}) copy-start(f32[4,32]{1,0:T(4,128)} %weight_ref.1) | copy-start | bytes 1540
  13.3 5.5 %copy-start.6 = (s32[8]{0:T(128)S(1)}, s32[8]{0:T(128)}, u32[]{:S(2)}) copy-start(s32[8]{0:T(128)} %agr_ref.1) | copy-start | bytes 100
  13.3 5.5 %copy-start.7 = (s32[4]{0:T(128)S(1)}, s32[4]{0:T(128)}, u32[]{:S(2)}) copy-start(s32[4]{0:T(128)} %cpty_ref.1) | copy-start | bytes 52
  13.3 5.5 %copy-start.8 = (s32[4]{0:T(128)S(1)}, s32[4]{0:T(128)}, u32[]{:S(2)}) copy-start(s32[4]{0:T(128)} %lag_ref.1) | copy-start | bytes 52
  17.4 1.3 %collective-permute-start = (bf16[8,64,128]{2,1,0:T(8,128)(2,1)S(1)}, bf16[8,64,128]{2,1,0:T(8,128)(2,1)S(1)}, u32[]{:S(2)}, u32[]{:S(2)}) collective-permute-start(bf16[8,64,128]{2,1,0:T(8,128)(2,1)S(1)} %all-to-all-done.in_ref.refs_0_), channel_id=1, source_target_pairs={{0,1},{1,0},{2,3},{3,2},{4,5},{5,4},{6,7},{7,6},{8,9},{9,8},{10,11... | collective-permute-start | bytes 393224 | tf_op jit(solution)/shard_map/ppermute | solution.py:381
  18.4 13.9 %copy-start.2 = (f32[8,512]{1,0:T(8,128)S(1)}, f32[8,512]{1,0:T(8,128)}, u32[]{:S(2)}) copy-start(f32[8,512]{1,0:T(8,128)} %get-tuple-element.8.place_ref) | copy-start | bytes 49156
  18.4 13.9 %copy-start.4 = (f32[512]{0:T(512)S(1)}, f32[512]{0:T(512)}, u32[]{:S(2)}) copy-start(f32[512]{0:T(512)} %param.14) | copy-start | bytes 6148

commit v13 on v12

--- a/solution.py
+++ b/solution.py
@@ -266,7 +266,9 @@
 
     grads = jnp.concatenate(grads, axis=1)
     dots = [
-        lax.dot_general(grads, values[...], BOTH_LANES, preferred_element_type=F32)
+        jnp.transpose(
+            lax.dot_general(values[...], grads, BOTH_LANES, preferred_element_type=F32)
+        )
         for values in val_refs
     ]
     dots = jnp.concatenate(dots, axis=1)

time: 33.4 us -> 33.5 us (level)
  no operation moved by 1% of the time
where the time goes in v13:
time: 33.5 us; the launch traced here: 33.2 us
  Pallas kernels  11.3 us (34%)
  blocking collectives  9.34 us (28%)
  starting transfers between devices  7.29 us (22%)
  waiting for transfers between devices  4.42 us (13%)
  between operations  0.77 us (2%)
    all_to_all x1, blocking collectives, body(): lax.all_to_all(lines_out, ('trade', 'path'), split_axis=0, concat_axis=0,...  9.34 us
    all_to_all x1, starting transfers between devices, body(): lax.all_to_all(outgoing, 'trade', split_axis=0, concat_axis=0, tiled=True)  7.29 us
    pallas_call x1, Pallas kernels, body(): pl.pallas_call(functools.partial(main_kernel, plan, path_total), out_shap...  4.23 us
    all_to_all x1, waiting for transfers between devices, body(): lax.all_to_all(outgoing, 'trade', split_axis=0, concat_axis=0, tiled=True)  4.1 us
    pallas_call x1, Pallas kernels, body(): pl.pallas_call(functools.partial(basis_kernel, plan), out_shape=jax.Shape...  3.16 us
    pallas_call x1, Pallas kernels, body(): pl.pallas_call(functools.partial(pack_kernel, plan), out_shape=[jax.Shape...  2.1 us
    pallas_call x1, Pallas kernels, body(): pl.pallas_call(functools.partial(price_kernel, plan), out_shape=jax.Shape...  1 us
    pallas_call x1, Pallas kernels, body(): pl.pallas_call(functools.partial(finish_kernel, plan), out_shape=[jax.Sha...  0.81 us
  transfers between devices with their start and end apart: 2, of which 2 were waited for; matrix products, arithmetic and copies ran while one was open for 0% of the time, Pallas kernels for 13%

profile of v13, /device:TPU:0, one launch (start us, length us, event | category | flops | bytes accessed | tf_op | source)
XLA Modules:
  0.0 33.2 jit_solution(1808427552736161939)
XLA Ops:
  0.6 0.0 copy-start
  0.6 0.0 copy-start.1
  0.7 0.0 copy-start.5
  0.7 2.1 %pack.1 = (f32[8,512]{1,0:T(8,128)}, bf16[8,64,128]{2,1,0:T(8,128)(2,1)}) custom-call(s32[1]{0:T(128)} %bitcast.me_ref, s32[1]{0:T(128)} %bitcast.1.half_ref, s32[32,128]{1,0:T(8,128)} %bitcast.16, bf16[160,512]{1,0:T(8,128)(2,1)} %bitcast.15, f32[4,128]{1,0:T(4,128)} %bitcast.12), custom_call_target="tpu_custom_call" | custom-call | flops 4294967296 | bytes 524288 | tf_op jit(solution)/shard_map/pack/pallas_call | solution.py:342
  2.8 7.3 %all-to-all-start = ((bf16[8,64,128]{2,1,0:T(8,128)(2,1)}), bf16[8,64,128]{2,1,0:T(8,128)(2,1)S(1)}, u32[]{:S(2)}, u32[]{:S(2)}) async-start(bf16[8,64,128]{2,1,0:T(8,128)(2,1)} %get-tuple-element.9), calls=%async_computation | async-start | bytes 262144 | tf_op jit(solution)/shard_map/all_to_all | solution.py:359
  10.1 0.0 copy-done
  10.1 0.0 copy-done.1
  10.1 0.0 copy-done.5
  10.1 3.2 %basis.1.basis_ref = bf16[256,4096]{1,0:T(8,128)(2,1)S(1)} custom-call(bf16[2560,128]{1,0:T(8,128)(2,1)S(1)} %bitcast.10, f32[1,80]{1,0:T(1,128)S(1)} %bitcast.14, f32[80,80]{1,0:T(8,128)S(1)} %copy-done.1), custom_call_target="tpu_custom_call" | custom-call | flops 262144000 | bytes 4194304 | tf_op jit(solution)/shard_map/basis/pallas_call | solution.py:360
  13.3 0.0 copy-start.3
  13.3 0.0 copy-start.6
  13.3 0.0 copy-start.7
  13.3 0.0 copy-start.8
  13.3 4.1 %all-to-all-done.in_ref.refs_0_ = bf16[8,64,128]{2,1,0:T(8,128)(2,1)S(1)} async-done(((bf16[8,64,128]{2,1,0:T(8,128)(2,1)}), bf16[8,64,128]{2,1,0:T(8,128)(2,1)S(1)}, u32[]{:S(2)}, u32[]{:S(2)}) %all-to-all-start) | async-done | bytes 131104 | tf_op jit(solution)/shard_map/all_to_all | solution.py:359
  17.4 0.0 collective-permute-start
  17.4 1.0 %price_own_half.1.refs_2_ = bf16[384,4096]{1,0:T(8,128)(2,1)S(1)} custom-call(bf16[256,4096]{1,0:T(8,128)(2,1)S(1)} %basis.1.basis_ref, bf16[8,64,128]{2,1,0:T(8,128)(2,1)S(1)} %all-to-all-done.in_ref.refs_0_), custom_call_target="tpu_custom_call" | custom-call | flops 805306368 | bytes 6291456 | tf_op jit(solution)/shard_map/price_own_half/pallas_call | solution.py:385
  18.4 0.0 copy-start.2
  18.4 0.0 copy-start.4
  18.4 0.3 collective-permute-done.refs_1_
  18.8 0.0 copy-done.3
  18.8 0.0 copy-done.6
  18.8 0.0 copy-done.7
  18.8 0.0 copy-done.8
  18.8 4.2 %value_and_allocate.1 = f32[32,1,128]{2,1,0:T(1,128)S(1)} custom-call(s32[1]{0:T(128)} %bitcast.me_ref, s32[8]{0:T(128)S(1)} %copy-done.6, s32[4]{0:T(128)S(1)} %copy-done.7, s32[4]{0:T(128)S(1)} %copy-done.8, f32[4,32]{1,0:T(4,128)S(1)} %copy-done.3, bf16[256,4096]{1,0:T(8,128)(2,1)S(1)} %basis.1.basis_ref, ...), custom_call_target="tpu_custom_call" | custom-call | tf_op jit(solution)/shard_map/value_and_allocate/pallas_call | solution.py:399
  23.0 9.3 %all_to_all.10 = f32[32,1,128]{2,1,0:T(1,128)S(1)} all-to-all(f32[32,1,128]{2,1,0:T(1,128)S(1)} %value_and_allocate.1), channel_id=1, replica_groups=mesh['trade'=8,'path'=4] {'trade','path'}, dimensions={0} | all-to-all | bytes 32768 | tf_op jit(solution)/shard_map/all_to_all | solution.py:409
  32.3 0.0 copy-done.2
  32.4 0.0 copy-done.4
  32.4 0.8 %finish.1 = (f32[1,512]{1,0:T(1,128)}, f32[1,4]{1,0:T(1,128)}) custom-call(s32[1]{0:T(128)} %bitcast.me_ref, f32[8,512]{1,0:T(8,128)S(1)} %copy-done.2, f32[4,128]{1,0:T(4,128)S(1)} %bitcast.13, f32[32,128]{1,0:T(8,128)S(1)} %bitcast.11), custom_call_target="tpu_custom_call" | custom-call | tf_op jit(solution)/shard_map/finish/pallas_call | solution.py:411
Async XLA Ops:
  0.6 9.4 %copy-start = (bf16[80,32,128]{2,1,0:T(8,128)(2,1)S(1)}, bf16[80,32,128]{2,1,0:T(8,128)(2,1)}, u32[]{:S(2)}) copy-start(bf16[80,32,128]{2,1,0:T(8,128)(2,1)} %param.10) | copy-start | bytes 1966084
  0.6 9.4 %copy-start.1 = (f32[80,80]{1,0:T(8,128)S(1)}, f32[80,80]{1,0:T(8,128)}, u32[]{:S(2)}) copy-start(f32[80,80]{1,0:T(8,128)} %loading_hbm.1) | copy-start | bytes 76804
  0.7 9.4 %copy-start.5 = (f32[80]{0:T(128)S(1)}, f32[80]{0:T(128)}, u32[]{:S(2)}) copy-start(f32[80]{0:T(128)} %param.11) | copy-start | bytes 964
  2.8 14.6 %all-to-all-start = ((bf16[8,64,128]{2,1,0:T(8,128)(2,1)}), bf16[8,64,128]{2,1,0:T(8,128)(2,1)S(1)}, u32[]{:S(2)}, u32[]{:S(2)}) async-start(bf16[8,64,128]{2,1,0:T(8,128)(2,1)} %get-tuple-element.9), calls=%async_computation | async-start | bytes 262144 | tf_op jit(solution)/shard_map/all_to_all | solution.py:359
  13.3 5.5 %copy-start.3 = (f32[4,32]{1,0:T(4,128)S(1)}, f32[4,32]{1,0:T(4,128)}, u32[]{:S(2)}) copy-start(f32[4,32]{1,0:T(4,128)} %weight_ref.1) | copy-start | bytes 1540
  13.3 5.5 %copy-start.6 = (s32[8]{0:T(128)S(1)}, s32[8]{0:T(128)}, u32[]{:S(2)}) copy-start(s32[8]{0:T(128)} %agr_ref.1) | copy-start | bytes 100
  13.3 5.5 %copy-start.7 = (s32[4]{0:T(128)S(1)}, s32[4]{0:T(128)}, u32[]{:S(2)}) copy-start(s32[4]{0:T(128)} %cpty_ref.1) | copy-start | bytes 52
  13.3 5.5 %copy-start.8 = (s32[4]{0:T(128)S(1)}, s32[4]{0:T(128)}, u32[]{:S(2)}) copy-start(s32[4]{0:T(128)} %lag_ref.1) | copy-start | bytes 52
  17.4 1.3 %collective-permute-start = (bf16[8,64,128]{2,1,0:T(8,128)(2,1)S(1)}, bf16[8,64,128]{2,1,0:T(8,128)(2,1)S(1)}, u32[]{:S(2)}, u32[]{:S(2)}) collective-permute-start(bf16[8,64,128]{2,1,0:T(8,128)(2,1)S(1)} %all-to-all-done.in_ref.refs_0_), channel_id=1, source_target_pairs={{0,1},{1,0},{2,3},{3,2},{4,5},{5,4},{6,7},{7,6},{8,9},{9,8},{10,11... | collective-permute-start | bytes 393224 | tf_op jit(solution)/shard_map/ppermute | solution.py:383
  18.4 13.9 %copy-start.2 = (f32[8,512]{1,0:T(8,128)S(1)}, f32[8,512]{1,0:T(8,128)}, u32[]{:S(2)}) copy-start(f32[8,512]{1,0:T(8,128)} %get-tuple-element.8.place_ref) | copy-start | bytes 49156
  18.4 13.9 %copy-start.4 = (f32[512]{0:T(512)S(1)}, f32[512]{0:T(512)}, u32[]{:S(2)}) copy-start(f32[512]{0:T(512)} %param.14) | copy-start | bytes 6148

commit v14 on v12

--- a/solution.py
+++ b/solution.py
@@ -70,7 +70,7 @@
         self.trades = owners * self.slots
         self.dates = dates
         self.width = 512
-        self.step = 2048 if self.trades <= 1024 else 512
+        self.step = 4096 if self.trades <= 1024 else 512
 
 
 def pack_kernel(plan, me_ref, half_ref, sets_hbm, coef_hbm, notional_hbm, place_ref, out_ref, *refs):
@@ -222,7 +222,7 @@
     for n in range(NS_DEV):
         agr = jnp.where(local == n, agr_ref[n] - me * AG_DEV, agr)
     row = iota((SUBS, plan.trades), 0)
-    hot = lax.rem(row, AG_DEV) == agr
+    hot = (row & (AG_DEV - 1)) == agr
     netting = jnp.where(hot, jnp.where(row < AG_DEV, info[0:1], info[1:2]), 0.0).astype(BF16)
 
     price(plan, left, basis_ref, val_ref)
@@ -235,7 +235,7 @@
     both = both + pltpu.roll(both, AG_DEV, 0)
     owed = [both[:, LANES * t : LANES * (t + 1)] for t in range(dates)]
 
-    member = lax.rem(iota((SUBS, LANES), 0), AG_DEV)
+    member = iota((SUBS, LANES), 0) & (AG_DEV - 1)
     lag = jnp.zeros((SUBS, LANES), jnp.int32)
     cpty = jnp.zeros((SUBS, LANES), jnp.int32)
     for a in range(AG_DEV):
@@ -299,16 +299,19 @@
     count = lines.shape[0]
     paths = count // plan.owners
     pieces = jnp.concatenate(split_bf16(lines, 3), axis=0)
-    half = lax.rem(lax.rem(iota((pieces.shape[0], rows), 0), paths), plan.halves)
-    found = jnp.zeros(half.shape, F32)
+    row = iota((pieces.shape[0], 1), 0) & (count - 1)
+    shift = paths.bit_length() - 1
+    half = row & (plan.halves - 1)
+    found = jnp.zeros((pieces.shape[0], rows), F32)
     for h in range(plan.halves):
-        slot = lax.rem(rank + plan.room * h, plan.slots)
+        slot = rank + plan.room * h
+        slot = jnp.where(slot >= plan.slots, slot - plan.slots, slot)
         hot = mask_bf16(iota((LANES, rows), 0) == slot)
         found = jnp.where(half == h, jnp.dot(pieces, hot, preferred_element_type=F32), found)
-    wanted = lax.rem(iota(found.shape, 0), count) // paths == key
+    wanted = lax.shift_right_logical(row, shift) == key
     share = jnp.sum(jnp.where(wanted, found, 0.0), axis=0, keepdims=True)
     alloc_ref[...] = share * in_a_row(notional_ref[...])
-    own = iota(lines.shape, 0) // paths == me
+    own = lax.shift_right_logical(iota((count, 1), 0), shift) == me
     cva = jnp.sum(jnp.where(own, lines, 0.0), axis=0, keepdims=True)
     cva_ref[...] = cva[:, plan.slots : plan.slots + cva_ref.shape[1]]
 

time: 33.4 us -> 33.4 us (level)
  no operation moved by 1% of the time
where the time goes in v14:
time: 33.4 us; the launch traced here: 33.1 us
  Pallas kernels  11.2 us (34%)
  blocking collectives  9.34 us (28%)
  starting transfers between devices  7.29 us (22%)
  waiting for transfers between devices  4.42 us (13%)
  between operations  0.77 us (2%)
    all_to_all x1, blocking collectives, body(): lax.all_to_all(lines_out, ('trade', 'path'), split_axis=0, concat_axis=0,...  9.34 us
    all_to_all x1, starting transfers between devices, body(): lax.all_to_all(outgoing, 'trade', split_axis=0, concat_axis=0, tiled=True)  7.29 us
    pallas_call x1, Pallas kernels, body(): pl.pallas_call(functools.partial(main_kernel, plan, path_total), out_shap...  4.17 us
    all_to_all x1, waiting for transfers between devices, body(): lax.all_to_all(outgoing, 'trade', split_axis=0, concat_axis=0, tiled=True)  4.1 us
    pallas_call x1, Pallas kernels, body(): pl.pallas_call(functools.partial(basis_kernel, plan), out_shape=jax.Shape...  3.16 us
    pallas_call x1, Pallas kernels, body(): pl.pallas_call(functools.partial(pack_kernel, plan), out_shape=[jax.Shape...  2.1 us
    pallas_call x1, Pallas kernels, body(): pl.pallas_call(functools.partial(price_kernel, plan), out_shape=jax.Shape...  1 us
    pallas_call x1, Pallas kernels, body(): pl.pallas_call(functools.partial(finish_kernel, plan), out_shape=[jax.Sha...  0.81 us
  transfers between devices with their start and end apart: 2, of which 2 were waited for; matrix products, arithmetic and copies ran while one was open for 0% of the time, Pallas kernels for 13%

profile of v14, /device:TPU:0, one launch (start us, length us, event | category | flops | bytes accessed | tf_op | source)
XLA Modules:
  0.0 33.1 jit_solution(18148092828000032941)
XLA Ops:
  0.6 0.0 copy-start
  0.6 0.0 copy-start.1
  0.7 0.0 copy-start.5
  0.7 2.1 %pack.1 = (f32[8,512]{1,0:T(8,128)}, bf16[8,64,128]{2,1,0:T(8,128)(2,1)}) custom-call(s32[1]{0:T(128)} %bitcast.me_ref, s32[1]{0:T(128)} %bitcast.1.half_ref, s32[32,128]{1,0:T(8,128)} %bitcast.16, bf16[160,512]{1,0:T(8,128)(2,1)} %bitcast.15, f32[4,128]{1,0:T(4,128)} %bitcast.12), custom_call_target="tpu_custom_call" | custom-call | flops 4294967296 | bytes 524288 | tf_op jit(solution)/shard_map/pack/pallas_call | solution.py:343
  2.8 7.3 %all-to-all-start = ((bf16[8,64,128]{2,1,0:T(8,128)(2,1)}), bf16[8,64,128]{2,1,0:T(8,128)(2,1)S(1)}, u32[]{:S(2)}, u32[]{:S(2)}) async-start(bf16[8,64,128]{2,1,0:T(8,128)(2,1)} %get-tuple-element.9), calls=%async_computation | async-start | bytes 262144 | tf_op jit(solution)/shard_map/all_to_all | solution.py:360
  10.1 0.0 copy-done
  10.1 0.0 copy-done.1
  10.1 0.0 copy-done.5
  10.1 3.2 %basis.1.basis_ref = bf16[256,4096]{1,0:T(8,128)(2,1)S(1)} custom-call(bf16[2560,128]{1,0:T(8,128)(2,1)S(1)} %bitcast.10, f32[1,80]{1,0:T(1,128)S(1)} %bitcast.14, f32[80,80]{1,0:T(8,128)S(1)} %copy-done.1), custom_call_target="tpu_custom_call" | custom-call | flops 262144000 | bytes 4194304 | tf_op jit(solution)/shard_map/basis/pallas_call | solution.py:361
  13.3 0.0 copy-start.3
  13.3 0.0 copy-start.6
  13.3 0.0 copy-start.7
  13.3 0.0 copy-start.8
  13.3 4.1 %all-to-all-done.in_ref.refs_0_ = bf16[8,64,128]{2,1,0:T(8,128)(2,1)S(1)} async-done(((bf16[8,64,128]{2,1,0:T(8,128)(2,1)}), bf16[8,64,128]{2,1,0:T(8,128)(2,1)S(1)}, u32[]{:S(2)}, u32[]{:S(2)}) %all-to-all-start) | async-done | bytes 131104 | tf_op jit(solution)/shard_map/all_to_all | solution.py:360
  17.4 0.0 collective-permute-start
  17.4 1.0 %price_own_half.1.refs_2_ = bf16[384,4096]{1,0:T(8,128)(2,1)S(1)} custom-call(bf16[256,4096]{1,0:T(8,128)(2,1)S(1)} %basis.1.basis_ref, bf16[8,64,128]{2,1,0:T(8,128)(2,1)S(1)} %all-to-all-done.in_ref.refs_0_), custom_call_target="tpu_custom_call" | custom-call | flops 805306368 | bytes 6291456 | tf_op jit(solution)/shard_map/price_own_half/pallas_call | solution.py:386
  18.4 0.0 copy-start.2
  18.4 0.0 copy-start.4
  18.4 0.3 collective-permute-done.refs_1_
  18.8 0.0 copy-done.3
  18.8 0.0 copy-done.6
  18.8 0.0 copy-done.7
  18.8 0.0 copy-done.8
  18.8 4.2 %value_and_allocate.1 = f32[32,1,128]{2,1,0:T(1,128)S(1)} custom-call(s32[1]{0:T(128)} %bitcast.me_ref, s32[8]{0:T(128)S(1)} %copy-done.6, s32[4]{0:T(128)S(1)} %copy-done.7, s32[4]{0:T(128)S(1)} %copy-done.8, f32[4,32]{1,0:T(4,128)S(1)} %copy-done.3, bf16[256,4096]{1,0:T(8,128)(2,1)S(1)} %basis.1.basis_ref, ...), custom_call_target="tpu_custom_call" | custom-call | tf_op jit(solution)/shard_map/value_and_allocate/pallas_call | solution.py:400
  23.0 9.3 %all_to_all.10 = f32[32,1,128]{2,1,0:T(1,128)S(1)} all-to-all(f32[32,1,128]{2,1,0:T(1,128)S(1)} %value_and_allocate.1), channel_id=1, replica_groups=mesh['trade'=8,'path'=4] {'trade','path'}, dimensions={0} | all-to-all | bytes 32768 | tf_op jit(solution)/shard_map/all_to_all | solution.py:410
  32.3 0.0 copy-done.2
  32.3 0.0 copy-done.4
  32.3 0.8 %finish.1 = (f32[1,512]{1,0:T(1,128)}, f32[1,4]{1,0:T(1,128)}) custom-call(s32[1]{0:T(128)} %bitcast.me_ref, f32[8,512]{1,0:T(8,128)S(1)} %copy-done.2, f32[4,128]{1,0:T(4,128)S(1)} %bitcast.13, f32[32,128]{1,0:T(8,128)S(1)} %bitcast.11), custom_call_target="tpu_custom_call" | custom-call | tf_op jit(solution)/shard_map/finish/pallas_call | solution.py:412
Async XLA Ops:
  0.6 9.4 %copy-start = (bf16[80,32,128]{2,1,0:T(8,128)(2,1)S(1)}, bf16[80,32,128]{2,1,0:T(8,128)(2,1)}, u32[]{:S(2)}) copy-start(bf16[80,32,128]{2,1,0:T(8,128)(2,1)} %param.10) | copy-start | bytes 1966084
  0.6 9.4 %copy-start.1 = (f32[80,80]{1,0:T(8,128)S(1)}, f32[80,80]{1,0:T(8,128)}, u32[]{:S(2)}) copy-start(f32[80,80]{1,0:T(8,128)} %loading_hbm.1) | copy-start | bytes 76804
  0.7 9.4 %copy-start.5 = (f32[80]{0:T(128)S(1)}, f32[80]{0:T(128)}, u32[]{:S(2)}) copy-start(f32[80]{0:T(128)} %param.11) | copy-start | bytes 964
  2.8 14.6 %all-to-all-start = ((bf16[8,64,128]{2,1,0:T(8,128)(2,1)}), bf16[8,64,128]{2,1,0:T(8,128)(2,1)S(1)}, u32[]{:S(2)}, u32[]{:S(2)}) async-start(bf16[8,64,128]{2,1,0:T(8,128)(2,1)} %get-tuple-element.9), calls=%async_computation | async-start | bytes 262144 | tf_op jit(solution)/shard_map/all_to_all | solution.py:360
  13.3 5.5 %copy-start.3 = (f32[4,32]{1,0:T(4,128)S(1)}, f32[4,32]{1,0:T(4,128)}, u32[]{:S(2)}) copy-start(f32[4,32]{1,0:T(4,128)} %weight_ref.1) | copy-start | bytes 1540
  13.3 5.5 %copy-start.6 = (s32[8]{0:T(128)S(1)}, s32[8]{0:T(128)}, u32[]{:S(2)}) copy-start(s32[8]{0:T(128)} %agr_ref.1) | copy-start | bytes 100
  13.3 5.5 %copy-start.7 = (s32[4]{0:T(128)S(1)}, s32[4]{0:T(128)}, u32[]{:S(2)}) copy-start(s32[4]{0:T(128)} %cpty_ref.1) | copy-start | bytes 52
  13.3 5.5 %copy-start.8 = (s32[4]{0:T(128)S(1)}, s32[4]{0:T(128)}, u32[]{:S(2)}) copy-start(s32[4]{0:T(128)} %lag_ref.1) | copy-start | bytes 52
  17.4 1.3 %collective-permute-start = (bf16[8,64,128]{2,1,0:T(8,128)(2,1)S(1)}, bf16[8,64,128]{2,1,0:T(8,128)(2,1)S(1)}, u32[]{:S(2)}, u32[]{:S(2)}) collective-permute-start(bf16[8,64,128]{2,1,0:T(8,128)(2,1)S(1)} %all-to-all-done.in_ref.refs_0_), channel_id=1, source_target_pairs={{0,1},{1,0},{2,3},{3,2},{4,5},{5,4},{6,7},{7,6},{8,9},{9,8},{10,11... | collective-permute-start | bytes 393224 | tf_op jit(solution)/shard_map/ppermute | solution.py:384
  18.4 13.9 %copy-start.2 = (f32[8,512]{1,0:T(8,128)S(1)}, f32[8,512]{1,0:T(8,128)}, u32[]{:S(2)}) copy-start(f32[8,512]{1,0:T(8,128)} %get-tuple-element.8.place_ref) | copy-start | bytes 49156
  18.4 13.9 %copy-start.4 = (f32[512]{0:T(512)S(1)}, f32[512]{0:T(512)}, u32[]{:S(2)}) copy-start(f32[512]{0:T(512)} %param.14) | copy-start | bytes 6148

commit v15 on v14

--- a/solution.py
+++ b/solution.py
@@ -69,8 +69,8 @@
         self.slots = self.halves * self.room
         self.trades = owners * self.slots
         self.dates = dates
-        self.width = 512
-        self.step = 4096 if self.trades <= 1024 else 512
+        self.width = 1024
+        self.step = 2048 if self.trades <= 1024 else 512
 
 
 def pack_kernel(plan, me_ref, half_ref, sets_hbm, coef_hbm, notional_hbm, place_ref, out_ref, *refs):

time: 33.4 us -> 33.4 us (level)
  waiting for transfers between devices: 4.42 us -> 5.1 us
  Pallas kernels: 11.2 us -> 10.6 us
    all_to_all x1, waiting for transfers between devices: 4.1 us -> 4.78 us  [body(): lax.all_to_all(outgoing, 'trade', split_axis=0, concat_axis=0, tiled=True)]
    pallas_call x1, Pallas kernels: 3.16 us -> 2.48 us  [body(): pl.pallas_call(functools.partial(basis_kernel, plan), out_shape=jax.Shape...]
  transfers between devices with their start and end apart: 2 -> 2, of which waited for: 2 -> 2; matrix products, arithmetic and copies ran while one was open for 0% -> 0% of each run, Pallas kernels for 13% -> 11%
where the time goes in v15:
time: 33.4 us; the launch traced here: 33.1 us
  Pallas kernels  10.6 us (32%)
  blocking collectives  9.34 us (28%)
  starting transfers between devices  7.29 us (22%)
  waiting for transfers between devices  5.1 us (15%)
  between operations  0.77 us (2%)
    all_to_all x1, blocking collectives, body(): lax.all_to_all(lines_out, ('trade', 'path'), split_axis=0, concat_axis=0,...  9.34 us
    all_to_all x1, starting transfers between devices, body(): lax.all_to_all(outgoing, 'trade', split_axis=0, concat_axis=0, tiled=True)  7.29 us
    all_to_all x1, waiting for transfers between devices, body(): lax.all_to_all(outgoing, 'trade', split_axis=0, concat_axis=0, tiled=True)  4.78 us
    pallas_call x1, Pallas kernels, body(): pl.pallas_call(functools.partial(main_kernel, plan, path_total), out_shap...  4.16 us
    pallas_call x1, Pallas kernels, body(): pl.pallas_call(functools.partial(basis_kernel, plan), out_shape=jax.Shape...  2.48 us
    pallas_call x1, Pallas kernels, body(): pl.pallas_call(functools.partial(pack_kernel, plan), out_shape=[jax.Shape...  2.1 us
    pallas_call x1, Pallas kernels, body(): pl.pallas_call(functools.partial(price_kernel, plan), out_shape=jax.Shape...  1 us
    pallas_call x1, Pallas kernels, body(): pl.pallas_call(functools.partial(finish_kernel, plan), out_shape=[jax.Sha...  0.81 us
  transfers between devices with their start and end apart: 2, of which 2 were waited for; matrix products, arithmetic and copies ran while one was open for 0% of the time, Pallas kernels for 11%

profile of v15, /device:TPU:0, one launch (start us, length us, event | category | flops | bytes accessed | tf_op | source)
XLA Modules:
  0.0 33.1 jit_solution(18318830452713362806)
XLA Ops:
  0.6 0.0 copy-start
  0.6 0.0 copy-start.1
  0.7 0.0 copy-start.5
  0.7 2.1 %pack.1 = (f32[8,512]{1,0:T(8,128)}, bf16[8,64,128]{2,1,0:T(8,128)(2,1)}) custom-call(s32[1]{0:T(128)} %bitcast.me_ref, s32[1]{0:T(128)} %bitcast.1.half_ref, s32[32,128]{1,0:T(8,128)} %bitcast.16, bf16[160,512]{1,0:T(8,128)(2,1)} %bitcast.15, f32[4,128]{1,0:T(4,128)} %bitcast.12), custom_call_target="tpu_custom_call" | custom-call | flops 4294967296 | bytes 524288 | tf_op jit(solution)/shard_map/pack/pallas_call | solution.py:343
  2.8 7.3 %all-to-all-start = ((bf16[8,64,128]{2,1,0:T(8,128)(2,1)}), bf16[8,64,128]{2,1,0:T(8,128)(2,1)S(1)}, u32[]{:S(2)}, u32[]{:S(2)}) async-start(bf16[8,64,128]{2,1,0:T(8,128)(2,1)} %get-tuple-element.9), calls=%async_computation | async-start | bytes 262144 | tf_op jit(solution)/shard_map/all_to_all | solution.py:360
  10.1 0.0 copy-done
  10.1 0.0 copy-done.1
  10.1 0.0 copy-done.5
  10.1 2.5 %basis.1.basis_ref = bf16[256,4096]{1,0:T(8,128)(2,1)S(1)} custom-call(bf16[2560,128]{1,0:T(8,128)(2,1)S(1)} %bitcast.10, f32[1,80]{1,0:T(1,128)S(1)} %bitcast.14, f32[80,80]{1,0:T(8,128)S(1)} %copy-done.1), custom_call_target="tpu_custom_call" | custom-call | flops 262144000 | bytes 4194304 | tf_op jit(solution)/shard_map/basis/pallas_call | solution.py:361
  12.6 0.0 copy-start.3
  12.6 0.0 copy-start.6
  12.6 0.0 copy-start.7
  12.6 0.0 copy-start.8
  12.6 4.8 %all-to-all-done.in_ref.refs_0_ = bf16[8,64,128]{2,1,0:T(8,128)(2,1)S(1)} async-done(((bf16[8,64,128]{2,1,0:T(8,128)(2,1)}), bf16[8,64,128]{2,1,0:T(8,128)(2,1)S(1)}, u32[]{:S(2)}, u32[]{:S(2)}) %all-to-all-start) | async-done | bytes 131104 | tf_op jit(solution)/shard_map/all_to_all | solution.py:360
  17.4 0.0 collective-permute-start
  17.4 1.0 %price_own_half.1.refs_2_ = bf16[384,4096]{1,0:T(8,128)(2,1)S(1)} custom-call(bf16[256,4096]{1,0:T(8,128)(2,1)S(1)} %basis.1.basis_ref, bf16[8,64,128]{2,1,0:T(8,128)(2,1)S(1)} %all-to-all-done.in_ref.refs_0_), custom_call_target="tpu_custom_call" | custom-call | flops 805306368 | bytes 6291456 | tf_op jit(solution)/shard_map/price_own_half/pallas_call | solution.py:386
  18.4 0.0 copy-start.2
  18.4 0.0 copy-start.4
  18.4 0.3 collective-permute-done.refs_1_
  18.8 0.0 copy-done.3
  18.8 0.0 copy-done.6
  18.8 0.0 copy-done.7
  18.8 0.0 copy-done.8
  18.8 4.2 %value_and_allocate.1 = f32[32,1,128]{2,1,0:T(1,128)S(1)} custom-call(s32[1]{0:T(128)} %bitcast.me_ref, s32[8]{0:T(128)S(1)} %copy-done.6, s32[4]{0:T(128)S(1)} %copy-done.7, s32[4]{0:T(128)S(1)} %copy-done.8, f32[4,32]{1,0:T(4,128)S(1)} %copy-done.3, bf16[256,4096]{1,0:T(8,128)(2,1)S(1)} %basis.1.basis_ref, ...), custom_call_target="tpu_custom_call" | custom-call | tf_op jit(solution)/shard_map/value_and_allocate/pallas_call | solution.py:400
  22.9 9.3 %all_to_all.10 = f32[32,1,128]{2,1,0:T(1,128)S(1)} all-to-all(f32[32,1,128]{2,1,0:T(1,128)S(1)} %value_and_allocate.1), channel_id=1, replica_groups=mesh['trade'=8,'path'=4] {'trade','path'}, dimensions={0} | all-to-all | bytes 32768 | tf_op jit(solution)/shard_map/all_to_all | solution.py:410
  32.3 0.0 copy-done.2
  32.3 0.0 copy-done.4
  32.3 0.8 %finish.1 = (f32[1,512]{1,0:T(1,128)}, f32[1,4]{1,0:T(1,128)}) custom-call(s32[1]{0:T(128)} %bitcast.me_ref, f32[8,512]{1,0:T(8,128)S(1)} %copy-done.2, f32[4,128]{1,0:T(4,128)S(1)} %bitcast.13, f32[32,128]{1,0:T(8,128)S(1)} %bitcast.11), custom_call_target="tpu_custom_call" | custom-call | tf_op jit(solution)/shard_map/finish/pallas_call | solution.py:412
Async XLA Ops:
  0.6 9.4 %copy-start = (bf16[80,32,128]{2,1,0:T(8,128)(2,1)S(1)}, bf16[80,32,128]{2,1,0:T(8,128)(2,1)}, u32[]{:S(2)}) copy-start(bf16[80,32,128]{2,1,0:T(8,128)(2,1)} %param.10) | copy-start | bytes 1966084
  0.6 9.4 %copy-start.1 = (f32[80,80]{1,0:T(8,128)S(1)}, f32[80,80]{1,0:T(8,128)}, u32[]{:S(2)}) copy-start(f32[80,80]{1,0:T(8,128)} %loading_hbm.1) | copy-start | bytes 76804
  0.7 9.4 %copy-start.5 = (f32[80]{0:T(128)S(1)}, f32[80]{0:T(128)}, u32[]{:S(2)}) copy-start(f32[80]{0:T(128)} %param.11) | copy-start | bytes 964
  2.8 14.6 %all-to-all-start = ((bf16[8,64,128]{2,1,0:T(8,128)(2,1)}), bf16[8,64,128]{2,1,0:T(8,128)(2,1)S(1)}, u32[]{:S(2)}, u32[]{:S(2)}) async-start(bf16[8,64,128]{2,1,0:T(8,128)(2,1)} %get-tuple-element.9), calls=%async_computation | async-start | bytes 262144 | tf_op jit(solution)/shard_map/all_to_all | solution.py:360
  12.6 6.2 %copy-start.3 = (f32[4,32]{1,0:T(4,128)S(1)}, f32[4,32]{1,0:T(4,128)}, u32[]{:S(2)}) copy-start(f32[4,32]{1,0:T(4,128)} %weight_ref.1) | copy-start | bytes 1540
  12.6 6.2 %copy-start.6 = (s32[8]{0:T(128)S(1)}, s32[8]{0:T(128)}, u32[]{:S(2)}) copy-start(s32[8]{0:T(128)} %agr_ref.1) | copy-start | bytes 100
  12.6 6.2 %copy-start.7 = (s32[4]{0:T(128)S(1)}, s32[4]{0:T(128)}, u32[]{:S(2)}) copy-start(s32[4]{0:T(128)} %cpty_ref.1) | copy-start | bytes 52
  12.6 6.2 %copy-start.8 = (s32[4]{0:T(128)S(1)}, s32[4]{0:T(128)}, u32[]{:S(2)}) copy-start(s32[4]{0:T(128)} %lag_ref.1) | copy-start | bytes 52
  17.4 1.3 %collective-permute-start = (bf16[8,64,128]{2,1,0:T(8,128)(2,1)S(1)}, bf16[8,64,128]{2,1,0:T(8,128)(2,1)S(1)}, u32[]{:S(2)}, u32[]{:S(2)}) collective-permute-start(bf16[8,64,128]{2,1,0:T(8,128)(2,1)S(1)} %all-to-all-done.in_ref.refs_0_), channel_id=1, source_target_pairs={{0,1},{1,0},{2,3},{3,2},{4,5},{5,4},{6,7},{7,6},{8,9},{9,8},{10,11... | collective-permute-start | bytes 393224 | tf_op jit(solution)/shard_map/ppermute | solution.py:384
  18.4 13.9 %copy-start.2 = (f32[8,512]{1,0:T(8,128)S(1)}, f32[8,512]{1,0:T(8,128)}, u32[]{:S(2)}) copy-start(f32[8,512]{1,0:T(8,128)} %get-tuple-element.8.place_ref) | copy-start | bytes 49156
  18.4 13.9 %copy-start.4 = (f32[512]{0:T(512)S(1)}, f32[512]{0:T(512)}, u32[]{:S(2)}) copy-start(f32[512]{0:T(512)} %param.14) | copy-start | bytes 6148

commit v16 on v15

--- a/solution.py
+++ b/solution.py
@@ -83,6 +83,7 @@
     lines = notional_ref.shape[0]
     rows = lines * LANES
     shared = SUBS // lines
+    before = mask_bf16(iota((rows, rows), 0) < iota((rows, rows), 1))
     copies[0].wait()
     block = sets_ref[pl.ds(pl.multiple_of(me // shared * SUBS, SUBS), SUBS), :]
     own = block[0:lines]
@@ -91,16 +92,6 @@
     sets = in_a_row(own)
     key = lax.shift_right_logical(sets, 3)
     local = sets - key * NS_DEV
-    hot = iota((owners, rows), 0) == key
-    before = mask_bf16(iota((rows, rows), 0) < iota((rows, rows), 1))
-    count = jnp.dot(mask_bf16(hot), before, preferred_element_type=F32)
-    rank = jnp.sum(jnp.where(hot, count, 0.0), axis=0, keepdims=True)
-    place_ref[...] = jnp.concatenate(
-        [key.astype(F32), rank, jnp.zeros((SUBS - 2, rows), F32)], axis=0
-    )
-    mine = rank.astype(jnp.int32) - room * half_ref[0]
-    spot = jnp.where((mine >= 0) & (mine < room), key * room + mine, -1)
-    chosen = mask_bf16(iota((owners * room, rows), 0) == spot)
     copies[1].wait()
     notional = in_a_row(notional_ref[...])
     high = notional.astype(BF16).astype(F32)
@@ -109,6 +100,15 @@
     )
     copies[2].wait()
     table = jnp.concatenate([coef_ref[...], info.astype(BF16)], axis=0)
+    hot = iota((owners, rows), 0) == key
+    count = jnp.dot(mask_bf16(hot), before, preferred_element_type=F32)
+    rank = jnp.sum(jnp.where(hot, count, 0.0), axis=0, keepdims=True)
+    place_ref[...] = jnp.concatenate(
+        [key.astype(F32), rank, jnp.zeros((SUBS - 2, rows), F32)], axis=0
+    )
+    mine = rank.astype(jnp.int32) - room * half_ref[0]
+    spot = jnp.where((mine >= 0) & (mine < room), key * room + mine, -1)
+    chosen = mask_bf16(iota((owners * room, rows), 0) == spot)
     moved = lax.dot_general(chosen, table, BOTH_LANES, preferred_element_type=F32)
     ids = LANES + extra
     for d in range(owners):

time: 33.4 us -> 33.4 us (level)
  transfers between devices with their start and end apart: 2 -> 2, of which waited for: 2 -> 2; matrix products, arithmetic and copies ran while one was open for 0% -> 0% of each run, Pallas kernels for 11% -> 10%
where the time goes in v16:
time: 33.4 us; the launch traced here: 33.2 us
  Pallas kernels  10.6 us (32%)
  blocking collectives  9.34 us (28%)
  starting transfers between devices  7.3 us (22%)
  waiting for transfers between devices  5.1 us (15%)
  between operations  0.77 us (2%)
    all_to_all x1, blocking collectives, body(): lax.all_to_all(lines_out, ('trade', 'path'), split_axis=0, concat_axis=0,...  9.34 us
    all_to_all x1, starting transfers between devices, body(): lax.all_to_all(outgoing, 'trade', split_axis=0, concat_axis=0, tiled=True)  7.29 us
    all_to_all x1, waiting for transfers between devices, body(): lax.all_to_all(outgoing, 'trade', split_axis=0, concat_axis=0, tiled=True)  4.78 us
    pallas_call x1, Pallas kernels, body(): pl.pallas_call(functools.partial(main_kernel, plan, path_total), out_shap...  4.16 us
    pallas_call x1, Pallas kernels, body(): pl.pallas_call(functools.partial(basis_kernel, plan), out_shape=jax.Shape...  2.48 us
    pallas_call x1, Pallas kernels, body(): pl.pallas_call(functools.partial(pack_kernel, plan), out_shape=[jax.Shape...  2.15 us
    pallas_call x1, Pallas kernels, body(): pl.pallas_call(functools.partial(price_kernel, plan), out_shape=jax.Shape...  1 us
    pallas_call x1, Pallas kernels, body(): pl.pallas_call(functools.partial(finish_kernel, plan), out_shape=[jax.Sha...  0.81 us
  transfers between devices with their start and end apart: 2, of which 2 were waited for; matrix products, arithmetic and copies ran while one was open for 0% of the time, Pallas kernels for 10%

profile of v16, /device:TPU:0, one launch (start us, length us, event | category | flops | bytes accessed | tf_op | source)
XLA Modules:
  0.0 33.2 jit_solution(16688853107900047500)
XLA Ops:
  0.6 0.0 copy-start
  0.6 0.0 copy-start.1
  0.7 0.0 copy-start.5
  0.7 2.1 %pack.1 = (f32[8,512]{1,0:T(8,128)}, bf16[8,64,128]{2,1,0:T(8,128)(2,1)}) custom-call(s32[1]{0:T(128)} %bitcast.me_ref, s32[1]{0:T(128)} %bitcast.1.half_ref, s32[32,128]{1,0:T(8,128)} %bitcast.16, bf16[160,512]{1,0:T(8,128)(2,1)} %bitcast.15, f32[4,128]{1,0:T(4,128)} %bitcast.12), custom_call_target="tpu_custom_call" | custom-call | flops 4294967296 | bytes 524288 | tf_op jit(solution)/shard_map/pack/pallas_call | solution.py:343
  2.8 7.3 %all-to-all-start = ((bf16[8,64,128]{2,1,0:T(8,128)(2,1)}), bf16[8,64,128]{2,1,0:T(8,128)(2,1)S(1)}, u32[]{:S(2)}, u32[]{:S(2)}) async-start(bf16[8,64,128]{2,1,0:T(8,128)(2,1)} %get-tuple-element.9), calls=%async_computation | async-start | bytes 262144 | tf_op jit(solution)/shard_map/all_to_all | solution.py:360
  10.1 0.0 copy-done
  10.1 0.0 copy-done.1
  10.1 0.0 copy-done.5
  10.1 2.5 %basis.1.basis_ref = bf16[256,4096]{1,0:T(8,128)(2,1)S(1)} custom-call(bf16[2560,128]{1,0:T(8,128)(2,1)S(1)} %bitcast.10, f32[1,80]{1,0:T(1,128)S(1)} %bitcast.14, f32[80,80]{1,0:T(8,128)S(1)} %copy-done.1), custom_call_target="tpu_custom_call" | custom-call | flops 262144000 | bytes 4194304 | tf_op jit(solution)/shard_map/basis/pallas_call | solution.py:361
  12.6 0.0 copy-start.3
  12.6 0.0 copy-start.6
  12.7 0.0 copy-start.7
  12.7 0.0 copy-start.8
  12.7 4.8 %all-to-all-done.in_ref.refs_0_ = bf16[8,64,128]{2,1,0:T(8,128)(2,1)S(1)} async-done(((bf16[8,64,128]{2,1,0:T(8,128)(2,1)}), bf16[8,64,128]{2,1,0:T(8,128)(2,1)S(1)}, u32[]{:S(2)}, u32[]{:S(2)}) %all-to-all-start) | async-done | bytes 131104 | tf_op jit(solution)/shard_map/all_to_all | solution.py:360
  17.5 0.0 collective-permute-start
  17.5 1.0 %price_own_half.1.refs_2_ = bf16[384,4096]{1,0:T(8,128)(2,1)S(1)} custom-call(bf16[256,4096]{1,0:T(8,128)(2,1)S(1)} %basis.1.basis_ref, bf16[8,64,128]{2,1,0:T(8,128)(2,1)S(1)} %all-to-all-done.in_ref.refs_0_), custom_call_target="tpu_custom_call" | custom-call | flops 805306368 | bytes 6291456 | tf_op jit(solution)/shard_map/price_own_half/pallas_call | solution.py:386
  18.5 0.0 copy-start.2
  18.5 0.0 copy-start.4
  18.5 0.3 collective-permute-done.refs_1_
  18.8 0.0 copy-done.3
  18.8 0.0 copy-done.6
  18.8 0.0 copy-done.7
  18.8 0.0 copy-done.8
  18.8 4.2 %value_and_allocate.1 = f32[32,1,128]{2,1,0:T(1,128)S(1)} custom-call(s32[1]{0:T(128)} %bitcast.me_ref, s32[8]{0:T(128)S(1)} %copy-done.6, s32[4]{0:T(128)S(1)} %copy-done.7, s32[4]{0:T(128)S(1)} %copy-done.8, f32[4,32]{1,0:T(4,128)S(1)} %copy-done.3, bf16[256,4096]{1,0:T(8,128)(2,1)S(1)} %basis.1.basis_ref, ...), custom_call_target="tpu_custom_call" | custom-call | tf_op jit(solution)/shard_map/value_and_allocate/pallas_call | solution.py:400
  23.0 9.3 %all_to_all.10 = f32[32,1,128]{2,1,0:T(1,128)S(1)} all-to-all(f32[32,1,128]{2,1,0:T(1,128)S(1)} %value_and_allocate.1), channel_id=1, replica_groups=mesh['trade'=8,'path'=4] {'trade','path'}, dimensions={0} | all-to-all | bytes 32768 | tf_op jit(solution)/shard_map/all_to_all | solution.py:410
  32.3 0.0 copy-done.2
  32.3 0.0 copy-done.4
  32.3 0.8 %finish.1 = (f32[1,512]{1,0:T(1,128)}, f32[1,4]{1,0:T(1,128)}) custom-call(s32[1]{0:T(128)} %bitcast.me_ref, f32[8,512]{1,0:T(8,128)S(1)} %copy-done.2, f32[4,128]{1,0:T(4,128)S(1)} %bitcast.13, f32[32,128]{1,0:T(8,128)S(1)} %bitcast.11), custom_call_target="tpu_custom_call" | custom-call | tf_op jit(solution)/shard_map/finish/pallas_call | solution.py:412
Async XLA Ops:
  0.6 9.5 %copy-start = (bf16[80,32,128]{2,1,0:T(8,128)(2,1)S(1)}, bf16[80,32,128]{2,1,0:T(8,128)(2,1)}, u32[]{:S(2)}) copy-start(bf16[80,32,128]{2,1,0:T(8,128)(2,1)} %param.10) | copy-start | bytes 1966084
  0.6 9.5 %copy-start.1 = (f32[80,80]{1,0:T(8,128)S(1)}, f32[80,80]{1,0:T(8,128)}, u32[]{:S(2)}) copy-start(f32[80,80]{1,0:T(8,128)} %loading_hbm.1) | copy-start | bytes 76804
  0.7 9.5 %copy-start.5 = (f32[80]{0:T(128)S(1)}, f32[80]{0:T(128)}, u32[]{:S(2)}) copy-start(f32[80]{0:T(128)} %param.11) | copy-start | bytes 964
  2.8 14.6 %all-to-all-start = ((bf16[8,64,128]{2,1,0:T(8,128)(2,1)}), bf16[8,64,128]{2,1,0:T(8,128)(2,1)S(1)}, u32[]{:S(2)}, u32[]{:S(2)}) async-start(bf16[8,64,128]{2,1,0:T(8,128)(2,1)} %get-tuple-element.9), calls=%async_computation | async-start | bytes 262144 | tf_op jit(solution)/shard_map/all_to_all | solution.py:360
  12.6 6.2 %copy-start.3 = (f32[4,32]{1,0:T(4,128)S(1)}, f32[4,32]{1,0:T(4,128)}, u32[]{:S(2)}) copy-start(f32[4,32]{1,0:T(4,128)} %weight_ref.1) | copy-start | bytes 1540
  12.6 6.2 %copy-start.6 = (s32[8]{0:T(128)S(1)}, s32[8]{0:T(128)}, u32[]{:S(2)}) copy-start(s32[8]{0:T(128)} %agr_ref.1) | copy-start | bytes 100
  12.7 6.2 %copy-start.7 = (s32[4]{0:T(128)S(1)}, s32[4]{0:T(128)}, u32[]{:S(2)}) copy-start(s32[4]{0:T(128)} %cpty_ref.1) | copy-start | bytes 52
  12.7 6.2 %copy-start.8 = (s32[4]{0:T(128)S(1)}, s32[4]{0:T(128)}, u32[]{:S(2)}) copy-start(s32[4]{0:T(128)} %lag_ref.1) | copy-start | bytes 52
  17.5 1.3 %collective-permute-start = (bf16[8,64,128]{2,1,0:T(8,128)(2,1)S(1)}, bf16[8,64,128]{2,1,0:T(8,128)(2,1)S(1)}, u32[]{:S(2)}, u32[]{:S(2)}) collective-permute-start(bf16[8,64,128]{2,1,0:T(8,128)(2,1)S(1)} %all-to-all-done.in_ref.refs_0_), channel_id=1, source_target_pairs={{0,1},{1,0},{2,3},{3,2},{4,5},{5,4},{6,7},{7,6},{8,9},{9,8},{10,11... | collective-permute-start | bytes 393224 | tf_op jit(solution)/shard_map/ppermute | solution.py:384
  18.5 13.9 %copy-start.2 = (f32[8,512]{1,0:T(8,128)S(1)}, f32[8,512]{1,0:T(8,128)}, u32[]{:S(2)}) copy-start(f32[8,512]{1,0:T(8,128)} %get-tuple-element.8.place_ref) | copy-start | bytes 49156
  18.5 13.9 %copy-start.4 = (f32[512]{0:T(512)S(1)}, f32[512]{0:T(512)}, u32[]{:S(2)}) copy-start(f32[512]{0:T(512)} %param.14) | copy-start | bytes 6148

commit v17 on v15

--- a/solution.py
+++ b/solution.py
@@ -73,17 +73,12 @@
         self.step = 2048 if self.trades <= 1024 else 512
 
 
-def pack_kernel(plan, me_ref, half_ref, sets_hbm, coef_hbm, notional_hbm, place_ref, out_ref, *refs):
-    sets_ref, coef_ref, notional_ref, sems = refs
-    copies = fetch(
-        [sets_hbm, notional_hbm, coef_hbm], [sets_ref, notional_ref, coef_ref], sems
-    )
+def pack_kernel(plan, me_ref, half_ref, sets_ref, coef_ref, notional_ref, place_ref, out_ref):
     me = me_ref[0]
     owners, part, room, extra = plan.owners, plan.part, plan.room, plan.extra
     lines = notional_ref.shape[0]
     rows = lines * LANES
     shared = SUBS // lines
-    copies[0].wait()
     block = sets_ref[pl.ds(pl.multiple_of(me // shared * SUBS, SUBS), SUBS), :]
     own = block[0:lines]
     for b in range(1, shared):
@@ -101,13 +96,11 @@
     mine = rank.astype(jnp.int32) - room * half_ref[0]
     spot = jnp.where((mine >= 0) & (mine < room), key * room + mine, -1)
     chosen = mask_bf16(iota((owners * room, rows), 0) == spot)
-    copies[1].wait()
     notional = in_a_row(notional_ref[...])
     high = notional.astype(BF16).astype(F32)
     info = jnp.concatenate(
         [high, notional - high, local.astype(F32), jnp.zeros((13, rows), F32)], axis=0
     )
-    copies[2].wait()
     table = jnp.concatenate([coef_ref[...], info.astype(BF16)], axis=0)
     moved = lax.dot_general(chosen, table, BOTH_LANES, preferred_element_type=F32)
     ids = LANES + extra
@@ -226,12 +219,8 @@
     netting = jnp.where(hot, jnp.where(row < AG_DEV, info[0:1], info[1:2]), 0.0).astype(BF16)
 
     price(plan, left, basis_ref, val_ref)
-    size = val_ref.shape[0]
-    both = jnp.zeros((SUBS, val_ref.shape[1]), F32)
-    for h, values in enumerate(val_refs):
-        both = both + jnp.dot(
-            netting[:, size * h : size * (h + 1)], values[...], preferred_element_type=F32
-        )
+    values = jnp.concatenate([ref[...] for ref in val_refs], axis=0)
+    both = jnp.dot(netting, values, preferred_element_type=F32)
     both = both + pltpu.roll(both, AG_DEV, 0)
     owed = [both[:, LANES * t : LANES * (t + 1)] for t in range(dates)]
 
@@ -265,11 +254,8 @@
         grads.append(((slopes[t] - after) * (1.0 / path_total)).astype(BF16))
 
     grads = jnp.concatenate(grads, axis=1)
-    dots = [
-        lax.dot_general(grads, values[...], BOTH_LANES, preferred_element_type=F32)
-        for values in val_refs
-    ]
-    dots = jnp.concatenate(dots, axis=1)
+    values = jnp.concatenate([ref[...] for ref in val_refs], axis=0)
+    dots = lax.dot_general(grads, values, BOTH_LANES, preferred_element_type=F32)
     share = jnp.sum(jnp.where(hot & (row < AG_DEV), dots, 0.0), axis=0, keepdims=True)
     spent = jnp.sum(spent, axis=1, keepdims=True) * (1.0 / path_total)
     mine = (lane - plan.slots == cpty) & (iota((SUBS, LANES), 0) < AG_DEV)
@@ -346,14 +332,8 @@
             jax.ShapeDtypeStruct((SUBS, rows), F32),
             jax.ShapeDtypeStruct((owners, plan.height, LANES), BF16),
         ],
-        in_specs=[SMEM] * 2 + [HBM] * 3,
+        in_specs=[SMEM] * 2 + [VMEM] * 3,
         out_specs=[VMEM, VMEM],
-        scratch_shapes=[
-            pltpu.VMEM((owners * lines, LANES), jnp.int32),
-            pltpu.VMEM((2 * tenors, rows), BF16),
-            pltpu.VMEM((lines, LANES), F32),
-            pltpu.SemaphoreType.DMA((3,)),
-        ],
         name="pack",
         cost_estimate=pl.CostEstimate(flops=1 << 32, bytes_accessed=1 << 19, transcendentals=0),
     )(me, half, ns_of_trade.reshape(owners * lines, LANES), coefficient.T, notional)

time: 33.4 us -> 33.8 us (1.012)
  Pallas kernels: 10.6 us -> 11 us
    pallas_call x1, Pallas kernels: 4.16 us -> 4.62 us  [body(): pl.pallas_call(functools.partial(main_kernel, plan, path_total), out_shap...]
  transfers between devices with their start and end apart: 2 -> 2, of which waited for: 2 -> 2; matrix products, arithmetic and copies ran while one was open for 0% -> 0% of each run, Pallas kernels for 11% -> 10%
where the time goes in v17:
time: 33.8 us; the launch traced here: 33.6 us
  Pallas kernels  11 us (33%)
  blocking collectives  9.34 us (28%)
  starting transfers between devices  7.28 us (22%)
  waiting for transfers between devices  5.1 us (15%)
  between operations  0.76 us (2%)
    all_to_all x1, blocking collectives, body(): lax.all_to_all(lines_out, ('trade', 'path'), split_axis=0, concat_axis=0,...  9.34 us
    all_to_all x1, starting transfers between devices, body(): lax.all_to_all(outgoing, 'trade', split_axis=0, concat_axis=0, tiled=True)  7.28 us
    all_to_all x1, waiting for transfers between devices, body(): lax.all_to_all(outgoing, 'trade', split_axis=0, concat_axis=0, tiled=True)  4.78 us
    pallas_call x1, Pallas kernels, body(): pl.pallas_call(functools.partial(main_kernel, plan, path_total), out_shap...  4.62 us
    pallas_call x1, Pallas kernels, body(): pl.pallas_call(functools.partial(basis_kernel, plan), out_shape=jax.Shape...  2.48 us
    pallas_call x1, Pallas kernels, body(): pl.pallas_call(functools.partial(pack_kernel, plan), out_shape=[jax.Shape...  2.12 us
    pallas_call x1, Pallas kernels, body(): pl.pallas_call(functools.partial(price_kernel, plan), out_shape=jax.Shape...  1 us
    pallas_call x1, Pallas kernels, body(): pl.pallas_call(functools.partial(finish_kernel, plan), out_shape=[jax.Sha...  0.81 us
  transfers between devices with their start and end apart: 2, of which 2 were waited for; matrix products, arithmetic and copies ran while one was open for 0% of the time, Pallas kernels for 10%

profile of v17, /device:TPU:0, one launch (start us, length us, event | category | flops | bytes accessed | tf_op | source)
XLA Modules:
  0.0 33.6 jit_solution(17452030359179975421)
XLA Ops:
  0.6 0.0 copy-start
  0.6 0.0 copy-start.1
  0.7 0.0 copy-start.5
  0.7 2.1 %pack.1 = (f32[8,512]{1,0:T(8,128)}, bf16[8,64,128]{2,1,0:T(8,128)(2,1)}) custom-call(s32[1]{0:T(128)} %bitcast.me_ref, s32[1]{0:T(128)} %bitcast.1.half_ref, s32[32,128]{1,0:T(8,128)} %bitcast.16, bf16[160,512]{1,0:T(8,128)(2,1)} %bitcast.15, f32[4,128]{1,0:T(4,128)} %bitcast.12), custom_call_target="tpu_custom_call" | custom-call | flops 4294967296 | bytes 524288 | tf_op jit(solution)/shard_map/pack/pallas_call | solution.py:329
  2.8 7.3 %all-to-all-start = ((bf16[8,64,128]{2,1,0:T(8,128)(2,1)}), bf16[8,64,128]{2,1,0:T(8,128)(2,1)S(1)}, u32[]{:S(2)}, u32[]{:S(2)}) async-start(bf16[8,64,128]{2,1,0:T(8,128)(2,1)} %get-tuple-element.9), calls=%async_computation | async-start | bytes 262144 | tf_op jit(solution)/shard_map/all_to_all | solution.py:340
  10.1 0.0 copy-done
  10.1 0.0 copy-done.1
  10.1 0.0 copy-done.5
  10.1 2.5 %basis.1.basis_ref = bf16[256,4096]{1,0:T(8,128)(2,1)S(1)} custom-call(bf16[2560,128]{1,0:T(8,128)(2,1)S(1)} %bitcast.10, f32[1,80]{1,0:T(1,128)S(1)} %bitcast.14, f32[80,80]{1,0:T(8,128)S(1)} %copy-done.1), custom_call_target="tpu_custom_call" | custom-call | flops 262144000 | bytes 4194304 | tf_op jit(solution)/shard_map/basis/pallas_call | solution.py:341
  12.6 0.0 copy-start.3
  12.6 0.0 copy-start.6
  12.6 0.0 copy-start.7
  12.6 0.0 copy-start.8
  12.6 4.8 %all-to-all-done.in_ref.refs_0_ = bf16[8,64,128]{2,1,0:T(8,128)(2,1)S(1)} async-done(((bf16[8,64,128]{2,1,0:T(8,128)(2,1)}), bf16[8,64,128]{2,1,0:T(8,128)(2,1)S(1)}, u32[]{:S(2)}, u32[]{:S(2)}) %all-to-all-start) | async-done | bytes 131104 | tf_op jit(solution)/shard_map/all_to_all | solution.py:340
  17.4 0.0 collective-permute-start
  17.4 1.0 %price_own_half.1.refs_2_ = bf16[384,4096]{1,0:T(8,128)(2,1)S(1)} custom-call(bf16[256,4096]{1,0:T(8,128)(2,1)S(1)} %basis.1.basis_ref, bf16[8,64,128]{2,1,0:T(8,128)(2,1)S(1)} %all-to-all-done.in_ref.refs_0_), custom_call_target="tpu_custom_call" | custom-call | flops 805306368 | bytes 6291456 | tf_op jit(solution)/shard_map/price_own_half/pallas_call | solution.py:366
  18.4 0.0 copy-start.2
  18.4 0.0 copy-start.4
  18.4 0.3 collective-permute-done.refs_1_
  18.8 0.0 copy-done.3
  18.8 0.0 copy-done.6
  18.8 0.0 copy-done.7
  18.8 0.0 copy-done.8
  18.8 4.6 %value_and_allocate.1 = f32[32,1,128]{2,1,0:T(1,128)S(1)} custom-call(s32[1]{0:T(128)} %bitcast.me_ref, s32[8]{0:T(128)S(1)} %copy-done.6, s32[4]{0:T(128)S(1)} %copy-done.7, s32[4]{0:T(128)S(1)} %copy-done.8, f32[4,32]{1,0:T(4,128)S(1)} %copy-done.3, bf16[256,4096]{1,0:T(8,128)(2,1)S(1)} %basis.1.basis_ref, ...), custom_call_target="tpu_custom_call" | custom-call | tf_op jit(solution)/shard_map/value_and_allocate/pallas_call | solution.py:380
  23.4 9.3 %all_to_all.10 = f32[32,1,128]{2,1,0:T(1,128)S(1)} all-to-all(f32[32,1,128]{2,1,0:T(1,128)S(1)} %value_and_allocate.1), channel_id=1, replica_groups=mesh['trade'=8,'path'=4] {'trade','path'}, dimensions={0} | all-to-all | bytes 32768 | tf_op jit(solution)/shard_map/all_to_all | solution.py:390
  32.7 0.0 copy-done.2
  32.7 0.0 copy-done.4
  32.8 0.8 %finish.1 = (f32[1,512]{1,0:T(1,128)}, f32[1,4]{1,0:T(1,128)}) custom-call(s32[1]{0:T(128)} %bitcast.me_ref, f32[8,512]{1,0:T(8,128)S(1)} %copy-done.2, f32[4,128]{1,0:T(4,128)S(1)} %bitcast.13, f32[32,128]{1,0:T(8,128)S(1)} %bitcast.11), custom_call_target="tpu_custom_call" | custom-call | tf_op jit(solution)/shard_map/finish/pallas_call | solution.py:392
Async XLA Ops:
  0.6 9.4 %copy-start = (bf16[80,32,128]{2,1,0:T(8,128)(2,1)S(1)}, bf16[80,32,128]{2,1,0:T(8,128)(2,1)}, u32[]{:S(2)}) copy-start(bf16[80,32,128]{2,1,0:T(8,128)(2,1)} %param.10) | copy-start | bytes 1966084
  0.6 9.4 %copy-start.1 = (f32[80,80]{1,0:T(8,128)S(1)}, f32[80,80]{1,0:T(8,128)}, u32[]{:S(2)}) copy-start(f32[80,80]{1,0:T(8,128)} %loading_hbm.1) | copy-start | bytes 76804
  0.7 9.4 %copy-start.5 = (f32[80]{0:T(128)S(1)}, f32[80]{0:T(128)}, u32[]{:S(2)}) copy-start(f32[80]{0:T(128)} %param.11) | copy-start | bytes 964
  2.8 14.6 %all-to-all-start = ((bf16[8,64,128]{2,1,0:T(8,128)(2,1)}), bf16[8,64,128]{2,1,0:T(8,128)(2,1)S(1)}, u32[]{:S(2)}, u32[]{:S(2)}) async-start(bf16[8,64,128]{2,1,0:T(8,128)(2,1)} %get-tuple-element.9), calls=%async_computation | async-start | bytes 262144 | tf_op jit(solution)/shard_map/all_to_all | solution.py:340
  12.6 6.2 %copy-start.3 = (f32[4,32]{1,0:T(4,128)S(1)}, f32[4,32]{1,0:T(4,128)}, u32[]{:S(2)}) copy-start(f32[4,32]{1,0:T(4,128)} %weight_ref.1) | copy-start | bytes 1540
  12.6 6.2 %copy-start.6 = (s32[8]{0:T(128)S(1)}, s32[8]{0:T(128)}, u32[]{:S(2)}) copy-start(s32[8]{0:T(128)} %agr_ref.1) | copy-start | bytes 100
  12.6 6.2 %copy-start.7 = (s32[4]{0:T(128)S(1)}, s32[4]{0:T(128)}, u32[]{:S(2)}) copy-start(s32[4]{0:T(128)} %cpty_ref.1) | copy-start | bytes 52
  12.6 6.2 %copy-start.8 = (s32[4]{0:T(128)S(1)}, s32[4]{0:T(128)}, u32[]{:S(2)}) copy-start(s32[4]{0:T(128)} %lag_ref.1) | copy-start | bytes 52
  17.4 1.3 %collective-permute-start = (bf16[8,64,128]{2,1,0:T(8,128)(2,1)S(1)}, bf16[8,64,128]{2,1,0:T(8,128)(2,1)S(1)}, u32[]{:S(2)}, u32[]{:S(2)}) collective-permute-start(bf16[8,64,128]{2,1,0:T(8,128)(2,1)S(1)} %all-to-all-done.in_ref.refs_0_), channel_id=1, source_target_pairs={{0,1},{1,0},{2,3},{3,2},{4,5},{5,4},{6,7},{7,6},{8,9},{9,8},{10,11... | collective-permute-start | bytes 393224 | tf_op jit(solution)/shard_map/ppermute | solution.py:364
  18.4 14.3 %copy-start.2 = (f32[8,512]{1,0:T(8,128)S(1)}, f32[8,512]{1,0:T(8,128)}, u32[]{:S(2)}) copy-start(f32[8,512]{1,0:T(8,128)} %get-tuple-element.8.place_ref) | copy-start | bytes 49156
  18.4 14.3 %copy-start.4 = (f32[512]{0:T(512)S(1)}, f32[512]{0:T(512)}, u32[]{:S(2)}) copy-start(f32[512]{0:T(512)} %param.14) | copy-start | bytes 6148

commit v18 on v15

--- a/solution.py
+++ b/solution.py
@@ -226,12 +226,20 @@
     netting = jnp.where(hot, jnp.where(row < AG_DEV, info[0:1], info[1:2]), 0.0).astype(BF16)
 
     price(plan, left, basis_ref, val_ref)
-    size = val_ref.shape[0]
-    both = jnp.zeros((SUBS, val_ref.shape[1]), F32)
-    for h, values in enumerate(val_refs):
-        both = both + jnp.dot(
-            netting[:, size * h : size * (h + 1)], values[...], preferred_element_type=F32
-        )
+    size, cols = val_ref.shape
+    pieces = [slice(c, c + plan.width) for c in range(0, cols, plan.width)]
+    both = []
+    for piece in pieces:
+        sums = [
+            jnp.dot(
+                netting[:, size * h : size * (h + 1)],
+                values[:, piece],
+                preferred_element_type=F32,
+            )
+            for h, values in enumerate(val_refs)
+        ]
+        both.append(sum(sums[1:], sums[0]))
+    both = jnp.concatenate(both, axis=1)
     both = both + pltpu.roll(both, AG_DEV, 0)
     owed = [both[:, LANES * t : LANES * (t + 1)] for t in range(dates)]
 
@@ -265,10 +273,15 @@
         grads.append(((slopes[t] - after) * (1.0 / path_total)).astype(BF16))
 
     grads = jnp.concatenate(grads, axis=1)
-    dots = [
-        lax.dot_general(grads, values[...], BOTH_LANES, preferred_element_type=F32)
-        for values in val_refs
-    ]
+    dots = []
+    for values in val_refs:
+        sums = [
+            lax.dot_general(
+                grads[:, piece], values[:, piece], BOTH_LANES, preferred_element_type=F32
+            )
+            for piece in pieces
+        ]
+        dots.append(sum(sums[1:], sums[0]))
     dots = jnp.concatenate(dots, axis=1)
     share = jnp.sum(jnp.where(hot & (row < AG_DEV), dots, 0.0), axis=0, keepdims=True)
     spent = jnp.sum(spent, axis=1, keepdims=True) * (1.0 / path_total)

time: 33.4 us -> 34.3 us (1.027)
  Pallas kernels: 10.6 us -> 11.5 us
    pallas_call x1, Pallas kernels: 4.16 us -> 5.08 us  [body(): pl.pallas_call(functools.partial(main_kernel, plan, path_total), out_shap...]
  transfers between devices with their start and end apart: 2 -> 2, of which waited for: 2 -> 2; matrix products, arithmetic and copies ran while one was open for 0% -> 0% of each run, Pallas kernels for 11% -> 10%
where the time goes in v18:
time: 34.3 us; the launch traced here: 34 us
  Pallas kernels  11.5 us (34%)
  blocking collectives  9.34 us (27%)
  starting transfers between devices  7.29 us (21%)
  waiting for transfers between devices  5.1 us (15%)
  between operations  0.77 us (2%)
    all_to_all x1, blocking collectives, body(): lax.all_to_all(lines_out, ('trade', 'path'), split_axis=0, concat_axis=0,...  9.34 us
    all_to_all x1, starting transfers between devices, body(): lax.all_to_all(outgoing, 'trade', split_axis=0, concat_axis=0, tiled=True)  7.29 us
    pallas_call x1, Pallas kernels, body(): pl.pallas_call(functools.partial(main_kernel, plan, path_total), out_shap...  5.08 us
    all_to_all x1, waiting for transfers between devices, body(): lax.all_to_all(outgoing, 'trade', split_axis=0, concat_axis=0, tiled=True)  4.78 us
    pallas_call x1, Pallas kernels, body(): pl.pallas_call(functools.partial(basis_kernel, plan), out_shape=jax.Shape...  2.48 us
    pallas_call x1, Pallas kernels, body(): pl.pallas_call(functools.partial(pack_kernel, plan), out_shape=[jax.Shape...  2.1 us
    pallas_call x1, Pallas kernels, body(): pl.pallas_call(functools.partial(price_kernel, plan), out_shape=jax.Shape...  1 us
    pallas_call x1, Pallas kernels, body(): pl.pallas_call(functools.partial(finish_kernel, plan), out_shape=[jax.Sha...  0.81 us
  transfers between devices with their start and end apart: 2, of which 2 were waited for; matrix products, arithmetic and copies ran while one was open for 0% of the time, Pallas kernels for 10%

profile of v18, /device:TPU:0, one launch (start us, length us, event | category | flops | bytes accessed | tf_op | source)
XLA Modules:
  0.0 34.0 jit_solution(9727768034974997783)
XLA Ops:
  0.6 0.0 copy-start
  0.6 0.0 copy-start.1
  0.7 0.0 copy-start.5
  0.7 2.1 %pack.1 = (f32[8,512]{1,0:T(8,128)}, bf16[8,64,128]{2,1,0:T(8,128)(2,1)}) custom-call(s32[1]{0:T(128)} %bitcast.me_ref, s32[1]{0:T(128)} %bitcast.1.half_ref, s32[32,128]{1,0:T(8,128)} %bitcast.16, bf16[160,512]{1,0:T(8,128)(2,1)} %bitcast.15, f32[4,128]{1,0:T(4,128)} %bitcast.12), custom_call_target="tpu_custom_call" | custom-call | flops 4294967296 | bytes 524288 | tf_op jit(solution)/shard_map/pack/pallas_call | solution.py:356
  2.8 7.3 %all-to-all-start = ((bf16[8,64,128]{2,1,0:T(8,128)(2,1)}), bf16[8,64,128]{2,1,0:T(8,128)(2,1)S(1)}, u32[]{:S(2)}, u32[]{:S(2)}) async-start(bf16[8,64,128]{2,1,0:T(8,128)(2,1)} %get-tuple-element.9), calls=%async_computation | async-start | bytes 262144 | tf_op jit(solution)/shard_map/all_to_all | solution.py:373
  10.1 0.0 copy-done
  10.1 0.0 copy-done.1
  10.1 0.0 copy-done.5
  10.1 2.5 %basis.1.basis_ref = bf16[256,4096]{1,0:T(8,128)(2,1)S(1)} custom-call(bf16[2560,128]{1,0:T(8,128)(2,1)S(1)} %bitcast.10, f32[1,80]{1,0:T(1,128)S(1)} %bitcast.14, f32[80,80]{1,0:T(8,128)S(1)} %copy-done.1), custom_call_target="tpu_custom_call" | custom-call | flops 262144000 | bytes 4194304 | tf_op jit(solution)/shard_map/basis/pallas_call | solution.py:374
  12.6 0.0 copy-start.3
  12.6 0.0 copy-start.6
  12.6 0.0 copy-start.7
  12.6 0.0 copy-start.8
  12.6 4.8 %all-to-all-done.in_ref.refs_0_ = bf16[8,64,128]{2,1,0:T(8,128)(2,1)S(1)} async-done(((bf16[8,64,128]{2,1,0:T(8,128)(2,1)}), bf16[8,64,128]{2,1,0:T(8,128)(2,1)S(1)}, u32[]{:S(2)}, u32[]{:S(2)}) %all-to-all-start) | async-done | bytes 131104 | tf_op jit(solution)/shard_map/all_to_all | solution.py:373
  17.4 0.0 collective-permute-start
  17.4 1.0 %price_own_half.1.refs_2_ = bf16[384,4096]{1,0:T(8,128)(2,1)S(1)} custom-call(bf16[256,4096]{1,0:T(8,128)(2,1)S(1)} %basis.1.basis_ref, bf16[8,64,128]{2,1,0:T(8,128)(2,1)S(1)} %all-to-all-done.in_ref.refs_0_), custom_call_target="tpu_custom_call" | custom-call | flops 805306368 | bytes 6291456 | tf_op jit(solution)/shard_map/price_own_half/pallas_call | solution.py:399
  18.4 0.0 copy-start.2
  18.4 0.0 copy-start.4
  18.4 0.3 collective-permute-done.refs_1_
  18.8 0.0 copy-done.3
  18.8 0.0 copy-done.6
  18.8 0.0 copy-done.7
  18.8 0.0 copy-done.8
  18.8 5.1 %value_and_allocate.1 = f32[32,1,128]{2,1,0:T(1,128)S(1)} custom-call(s32[1]{0:T(128)} %bitcast.me_ref, s32[8]{0:T(128)S(1)} %copy-done.6, s32[4]{0:T(128)S(1)} %copy-done.7, s32[4]{0:T(128)S(1)} %copy-done.8, f32[4,32]{1,0:T(4,128)S(1)} %copy-done.3, bf16[256,4096]{1,0:T(8,128)(2,1)S(1)} %basis.1.basis_ref, ...), custom_call_target="tpu_custom_call" | custom-call | tf_op jit(solution)/shard_map/value_and_allocate/pallas_call | solution.py:413
  23.9 9.3 %all_to_all.10 = f32[32,1,128]{2,1,0:T(1,128)S(1)} all-to-all(f32[32,1,128]{2,1,0:T(1,128)S(1)} %value_and_allocate.1), channel_id=1, replica_groups=mesh['trade'=8,'path'=4] {'trade','path'}, dimensions={0} | all-to-all | bytes 32768 | tf_op jit(solution)/shard_map/all_to_all | solution.py:423
  33.2 0.0 copy-done.2
  33.2 0.0 copy-done.4
  33.2 0.8 %finish.1 = (f32[1,512]{1,0:T(1,128)}, f32[1,4]{1,0:T(1,128)}) custom-call(s32[1]{0:T(128)} %bitcast.me_ref, f32[8,512]{1,0:T(8,128)S(1)} %copy-done.2, f32[4,128]{1,0:T(4,128)S(1)} %bitcast.13, f32[32,128]{1,0:T(8,128)S(1)} %bitcast.11), custom_call_target="tpu_custom_call" | custom-call | tf_op jit(solution)/shard_map/finish/pallas_call | solution.py:425
Async XLA Ops:
  0.6 9.4 %copy-start = (bf16[80,32,128]{2,1,0:T(8,128)(2,1)S(1)}, bf16[80,32,128]{2,1,0:T(8,128)(2,1)}, u32[]{:S(2)}) copy-start(bf16[80,32,128]{2,1,0:T(8,128)(2,1)} %param.10) | copy-start | bytes 1966084
  0.6 9.4 %copy-start.1 = (f32[80,80]{1,0:T(8,128)S(1)}, f32[80,80]{1,0:T(8,128)}, u32[]{:S(2)}) copy-start(f32[80,80]{1,0:T(8,128)} %loading_hbm.1) | copy-start | bytes 76804
  0.7 9.4 %copy-start.5 = (f32[80]{0:T(128)S(1)}, f32[80]{0:T(128)}, u32[]{:S(2)}) copy-start(f32[80]{0:T(128)} %param.11) | copy-start | bytes 964
  2.8 14.6 %all-to-all-start = ((bf16[8,64,128]{2,1,0:T(8,128)(2,1)}), bf16[8,64,128]{2,1,0:T(8,128)(2,1)S(1)}, u32[]{:S(2)}, u32[]{:S(2)}) async-start(bf16[8,64,128]{2,1,0:T(8,128)(2,1)} %get-tuple-element.9), calls=%async_computation | async-start | bytes 262144 | tf_op jit(solution)/shard_map/all_to_all | solution.py:373
  12.6 6.2 %copy-start.3 = (f32[4,32]{1,0:T(4,128)S(1)}, f32[4,32]{1,0:T(4,128)}, u32[]{:S(2)}) copy-start(f32[4,32]{1,0:T(4,128)} %weight_ref.1) | copy-start | bytes 1540
  12.6 6.2 %copy-start.6 = (s32[8]{0:T(128)S(1)}, s32[8]{0:T(128)}, u32[]{:S(2)}) copy-start(s32[8]{0:T(128)} %agr_ref.1) | copy-start | bytes 100
  12.6 6.2 %copy-start.7 = (s32[4]{0:T(128)S(1)}, s32[4]{0:T(128)}, u32[]{:S(2)}) copy-start(s32[4]{0:T(128)} %cpty_ref.1) | copy-start | bytes 52
  12.6 6.2 %copy-start.8 = (s32[4]{0:T(128)S(1)}, s32[4]{0:T(128)}, u32[]{:S(2)}) copy-start(s32[4]{0:T(128)} %lag_ref.1) | copy-start | bytes 52
  17.4 1.3 %collective-permute-start = (bf16[8,64,128]{2,1,0:T(8,128)(2,1)S(1)}, bf16[8,64,128]{2,1,0:T(8,128)(2,1)S(1)}, u32[]{:S(2)}, u32[]{:S(2)}) collective-permute-start(bf16[8,64,128]{2,1,0:T(8,128)(2,1)S(1)} %all-to-all-done.in_ref.refs_0_), channel_id=1, source_target_pairs={{0,1},{1,0},{2,3},{3,2},{4,5},{5,4},{6,7},{7,6},{8,9},{9,8},{10,11... | collective-permute-start | bytes 393224 | tf_op jit(solution)/shard_map/ppermute | solution.py:397
  18.4 14.8 %copy-start.2 = (f32[8,512]{1,0:T(8,128)S(1)}, f32[8,512]{1,0:T(8,128)}, u32[]{:S(2)}) copy-start(f32[8,512]{1,0:T(8,128)} %get-tuple-element.8.place_ref) | copy-start | bytes 49156
  18.4 14.8 %copy-start.4 = (f32[512]{0:T(512)S(1)}, f32[512]{0:T(512)}, u32[]{:S(2)}) copy-start(f32[512]{0:T(512)} %param.14) | copy-start | bytes 6148

commit v19 on v15

--- a/solution.py
+++ b/solution.py
@@ -195,43 +195,52 @@
         val_ref[:, cols] = jnp.maximum(under.astype(BF16), 0)
 
 
-def price_kernel(plan, basis_ref, in_ref, val_ref):
-    price(plan, left_side(plan, in_ref)[0], basis_ref, val_ref)
-
-
-def main_kernel(plan, path_total, me_ref, agr_ref, cpty_ref, lag_ref, weight_ref, basis_ref, *refs):
-    *in_refs, out_ref, val_ref = refs
-    val_refs = [val_ref]
-    if plan.halves == 2:
-        val_refs = [in_refs.pop(), val_ref]
-    me = me_ref[0]
-    part, room, dates = plan.part, plan.room, plan.dates
-    cpty_dev = weight_ref.shape[0]
-
-    lane = iota((1, LANES), 1)
+def membership(plan, me, agr_ref, rest):
     info = []
-    for in_ref in in_refs:
-        left, rest = left_side(plan, in_ref)
-        for g in range(plan.groups):
-            first = 3 * plan.extra + SUBS * g
-            pick = mask_bf16(iota((SUBS, LANES), 1) == first + iota((SUBS, LANES), 0))
-            info.append(lax.dot_general(pick, rest, BOTH_LANES, preferred_element_type=F32))
+    for g in range(plan.groups):
+        first = 3 * plan.extra + SUBS * g
+        pick = mask_bf16(iota((SUBS, LANES), 1) == first + iota((SUBS, LANES), 0))
+        info.append(lax.dot_general(pick, rest, BOTH_LANES, preferred_element_type=F32))
     info = jnp.concatenate(info, axis=1)
     local = info[2:3].astype(jnp.int32)
     agr = jnp.zeros_like(local)
     for n in range(NS_DEV):
         agr = jnp.where(local == n, agr_ref[n] - me * AG_DEV, agr)
-    row = iota((SUBS, plan.trades), 0)
+    row = iota((SUBS, info.shape[1]), 0)
     hot = (row & (AG_DEV - 1)) == agr
     netting = jnp.where(hot, jnp.where(row < AG_DEV, info[0:1], info[1:2]), 0.0).astype(BF16)
-
+    return hot & (row < AG_DEV), netting
+
+
+def price_kernel(plan, me_ref, agr_ref, basis_ref, in_ref, val_ref, sum_ref):
+    left, rest = left_side(plan, in_ref)
+    netting = membership(plan, me_ref[0], agr_ref, rest)[1]
     price(plan, left, basis_ref, val_ref)
-    size = val_ref.shape[0]
-    both = jnp.zeros((SUBS, val_ref.shape[1]), F32)
-    for h, values in enumerate(val_refs):
-        both = both + jnp.dot(
-            netting[:, size * h : size * (h + 1)], values[...], preferred_element_type=F32
-        )
+    sum_ref[...] = jnp.dot(netting, val_ref[...], preferred_element_type=F32)
+
+
+def main_kernel(plan, path_total, me_ref, agr_ref, cpty_ref, lag_ref, weight_ref, basis_ref, *refs):
+    *in_refs, out_ref, val_ref = refs
+    val_refs = [val_ref]
+    if plan.halves == 2:
+        *in_refs, own_ref, sum_ref = in_refs
+        val_refs = [own_ref, val_ref]
+    me = me_ref[0]
+    part, room, dates = plan.part, plan.room, plan.dates
+    cpty_dev = weight_ref.shape[0]
+
+    lane = iota((1, LANES), 1)
+    hot = []
+    for in_ref in in_refs:
+        left, rest = left_side(plan, in_ref)
+        member, netting = membership(plan, me, agr_ref, rest)
+        hot.append(member)
+    hot = jnp.concatenate([member.astype(F32) for member in hot], axis=1)
+
+    price(plan, left, basis_ref, val_ref)
+    both = jnp.dot(netting, val_ref[...], preferred_element_type=F32)
+    if plan.halves == 2:
+        both = both + sum_ref[...]
     both = both + pltpu.roll(both, AG_DEV, 0)
     owed = [both[:, LANES * t : LANES * (t + 1)] for t in range(dates)]
 
@@ -270,7 +279,7 @@
         for values in val_refs
     ]
     dots = jnp.concatenate(dots, axis=1)
-    share = jnp.sum(jnp.where(hot & (row < AG_DEV), dots, 0.0), axis=0, keepdims=True)
+    share = jnp.sum(hot * dots, axis=0, keepdims=True)
     spent = jnp.sum(spent, axis=1, keepdims=True) * (1.0 / path_total)
     mine = (lane - plan.slots == cpty) & (iota((SUBS, LANES), 0) < AG_DEV)
     cva = jnp.sum(jnp.where(mine, spent, 0.0), axis=0, keepdims=True)
@@ -382,18 +391,21 @@
         incoming[0], basis = lax.optimization_barrier((incoming[0], basis))
         pairs = [(p, p ^ 1) for p in range(path_parts)]
         incoming.append(lax.ppermute(incoming[0], "path", pairs))
-        incoming.append(
+        incoming.extend(
             pl.pallas_call(
                 functools.partial(price_kernel, plan),
-                out_shape=jax.ShapeDtypeStruct((half_trades, cols), BF16),
-                in_specs=[VMEM] * 2,
-                out_specs=VMEM,
+                out_shape=[
+                    jax.ShapeDtypeStruct((half_trades, cols), BF16),
+                    jax.ShapeDtypeStruct((SUBS, cols), F32),
+                ],
+                in_specs=[SMEM] * 2 + [VMEM] * 2,
+                out_specs=[VMEM, VMEM],
                 name="price_own_half",
                 compiler_params=pltpu.CompilerParams(vmem_limit_bytes=24 << 20),
                 cost_estimate=pl.CostEstimate(
                     flops=4 * half_trades * LANES * cols, bytes_accessed=6 << 20, transcendentals=0
                 ),
-            )(basis, incoming[0])
+            )(me, agr_of_ns, basis, incoming[0])
         )
 
     need = 2 * plan.trades * cols + 8 * plan.trades * plan.step + (8 << 20)

time: 33.4 us -> 33.9 us (1.015)
  Pallas kernels: 10.6 us -> 11.1 us
    pallas_call x1, Pallas kernels: 1 us -> 1.95 us  [body(): pl.pallas_call(functools.partial(price_kernel, plan), out_shape=[jax.Shap...]
    pallas_call x1, Pallas kernels: 4.16 us -> 3.77 us  [body(): pl.pallas_call(functools.partial(main_kernel, plan, path_total), out_shap...]
  transfers between devices with their start and end apart: 2 -> 2, of which waited for: 2 -> 1; matrix products, arithmetic and copies ran while one was open for 0% -> 0% of each run, Pallas kernels for 11% -> 13%
where the time goes in v19:
time: 33.9 us; the launch traced here: 33.6 us
  Pallas kernels  11.1 us (33%)
  blocking collectives  9.45 us (28%)
  starting transfers between devices  7.42 us (22%)
  waiting for transfers between devices  4.83 us (14%)
  between operations  0.77 us (2%)
    all_to_all x1, blocking collectives, body(): lax.all_to_all(lines_out, ('trade', 'path'), split_axis=0, concat_axis=0,...  9.45 us
    all_to_all x1, starting transfers between devices, body(): lax.all_to_all(outgoing, 'trade', split_axis=0, concat_axis=0, tiled=True)  7.42 us
    all_to_all x1, waiting for transfers between devices, body(): lax.all_to_all(outgoing, 'trade', split_axis=0, concat_axis=0, tiled=True)  4.82 us
    pallas_call x1, Pallas kernels, body(): pl.pallas_call(functools.partial(main_kernel, plan, path_total), out_shap...  3.77 us
    pallas_call x1, Pallas kernels, body(): pl.pallas_call(functools.partial(basis_kernel, plan), out_shape=jax.Shape...  2.49 us
    pallas_call x1, Pallas kernels, body(): pl.pallas_call(functools.partial(pack_kernel, plan), out_shape=[jax.Shape...  2.1 us
    pallas_call x1, Pallas kernels, body(): pl.pallas_call(functools.partial(price_kernel, plan), out_shape=[jax.Shap...  1.95 us
    pallas_call x1, Pallas kernels, body(): pl.pallas_call(functools.partial(finish_kernel, plan), out_shape=[jax.Sha...  0.81 us
  transfers between devices with their start and end apart: 2, of which 1 were waited for; matrix products, arithmetic and copies ran while one was open for 0% of the time, Pallas kernels for 13%

profile of v19, /device:TPU:0, one launch (start us, length us, event | category | flops | bytes accessed | tf_op | source)
XLA Modules:
  0.0 33.6 jit_solution(16676043901105036410)
XLA Ops:
  0.6 0.0 copy-start
  0.6 0.0 copy-start.1
  0.7 0.0 copy-start.5
  0.7 0.0 copy-start.6
  0.7 2.1 %pack.1 = (f32[8,512]{1,0:T(8,128)}, bf16[8,64,128]{2,1,0:T(8,128)(2,1)}) custom-call(s32[1]{0:T(128)} %bitcast.me_ref, s32[1]{0:T(128)} %bitcast.1.half_ref, s32[32,128]{1,0:T(8,128)} %bitcast.16, bf16[160,512]{1,0:T(8,128)(2,1)} %bitcast.15, f32[4,128]{1,0:T(4,128)} %bitcast.12), custom_call_target="tpu_custom_call" | custom-call | flops 4294967296 | bytes 524288 | tf_op jit(solution)/shard_map/pack/pallas_call | solution.py:352
  2.8 0.0 copy-start.3
  2.8 0.0 copy-start.7
  2.8 0.0 copy-start.8
  2.8 7.4 %all-to-all-start = ((bf16[8,64,128]{2,1,0:T(8,128)(2,1)}), bf16[8,64,128]{2,1,0:T(8,128)(2,1)S(1)}, u32[]{:S(2)}, u32[]{:S(2)}) async-start(bf16[8,64,128]{2,1,0:T(8,128)(2,1)} %get-tuple-element.11), calls=%async_computation | async-start | bytes 262144 | tf_op jit(solution)/shard_map/all_to_all | solution.py:369
  10.2 0.0 copy-done
  10.2 0.0 copy-done.1
  10.3 0.0 copy-done.5
  10.3 2.5 %basis.1.basis_ref = bf16[256,4096]{1,0:T(8,128)(2,1)S(1)} custom-call(bf16[2560,128]{1,0:T(8,128)(2,1)S(1)} %bitcast.10, f32[1,80]{1,0:T(1,128)S(1)} %bitcast.14, f32[80,80]{1,0:T(8,128)S(1)} %copy-done.1), custom_call_target="tpu_custom_call" | custom-call | flops 262144000 | bytes 4194304 | tf_op jit(solution)/shard_map/basis/pallas_call | solution.py:370
  12.8 4.8 %all-to-all-done.in_ref.refs_0_ = bf16[8,64,128]{2,1,0:T(8,128)(2,1)S(1)} async-done(((bf16[8,64,128]{2,1,0:T(8,128)(2,1)}), bf16[8,64,128]{2,1,0:T(8,128)(2,1)S(1)}, u32[]{:S(2)}, u32[]{:S(2)}) %all-to-all-start) | async-done | bytes 131104 | tf_op jit(solution)/shard_map/all_to_all | solution.py:369
  17.6 0.0 collective-permute-start
  17.6 0.0 copy-done.6
  17.6 1.9 %price_own_half.1 = (bf16[384,4096]{1,0:T(8,128)(2,1)S(1)}, f32[8,4096]{1,0:T(8,128)S(1)}) custom-call(s32[1]{0:T(128)} %bitcast.me_ref, s32[8]{0:T(128)S(1)} %copy-done.6, bf16[256,4096]{1,0:T(8,128)(2,1)S(1)} %basis.1.basis_ref, bf16[8,64,128]{2,1,0:T(8,128)(2,1)S(1)} %all-to-all-done.in_ref.refs_0_), custom_call_target="tpu_custom_call" | custom-call | flops 805306368 | bytes 6291456 | tf_op jit(solution)/shard_map/price_own_half/pallas_call | solution.py:395
  19.5 0.0 copy-start.2
  19.5 0.0 copy-start.4
  19.5 0.0 collective-permute-done.refs_1_
  19.6 0.0 copy-done.3
  19.6 0.0 copy-done.7
  19.6 0.0 copy-done.8
  19.6 3.8 %value_and_allocate.1 = f32[32,1,128]{2,1,0:T(1,128)S(1)} custom-call(s32[1]{0:T(128)} %bitcast.me_ref, s32[8]{0:T(128)S(1)} %copy-done.6, s32[4]{0:T(128)S(1)} %copy-done.7, s32[4]{0:T(128)S(1)} %copy-done.8, f32[4,32]{1,0:T(4,128)S(1)} %copy-done.3, bf16[256,4096]{1,0:T(8,128)(2,1)S(1)} %basis.1.basis_ref, ...), custom_call_target="tpu_custom_call" | custom-call | tf_op jit(solution)/shard_map/value_and_allocate/pallas_call | solution.py:412
  23.4 9.5 %all_to_all.10 = f32[32,1,128]{2,1,0:T(1,128)S(1)} all-to-all(f32[32,1,128]{2,1,0:T(1,128)S(1)} %value_and_allocate.1), channel_id=1, replica_groups=mesh['trade'=8,'path'=4] {'trade','path'}, dimensions={0} | all-to-all | bytes 32768 | tf_op jit(solution)/shard_map/all_to_all | solution.py:422
  32.8 0.0 copy-done.2
  32.8 0.0 copy-done.4
  32.8 0.8 %finish.1 = (f32[1,512]{1,0:T(1,128)}, f32[1,4]{1,0:T(1,128)}) custom-call(s32[1]{0:T(128)} %bitcast.me_ref, f32[8,512]{1,0:T(8,128)S(1)} %copy-done.2, f32[4,128]{1,0:T(4,128)S(1)} %bitcast.13, f32[32,128]{1,0:T(8,128)S(1)} %bitcast.11), custom_call_target="tpu_custom_call" | custom-call | tf_op jit(solution)/shard_map/finish/pallas_call | solution.py:424
Async XLA Ops:
  0.6 9.6 %copy-start = (bf16[80,32,128]{2,1,0:T(8,128)(2,1)S(1)}, bf16[80,32,128]{2,1,0:T(8,128)(2,1)}, u32[]{:S(2)}) copy-start(bf16[80,32,128]{2,1,0:T(8,128)(2,1)} %param.10) | copy-start | bytes 1966084
  0.6 9.6 %copy-start.1 = (f32[80,80]{1,0:T(8,128)S(1)}, f32[80,80]{1,0:T(8,128)}, u32[]{:S(2)}) copy-start(f32[80,80]{1,0:T(8,128)} %loading_hbm.1) | copy-start | bytes 76804
  0.7 9.6 %copy-start.5 = (f32[80]{0:T(128)S(1)}, f32[80]{0:T(128)}, u32[]{:S(2)}) copy-start(f32[80]{0:T(128)} %param.11) | copy-start | bytes 964
  0.7 16.9 %copy-start.6 = (s32[8]{0:T(128)S(1)}, s32[8]{0:T(128)}, u32[]{:S(2)}) copy-start(s32[8]{0:T(128)} %agr_ref.3) | copy-start | bytes 100
  2.8 16.8 %copy-start.3 = (f32[4,32]{1,0:T(4,128)S(1)}, f32[4,32]{1,0:T(4,128)}, u32[]{:S(2)}) copy-start(f32[4,32]{1,0:T(4,128)} %weight_ref.1) | copy-start | bytes 1540
  2.8 16.8 %copy-start.7 = (s32[4]{0:T(128)S(1)}, s32[4]{0:T(128)}, u32[]{:S(2)}) copy-start(s32[4]{0:T(128)} %cpty_ref.1) | copy-start | bytes 52
  2.8 16.8 %copy-start.8 = (s32[4]{0:T(128)S(1)}, s32[4]{0:T(128)}, u32[]{:S(2)}) copy-start(s32[4]{0:T(128)} %lag_ref.1) | copy-start | bytes 52
  2.8 14.8 %all-to-all-start = ((bf16[8,64,128]{2,1,0:T(8,128)(2,1)}), bf16[8,64,128]{2,1,0:T(8,128)(2,1)S(1)}, u32[]{:S(2)}, u32[]{:S(2)}) async-start(bf16[8,64,128]{2,1,0:T(8,128)(2,1)} %get-tuple-element.11), calls=%async_computation | async-start | bytes 262144 | tf_op jit(solution)/shard_map/all_to_all | solution.py:369
  17.6 2.0 %collective-permute-start = (bf16[8,64,128]{2,1,0:T(8,128)(2,1)S(1)}, bf16[8,64,128]{2,1,0:T(8,128)(2,1)S(1)}, u32[]{:S(2)}, u32[]{:S(2)}) collective-permute-start(bf16[8,64,128]{2,1,0:T(8,128)(2,1)S(1)} %all-to-all-done.in_ref.refs_0_), channel_id=1, source_target_pairs={{0,1},{1,0},{2,3},{3,2},{4,5},{5,4},{6,7},{7,6},{8,9},{9,8},{10,11... | collective-permute-start | bytes 393224 | tf_op jit(solution)/shard_map/ppermute | solution.py:393
  19.5 13.3 %copy-start.2 = (f32[8,512]{1,0:T(8,128)S(1)}, f32[8,512]{1,0:T(8,128)}, u32[]{:S(2)}) copy-start(f32[8,512]{1,0:T(8,128)} %get-tuple-element.10.place_ref) | copy-start | bytes 49156
  19.5 13.3 %copy-start.4 = (f32[512]{0:T(512)S(1)}, f32[512]{0:T(512)}, u32[]{:S(2)}) copy-start(f32[512]{0:T(512)} %param.14) | copy-start | bytes 6148

commit v20 on v15

--- a/solution.py
+++ b/solution.py
@@ -225,10 +225,11 @@
     hot = (row & (AG_DEV - 1)) == agr
     netting = jnp.where(hot, jnp.where(row < AG_DEV, info[0:1], info[1:2]), 0.0).astype(BF16)
 
-    price(plan, left, basis_ref, val_ref)
     size = val_ref.shape[0]
     both = jnp.zeros((SUBS, val_ref.shape[1]), F32)
     for h, values in enumerate(val_refs):
+        if h == len(val_refs) - 1:
+            price(plan, left, basis_ref, val_ref)
         both = both + jnp.dot(
             netting[:, size * h : size * (h + 1)], values[...], preferred_element_type=F32
         )

time: 33.4 us -> 33.4 us (level)
  no operation moved by 1% of the time
where the time goes in v20:
time: 33.4 us; the launch traced here: 33.1 us
  Pallas kernels  10.6 us (32%)
  blocking collectives  9.34 us (28%)
  starting transfers between devices  7.29 us (22%)
  waiting for transfers between devices  5.1 us (15%)
  between operations  0.77 us (2%)
    all_to_all x1, blocking collectives, body(): lax.all_to_all(lines_out, ('trade', 'path'), split_axis=0, concat_axis=0,...  9.34 us
    all_to_all x1, starting transfers between devices, body(): lax.all_to_all(outgoing, 'trade', split_axis=0, concat_axis=0, tiled=True)  7.29 us
    all_to_all x1, waiting for transfers between devices, body(): lax.all_to_all(outgoing, 'trade', split_axis=0, concat_axis=0, tiled=True)  4.78 us
    pallas_call x1, Pallas kernels, body(): pl.pallas_call(functools.partial(main_kernel, plan, path_total), out_shap...  4.16 us
    pallas_call x1, Pallas kernels, body(): pl.pallas_call(functools.partial(basis_kernel, plan), out_shape=jax.Shape...  2.48 us
    pallas_call x1, Pallas kernels, body(): pl.pallas_call(functools.partial(pack_kernel, plan), out_shape=[jax.Shape...  2.1 us
    pallas_call x1, Pallas kernels, body(): pl.pallas_call(functools.partial(price_kernel, plan), out_shape=jax.Shape...  1 us
    pallas_call x1, Pallas kernels, body(): pl.pallas_call(functools.partial(finish_kernel, plan), out_shape=[jax.Sha...  0.81 us
  transfers between devices with their start and end apart: 2, of which 2 were waited for; matrix products, arithmetic and copies ran while one was open for 0% of the time, Pallas kernels for 11%

profile of v20, /device:TPU:0, one launch (start us, length us, event | category | flops | bytes accessed | tf_op | source)
XLA Modules:
  0.0 33.1 jit_solution(6552954648931521857)
XLA Ops:
  0.6 0.0 copy-start
  0.6 0.0 copy-start.1
  0.7 0.0 copy-start.5
  0.7 2.1 %pack.1 = (f32[8,512]{1,0:T(8,128)}, bf16[8,64,128]{2,1,0:T(8,128)(2,1)}) custom-call(s32[1]{0:T(128)} %bitcast.me_ref, s32[1]{0:T(128)} %bitcast.1.half_ref, s32[32,128]{1,0:T(8,128)} %bitcast.16, bf16[160,512]{1,0:T(8,128)(2,1)} %bitcast.15, f32[4,128]{1,0:T(4,128)} %bitcast.12), custom_call_target="tpu_custom_call" | custom-call | flops 4294967296 | bytes 524288 | tf_op jit(solution)/shard_map/pack/pallas_call | solution.py:344
  2.8 7.3 %all-to-all-start = ((bf16[8,64,128]{2,1,0:T(8,128)(2,1)}), bf16[8,64,128]{2,1,0:T(8,128)(2,1)S(1)}, u32[]{:S(2)}, u32[]{:S(2)}) async-start(bf16[8,64,128]{2,1,0:T(8,128)(2,1)} %get-tuple-element.9), calls=%async_computation | async-start | bytes 262144 | tf_op jit(solution)/shard_map/all_to_all | solution.py:361
  10.1 0.0 copy-done
  10.1 0.0 copy-done.1
  10.1 0.0 copy-done.5
  10.1 2.5 %basis.1.basis_ref = bf16[256,4096]{1,0:T(8,128)(2,1)S(1)} custom-call(bf16[2560,128]{1,0:T(8,128)(2,1)S(1)} %bitcast.10, f32[1,80]{1,0:T(1,128)S(1)} %bitcast.14, f32[80,80]{1,0:T(8,128)S(1)} %copy-done.1), custom_call_target="tpu_custom_call" | custom-call | flops 262144000 | bytes 4194304 | tf_op jit(solution)/shard_map/basis/pallas_call | solution.py:362
  12.6 0.0 copy-start.3
  12.6 0.0 copy-start.6
  12.6 0.0 copy-start.7
  12.6 0.0 copy-start.8
  12.6 4.8 %all-to-all-done.in_ref.refs_0_ = bf16[8,64,128]{2,1,0:T(8,128)(2,1)S(1)} async-done(((bf16[8,64,128]{2,1,0:T(8,128)(2,1)}), bf16[8,64,128]{2,1,0:T(8,128)(2,1)S(1)}, u32[]{:S(2)}, u32[]{:S(2)}) %all-to-all-start) | async-done | bytes 131104 | tf_op jit(solution)/shard_map/all_to_all | solution.py:361
  17.4 0.0 collective-permute-start
  17.4 1.0 %price_own_half.1.refs_2_ = bf16[384,4096]{1,0:T(8,128)(2,1)S(1)} custom-call(bf16[256,4096]{1,0:T(8,128)(2,1)S(1)} %basis.1.basis_ref, bf16[8,64,128]{2,1,0:T(8,128)(2,1)S(1)} %all-to-all-done.in_ref.refs_0_), custom_call_target="tpu_custom_call" | custom-call | flops 805306368 | bytes 6291456 | tf_op jit(solution)/shard_map/price_own_half/pallas_call | solution.py:387
  18.4 0.0 copy-start.2
  18.4 0.0 copy-start.4
  18.4 0.3 collective-permute-done.refs_1_
  18.8 0.0 copy-done.3
  18.8 0.0 copy-done.6
  18.8 0.0 copy-done.7
  18.8 0.0 copy-done.8
  18.8 4.2 %value_and_allocate.1 = f32[32,1,128]{2,1,0:T(1,128)S(1)} custom-call(s32[1]{0:T(128)} %bitcast.me_ref, s32[8]{0:T(128)S(1)} %copy-done.6, s32[4]{0:T(128)S(1)} %copy-done.7, s32[4]{0:T(128)S(1)} %copy-done.8, f32[4,32]{1,0:T(4,128)S(1)} %copy-done.3, bf16[256,4096]{1,0:T(8,128)(2,1)S(1)} %basis.1.basis_ref, ...), custom_call_target="tpu_custom_call" | custom-call | tf_op jit(solution)/shard_map/value_and_allocate/pallas_call | solution.py:401
  22.9 9.3 %all_to_all.10 = f32[32,1,128]{2,1,0:T(1,128)S(1)} all-to-all(f32[32,1,128]{2,1,0:T(1,128)S(1)} %value_and_allocate.1), channel_id=1, replica_groups=mesh['trade'=8,'path'=4] {'trade','path'}, dimensions={0} | all-to-all | bytes 32768 | tf_op jit(solution)/shard_map/all_to_all | solution.py:411
  32.3 0.0 copy-done.2
  32.3 0.0 copy-done.4
  32.3 0.8 %finish.1 = (f32[1,512]{1,0:T(1,128)}, f32[1,4]{1,0:T(1,128)}) custom-call(s32[1]{0:T(128)} %bitcast.me_ref, f32[8,512]{1,0:T(8,128)S(1)} %copy-done.2, f32[4,128]{1,0:T(4,128)S(1)} %bitcast.13, f32[32,128]{1,0:T(8,128)S(1)} %bitcast.11), custom_call_target="tpu_custom_call" | custom-call | tf_op jit(solution)/shard_map/finish/pallas_call | solution.py:413
Async XLA Ops:
  0.6 9.4 %copy-start = (bf16[80,32,128]{2,1,0:T(8,128)(2,1)S(1)}, bf16[80,32,128]{2,1,0:T(8,128)(2,1)}, u32[]{:S(2)}) copy-start(bf16[80,32,128]{2,1,0:T(8,128)(2,1)} %param.10) | copy-start | bytes 1966084
  0.6 9.4 %copy-start.1 = (f32[80,80]{1,0:T(8,128)S(1)}, f32[80,80]{1,0:T(8,128)}, u32[]{:S(2)}) copy-start(f32[80,80]{1,0:T(8,128)} %loading_hbm.1) | copy-start | bytes 76804
  0.7 9.4 %copy-start.5 = (f32[80]{0:T(128)S(1)}, f32[80]{0:T(128)}, u32[]{:S(2)}) copy-start(f32[80]{0:T(128)} %param.11) | copy-start | bytes 964
  2.8 14.6 %all-to-all-start = ((bf16[8,64,128]{2,1,0:T(8,128)(2,1)}), bf16[8,64,128]{2,1,0:T(8,128)(2,1)S(1)}, u32[]{:S(2)}, u32[]{:S(2)}) async-start(bf16[8,64,128]{2,1,0:T(8,128)(2,1)} %get-tuple-element.9), calls=%async_computation | async-start | bytes 262144 | tf_op jit(solution)/shard_map/all_to_all | solution.py:361
  12.6 6.2 %copy-start.3 = (f32[4,32]{1,0:T(4,128)S(1)}, f32[4,32]{1,0:T(4,128)}, u32[]{:S(2)}) copy-start(f32[4,32]{1,0:T(4,128)} %weight_ref.1) | copy-start | bytes 1540
  12.6 6.2 %copy-start.6 = (s32[8]{0:T(128)S(1)}, s32[8]{0:T(128)}, u32[]{:S(2)}) copy-start(s32[8]{0:T(128)} %agr_ref.1) | copy-start | bytes 100
  12.6 6.2 %copy-start.7 = (s32[4]{0:T(128)S(1)}, s32[4]{0:T(128)}, u32[]{:S(2)}) copy-start(s32[4]{0:T(128)} %cpty_ref.1) | copy-start | bytes 52
  12.6 6.2 %copy-start.8 = (s32[4]{0:T(128)S(1)}, s32[4]{0:T(128)}, u32[]{:S(2)}) copy-start(s32[4]{0:T(128)} %lag_ref.1) | copy-start | bytes 52
  17.4 1.3 %collective-permute-start = (bf16[8,64,128]{2,1,0:T(8,128)(2,1)S(1)}, bf16[8,64,128]{2,1,0:T(8,128)(2,1)S(1)}, u32[]{:S(2)}, u32[]{:S(2)}) collective-permute-start(bf16[8,64,128]{2,1,0:T(8,128)(2,1)S(1)} %all-to-all-done.in_ref.refs_0_), channel_id=1, source_target_pairs={{0,1},{1,0},{2,3},{3,2},{4,5},{5,4},{6,7},{7,6},{8,9},{9,8},{10,11... | collective-permute-start | bytes 393224 | tf_op jit(solution)/shard_map/ppermute | solution.py:385
  18.4 13.9 %copy-start.2 = (f32[8,512]{1,0:T(8,128)S(1)}, f32[8,512]{1,0:T(8,128)}, u32[]{:S(2)}) copy-start(f32[8,512]{1,0:T(8,128)} %get-tuple-element.8.place_ref) | copy-start | bytes 49156
  18.4 13.9 %copy-start.4 = (f32[512]{0:T(512)S(1)}, f32[512]{0:T(512)}, u32[]{:S(2)}) copy-start(f32[512]{0:T(512)} %param.14) | copy-start | bytes 6148

commit v21 on v15

--- a/solution.py
+++ b/solution.py
@@ -70,7 +70,7 @@
         self.trades = owners * self.slots
         self.dates = dates
         self.width = 1024
-        self.step = 2048 if self.trades <= 1024 else 512
+        self.step = 1024 if self.trades <= 1024 else 512
 
 
 def pack_kernel(plan, me_ref, half_ref, sets_hbm, coef_hbm, notional_hbm, place_ref, out_ref, *refs):

time: 33.4 us -> 33.4 us (level)
  no operation moved by 1% of the time
where the time goes in v21:
time: 33.4 us; the launch traced here: 33.1 us
  Pallas kernels  10.6 us (32%)
  blocking collectives  9.34 us (28%)
  starting transfers between devices  7.29 us (22%)
  waiting for transfers between devices  5.1 us (15%)
  between operations  0.77 us (2%)
    all_to_all x1, blocking collectives, body(): lax.all_to_all(lines_out, ('trade', 'path'), split_axis=0, concat_axis=0,...  9.34 us
    all_to_all x1, starting transfers between devices, body(): lax.all_to_all(outgoing, 'trade', split_axis=0, concat_axis=0, tiled=True)  7.29 us
    all_to_all x1, waiting for transfers between devices, body(): lax.all_to_all(outgoing, 'trade', split_axis=0, concat_axis=0, tiled=True)  4.78 us
    pallas_call x1, Pallas kernels, body(): pl.pallas_call(functools.partial(main_kernel, plan, path_total), out_shap...  4.16 us
    pallas_call x1, Pallas kernels, body(): pl.pallas_call(functools.partial(basis_kernel, plan), out_shape=jax.Shape...  2.48 us
    pallas_call x1, Pallas kernels, body(): pl.pallas_call(functools.partial(pack_kernel, plan), out_shape=[jax.Shape...  2.1 us
    pallas_call x1, Pallas kernels, body(): pl.pallas_call(functools.partial(price_kernel, plan), out_shape=jax.Shape...  1 us
    pallas_call x1, Pallas kernels, body(): pl.pallas_call(functools.partial(finish_kernel, plan), out_shape=[jax.Sha...  0.81 us
  transfers between devices with their start and end apart: 2, of which 2 were waited for; matrix products, arithmetic and copies ran while one was open for 0% of the time, Pallas kernels for 11%

profile of v21, /device:TPU:0, one launch (start us, length us, event | category | flops | bytes accessed | tf_op | source)
XLA Modules:
  0.0 33.1 jit_solution(17943017358468892347)
XLA Ops:
  0.6 0.0 copy-start
  0.6 0.0 copy-start.1
  0.7 0.0 copy-start.5
  0.7 2.1 %pack.1 = (f32[8,512]{1,0:T(8,128)}, bf16[8,64,128]{2,1,0:T(8,128)(2,1)}) custom-call(s32[1]{0:T(128)} %bitcast.me_ref, s32[1]{0:T(128)} %bitcast.1.half_ref, s32[32,128]{1,0:T(8,128)} %bitcast.16, bf16[160,512]{1,0:T(8,128)(2,1)} %bitcast.15, f32[4,128]{1,0:T(4,128)} %bitcast.12), custom_call_target="tpu_custom_call" | custom-call | flops 4294967296 | bytes 524288 | tf_op jit(solution)/shard_map/pack/pallas_call | solution.py:343
  2.8 7.3 %all-to-all-start = ((bf16[8,64,128]{2,1,0:T(8,128)(2,1)}), bf16[8,64,128]{2,1,0:T(8,128)(2,1)S(1)}, u32[]{:S(2)}, u32[]{:S(2)}) async-start(bf16[8,64,128]{2,1,0:T(8,128)(2,1)} %get-tuple-element.9), calls=%async_computation | async-start | bytes 262144 | tf_op jit(solution)/shard_map/all_to_all | solution.py:360
  10.1 0.0 copy-done
  10.1 0.0 copy-done.1
  10.1 0.0 copy-done.5
  10.1 2.5 %basis.1.basis_ref = bf16[256,4096]{1,0:T(8,128)(2,1)S(1)} custom-call(bf16[2560,128]{1,0:T(8,128)(2,1)S(1)} %bitcast.10, f32[1,80]{1,0:T(1,128)S(1)} %bitcast.14, f32[80,80]{1,0:T(8,128)S(1)} %copy-done.1), custom_call_target="tpu_custom_call" | custom-call | flops 262144000 | bytes 4194304 | tf_op jit(solution)/shard_map/basis/pallas_call | solution.py:361
  12.6 0.0 copy-start.3
  12.6 0.0 copy-start.6
  12.6 0.0 copy-start.7
  12.6 0.0 copy-start.8
  12.6 4.8 %all-to-all-done.in_ref.refs_0_ = bf16[8,64,128]{2,1,0:T(8,128)(2,1)S(1)} async-done(((bf16[8,64,128]{2,1,0:T(8,128)(2,1)}), bf16[8,64,128]{2,1,0:T(8,128)(2,1)S(1)}, u32[]{:S(2)}, u32[]{:S(2)}) %all-to-all-start) | async-done | bytes 131104 | tf_op jit(solution)/shard_map/all_to_all | solution.py:360
  17.4 0.0 collective-permute-start
  17.4 1.0 %price_own_half.1.refs_2_ = bf16[384,4096]{1,0:T(8,128)(2,1)S(1)} custom-call(bf16[256,4096]{1,0:T(8,128)(2,1)S(1)} %basis.1.basis_ref, bf16[8,64,128]{2,1,0:T(8,128)(2,1)S(1)} %all-to-all-done.in_ref.refs_0_), custom_call_target="tpu_custom_call" | custom-call | flops 805306368 | bytes 6291456 | tf_op jit(solution)/shard_map/price_own_half/pallas_call | solution.py:386
  18.4 0.0 copy-start.2
  18.4 0.0 copy-start.4
  18.4 0.3 collective-permute-done.refs_1_
  18.8 0.0 copy-done.3
  18.8 0.0 copy-done.6
  18.8 0.0 copy-done.7
  18.8 0.0 copy-done.8
  18.8 4.2 %value_and_allocate.1 = f32[32,1,128]{2,1,0:T(1,128)S(1)} custom-call(s32[1]{0:T(128)} %bitcast.me_ref, s32[8]{0:T(128)S(1)} %copy-done.6, s32[4]{0:T(128)S(1)} %copy-done.7, s32[4]{0:T(128)S(1)} %copy-done.8, f32[4,32]{1,0:T(4,128)S(1)} %copy-done.3, bf16[256,4096]{1,0:T(8,128)(2,1)S(1)} %basis.1.basis_ref, ...), custom_call_target="tpu_custom_call" | custom-call | tf_op jit(solution)/shard_map/value_and_allocate/pallas_call | solution.py:400
  22.9 9.3 %all_to_all.10 = f32[32,1,128]{2,1,0:T(1,128)S(1)} all-to-all(f32[32,1,128]{2,1,0:T(1,128)S(1)} %value_and_allocate.1), channel_id=1, replica_groups=mesh['trade'=8,'path'=4] {'trade','path'}, dimensions={0} | all-to-all | bytes 32768 | tf_op jit(solution)/shard_map/all_to_all | solution.py:410
  32.3 0.0 copy-done.2
  32.3 0.0 copy-done.4
  32.3 0.8 %finish.1 = (f32[1,512]{1,0:T(1,128)}, f32[1,4]{1,0:T(1,128)}) custom-call(s32[1]{0:T(128)} %bitcast.me_ref, f32[8,512]{1,0:T(8,128)S(1)} %copy-done.2, f32[4,128]{1,0:T(4,128)S(1)} %bitcast.13, f32[32,128]{1,0:T(8,128)S(1)} %bitcast.11), custom_call_target="tpu_custom_call" | custom-call | tf_op jit(solution)/shard_map/finish/pallas_call | solution.py:412
Async XLA Ops:
  0.6 9.4 %copy-start = (bf16[80,32,128]{2,1,0:T(8,128)(2,1)S(1)}, bf16[80,32,128]{2,1,0:T(8,128)(2,1)}, u32[]{:S(2)}) copy-start(bf16[80,32,128]{2,1,0:T(8,128)(2,1)} %param.10) | copy-start | bytes 1966084
  0.6 9.4 %copy-start.1 = (f32[80,80]{1,0:T(8,128)S(1)}, f32[80,80]{1,0:T(8,128)}, u32[]{:S(2)}) copy-start(f32[80,80]{1,0:T(8,128)} %loading_hbm.1) | copy-start | bytes 76804
  0.7 9.4 %copy-start.5 = (f32[80]{0:T(128)S(1)}, f32[80]{0:T(128)}, u32[]{:S(2)}) copy-start(f32[80]{0:T(128)} %param.11) | copy-start | bytes 964
  2.8 14.6 %all-to-all-start = ((bf16[8,64,128]{2,1,0:T(8,128)(2,1)}), bf16[8,64,128]{2,1,0:T(8,128)(2,1)S(1)}, u32[]{:S(2)}, u32[]{:S(2)}) async-start(bf16[8,64,128]{2,1,0:T(8,128)(2,1)} %get-tuple-element.9), calls=%async_computation | async-start | bytes 262144 | tf_op jit(solution)/shard_map/all_to_all | solution.py:360
  12.6 6.2 %copy-start.3 = (f32[4,32]{1,0:T(4,128)S(1)}, f32[4,32]{1,0:T(4,128)}, u32[]{:S(2)}) copy-start(f32[4,32]{1,0:T(4,128)} %weight_ref.1) | copy-start | bytes 1540
  12.6 6.2 %copy-start.6 = (s32[8]{0:T(128)S(1)}, s32[8]{0:T(128)}, u32[]{:S(2)}) copy-start(s32[8]{0:T(128)} %agr_ref.1) | copy-start | bytes 100
  12.6 6.2 %copy-start.7 = (s32[4]{0:T(128)S(1)}, s32[4]{0:T(128)}, u32[]{:S(2)}) copy-start(s32[4]{0:T(128)} %cpty_ref.1) | copy-start | bytes 52
  12.6 6.2 %copy-start.8 = (s32[4]{0:T(128)S(1)}, s32[4]{0:T(128)}, u32[]{:S(2)}) copy-start(s32[4]{0:T(128)} %lag_ref.1) | copy-start | bytes 52
  17.4 1.3 %collective-permute-start = (bf16[8,64,128]{2,1,0:T(8,128)(2,1)S(1)}, bf16[8,64,128]{2,1,0:T(8,128)(2,1)S(1)}, u32[]{:S(2)}, u32[]{:S(2)}) collective-permute-start(bf16[8,64,128]{2,1,0:T(8,128)(2,1)S(1)} %all-to-all-done.in_ref.refs_0_), channel_id=1, source_target_pairs={{0,1},{1,0},{2,3},{3,2},{4,5},{5,4},{6,7},{7,6},{8,9},{9,8},{10,11... | collective-permute-start | bytes 393224 | tf_op jit(solution)/shard_map/ppermute | solution.py:384
  18.4 13.9 %copy-start.2 = (f32[8,512]{1,0:T(8,128)S(1)}, f32[8,512]{1,0:T(8,128)}, u32[]{:S(2)}) copy-start(f32[8,512]{1,0:T(8,128)} %get-tuple-element.8.place_ref) | copy-start | bytes 49156
  18.4 13.9 %copy-start.4 = (f32[512]{0:T(512)S(1)}, f32[512]{0:T(512)}, u32[]{:S(2)}) copy-start(f32[512]{0:T(512)} %param.14) | copy-start | bytes 6148
